TPU v7x, 256 devices: a whole 4x4x8 slice. The times are simulated.
256 devices in a mesh: section: 16 (over z_hi, y, core), tok: 16 (over z_lo, x).
Axes of the slice: x: 4, y: 4, z: 8 (z_hi: 2, z_lo: 4; z = z_hi * 4 + z_lo), core: 2. Of those that a mesh axis runs over, the one named last changes fastest.
Arguments:
- tokens: bfloat16 [2, 2048, 512], P(None, 'tok'), may hold values from -6 to 6
- offsets: int32 [16], P('section'), may hold values from 1 to 127
- w_qkv: bfloat16 [16, 512, 1536], P('section'), may hold values from -0.25 to 0.25
- w_out: bfloat16 [16, 512, 512], P('section'), may hold values from -0.25 to 0.25
- w_up: bfloat16 [16, 512, 2048], P('section'), may hold values from -0.25 to 0.25
- w_down: bfloat16 [16, 512, 2048], P('section'), may hold values from -0.125 to 0.125
- w_head: bfloat16 [512, 128], replicated, may hold values from -0.25 to 0.25
- era5t: bfloat16 [2, 2048, 128], P(None, 'tok'), may hold values from -6 to 6
- era5: bfloat16 [2, 2048, 128], P(None, 'tok'), may hold values from -6 to 6
- flags: int32 [2, 32], P(None, 'tok'), may hold values 0 or 1
- buckets: int32 [2, 2048], P(None, 'tok'), may hold values from 0 to 7
Outputs:
- grad_qkv: float32 [16, 512, 1536], P('section', 'tok')
- grad_out: float32 [16, 512, 512], P('section', 'tok')
- grad_up: float32 [16, 512, 2048], P('section', 'tok')
- grad_down: float32 [16, 512, 2048], P('section', 'tok')
All inputs are finite; a program needn't handle non-finite values. No bound on the sum of `flags` on one device may be relied on, other than what follows from the above.
Results may differ from a plain program's by a relative error of at most 0.029.
Values may be sent and summed in bfloat16 or wider, within the bound.
No kernel may reach another device: no remote copies, remote signals or barrier semaphores. Data moves between devices by JAX's collectives and lax.ppermute only.
A program may use at most 128 MiB of HBM per device.

v0:
```python
import math

import jax
import jax.numpy as jnp
from jax import lax
from jax.sharding import PartitionSpec as P

HEAD_DIM = 32
WIN = 128


norm_eps = 1e-05
logit_scale = 10.0
floor_share = 0.75
decay_base = 0.8


def with_halo(cells, sides, width):
    for axis, dim in sides:
        count = lax.axis_size(axis)
        head = lax.slice_in_dim(cells, 0, width, axis=dim)
        tail = lax.slice_in_dim(cells, cells.shape[dim] - width, cells.shape[dim], axis=dim)
        cells = jnp.concatenate(
            [
                lax.ppermute(tail, axis, [(i, (i + 1) % count) for i in range(count)]),
                cells,
                lax.ppermute(head, axis, [((i + 1) % count, i) for i in range(count)]),
            ],
            axis=dim,
        )
    return cells


def from_partner(block, axis, stride):
    count = lax.axis_size(axis)
    route = []
    for low in range(count):
        high = low | 1 << stride
        if high != low and high < count:
            route += [(low, high), (high, low)]
    return lax.ppermute(block, axis, route)


def passed_along(block, axis, distance):
    devices = range(lax.axis_size(axis))
    route = [(i - distance, i) for i in devices if i - distance in devices]
    return lax.ppermute(block, axis, route)


def layer_norm(values):
    center = values - jnp.mean(values, axis=-1, keepdims=True)
    spread = jnp.mean(center * center, axis=-1, keepdims=True)
    return center * lax.rsqrt(spread + norm_eps)


def window_core(packed):
    windows, window_len, triple = packed.shape
    model_width = triple // 3
    head_count = model_width // HEAD_DIM
    queries = packed[:, :, :model_width].reshape(windows, window_len, head_count, HEAD_DIM)
    key_rows = packed[:, :, model_width : 2 * model_width].reshape(
        windows, window_len, head_count, HEAD_DIM
    )
    values = packed[:, :, 2 * model_width :].reshape(windows, window_len, head_count, HEAD_DIM)
    norm_floor = floor_share * math.sqrt(HEAD_DIM)
    queries = queries / jnp.maximum(
        jnp.sqrt(jnp.sum(queries * queries, axis=-1, keepdims=True)), norm_floor
    )
    key_rows = key_rows / jnp.maximum(
        jnp.sqrt(jnp.sum(key_rows * key_rows, axis=-1, keepdims=True)), norm_floor
    )
    scores = logit_scale * jnp.einsum("awhd,avhd->ahwv", queries, key_rows)
    weights = jnp.exp(scores)
    weights = weights / jnp.sum(weights, axis=-1, keepdims=True)
    weights = lax.optimization_barrier(weights.astype(jnp.bfloat16)).astype(jnp.float32)
    mixture = jnp.einsum("ahwv,avhd->awhd", weights, values)
    return mixture.reshape(windows, window_len, model_width)


def attend_forward(rows_in, qkv_weight, out_weight):
    row_total, model_width = rows_in.shape
    normed = layer_norm(rows_in.astype(jnp.float32)).astype(jnp.bfloat16)
    packed = jnp.dot(normed, qkv_weight, preferred_element_type=jnp.float32).astype(jnp.bfloat16)
    attended = window_core(
        packed.astype(jnp.float32).reshape(row_total // WIN, WIN, 3 * model_width)
    )
    attended = attended.reshape(row_total, model_width).astype(jnp.bfloat16)
    mixed_rows = rows_in.astype(jnp.float32) + jnp.dot(
        attended, out_weight, preferred_element_type=jnp.float32
    )
    return (normed, packed, attended, mixed_rows)


def attend_backward(normed, packed, grad_rows, qkv_weight, out_weight):
    row_total, model_width = normed.shape
    grad_att = lax.dot_general(
        grad_rows, out_weight, (((1,), (1,)), ((), ())), preferred_element_type=jnp.float32
    )
    unused, core_back = jax.vjp(
        window_core, packed.astype(jnp.float32).reshape(row_total // WIN, WIN, 3 * model_width)
    )
    grad_packed = core_back(grad_att.reshape(row_total // WIN, WIN, model_width))[0]
    grad_packed = grad_packed.reshape(row_total, 3 * model_width).astype(jnp.bfloat16)
    grad_normed = lax.dot_general(
        grad_packed, qkv_weight, (((1,), (1,)), ((), ())), preferred_element_type=jnp.float32
    )
    return (grad_normed, grad_packed)


def mlp_pieces(mixed_rows, up_weight):
    normed = layer_norm(mixed_rows).astype(jnp.bfloat16)
    lifted = jnp.dot(normed, up_weight, preferred_element_type=jnp.float32)
    hidden = jax.nn.gelu(lifted).astype(jnp.bfloat16)
    return (normed, lifted, hidden)


def mlp_forward(mixed_rows, up_weight, down_weight):
    normed, lifted, hidden = mlp_pieces(mixed_rows, up_weight)
    product = lax.dot_general(
        hidden, down_weight, (((1,), (1,)), ((), ())), preferred_element_type=jnp.float32
    )
    return (mixed_rows + product).astype(jnp.bfloat16)


def mlp_backward(mixed_rows, grad_output, up_weight, down_weight):
    normed, lifted, hidden = mlp_pieces(mixed_rows, up_weight)
    grad_rounded = grad_output.astype(jnp.bfloat16)
    grad_hidden = jnp.dot(grad_rounded, down_weight, preferred_element_type=jnp.float32)
    unused, gelu_back = jax.vjp(jax.nn.gelu, lifted)
    grad_lifted = gelu_back(grad_hidden)[0].astype(jnp.bfloat16)
    grad_normed = lax.dot_general(
        grad_lifted, up_weight, (((1,), (1,)), ((), ())), preferred_element_type=jnp.float32
    )
    unused_two, norm_back = jax.vjp(layer_norm, mixed_rows)
    grad_mixed = grad_output + norm_back(grad_normed)[0]
    return (grad_mixed, normed, grad_lifted, hidden, grad_rounded)


def head_gradient(final_rows, head_weight, target, row_decay, loss_scale):
    final_wide = final_rows.astype(jnp.float32)
    normed = layer_norm(final_wide).astype(jnp.bfloat16)
    predicted = jnp.dot(normed, head_weight, preferred_element_type=jnp.float32)
    grad_pred = (row_decay[:, None] * (predicted - target) * loss_scale).astype(jnp.bfloat16)
    grad_normed = lax.dot_general(
        grad_pred, head_weight, (((1,), (1,)), ((), ())), preferred_element_type=jnp.float32
    )
    unused, norm_back = jax.vjp(layer_norm, final_wide)
    return norm_back(grad_normed)[0]


def body(tokens, offsets, w_qkv, w_out, w_up, w_down, w_head, era5t, era5, flags, buckets):
    section_count = lax.axis_size("section")
    tok_count = lax.axis_size("tok")
    half_count = section_count // 2
    section_index = lax.axis_index("section")
    micro_count, row_count, model_width = tokens.shape
    segment_count = row_count + WIN
    shift_start = offsets[0]
    own_start = WIN - shift_start
    qkv_weight = w_qkv[0]
    out_weight = w_out[0]
    up_weight = w_up[0]
    down_weight = w_down[0]
    hidden_width = up_weight.shape[1]

    def with_rims(rows_in):
        return with_halo(rows_in, (("tok", 0),), WIN)

    def segment_of(extended):
        return lax.dynamic_slice_in_dim(extended, shift_start, segment_count, 0)

    def own_of(segment_rows):
        return lax.dynamic_slice_in_dim(segment_rows, own_start, row_count, 0)

    def mirrored(buffers):
        bit_total = section_count.bit_length() - 1
        bit_order = list(range(bit_total))
        for bit_index in bit_order:
            buffers = from_partner(buffers, "section", bit_index)
        return buffers

    def section_forward(extended):
        mixed_rows = attend_forward(segment_of(extended), qkv_weight, out_weight)[3]
        return mlp_forward(own_of(mixed_rows), up_weight, down_weight)

    def quiet_forward(extended):
        return jnp.zeros((row_count, model_width), jnp.bfloat16)

    def forward_phase(first_section, phase_state, skip_rows):

        def advance(step_index, loop_state):
            inbox_rows, saved_inputs, produced = loop_state
            position = section_index - first_section
            slot_index = step_index - position
            active = (
                (position >= 0)
                & (position < half_count)
                & (slot_index >= 0)
                & (slot_index < micro_count)
            )
            slot_clip = jnp.clip(slot_index, 0, micro_count - 1)
            merged = (
                inbox_rows[slot_clip].astype(jnp.float32) + skip_rows[slot_clip].astype(jnp.float32)
            ).astype(jnp.bfloat16)
            extended = with_rims(merged)
            result = lax.cond(active, section_forward, quiet_forward, extended)
            saved_inputs = saved_inputs.at[slot_clip].set(
                jnp.where(active, extended, saved_inputs[slot_clip])
            )
            produced = produced.at[slot_clip].set(jnp.where(active, result, produced[slot_clip]))
            incoming = passed_along(result, "section", 1)
            sender = position - 1
            sent_slot = step_index - sender
            arrived = (
                (sender >= 0) & (sender < half_count) & (sent_slot >= 0) & (sent_slot < micro_count)
            )
            sent_clip = jnp.clip(sent_slot, 0, micro_count - 1)
            inbox_rows = inbox_rows.at[sent_clip].set(
                jnp.where(arrived, incoming, inbox_rows[sent_clip])
            )
            return (inbox_rows, saved_inputs, produced)

        return lax.fori_loop(0, half_count + micro_count - 1, advance, phase_state)

    blank_rows = jnp.zeros((micro_count, row_count, model_width), jnp.bfloat16)
    saved_start = jnp.zeros((micro_count, row_count + 2 * WIN, model_width), jnp.bfloat16)
    phase_state = forward_phase(0, (tokens, saved_start, blank_rows), blank_rows)
    skip_rows = mirrored(phase_state[2])
    inbox_rows, saved_inputs, produced = forward_phase(half_count, phase_state, skip_rows)
    sample_rows = row_count // flags.shape[1]
    chosen = jnp.repeat(flags, sample_rows, axis=1)[:, :, None] == 1
    target = jnp.where(chosen, era5t.astype(jnp.float32), era5.astype(jnp.float32))
    row_decay = jnp.power(jnp.float32(decay_base), buckets.astype(jnp.float32))
    loss_scale = 1.0 / math.sqrt(micro_count * row_count * tok_count)
    head_grads = head_gradient(
        produced.reshape(micro_count * row_count, model_width),
        w_head,
        target.reshape(micro_count * row_count, target.shape[2]),
        row_decay.reshape(micro_count * row_count),
        loss_scale,
    )
    head_grads = head_grads.reshape(micro_count, row_count, model_width)

    def backward_first(extended, grad_input):
        normed, packed, attended, mixed_rows = attend_forward(
            segment_of(extended), qkv_weight, out_weight
        )
        grad_mixed, normed_two, grad_lifted, hidden, grad_rounded = mlp_backward(
            own_of(mixed_rows), grad_input, up_weight, down_weight
        )
        return (grad_mixed, normed_two, grad_lifted, hidden, grad_rounded, normed, packed, attended)

    def quiet_first(extended, grad_input):
        return (
            jnp.zeros((row_count, model_width), jnp.float32),
            jnp.zeros((row_count, model_width), jnp.bfloat16),
            jnp.zeros((row_count, hidden_width), jnp.bfloat16),
            jnp.zeros((row_count, hidden_width), jnp.bfloat16),
            jnp.zeros((row_count, model_width), jnp.bfloat16),
            jnp.zeros((segment_count, model_width), jnp.bfloat16),
            jnp.zeros((segment_count, 3 * model_width), jnp.bfloat16),
            jnp.zeros((segment_count, model_width), jnp.bfloat16),
        )

    def backward_second(extended, grad_rims, grad_mixed, normed, packed):
        segment_rows = segment_of(extended)
        grad_segment = segment_of(grad_rims)
        grad_normed, grad_packed = attend_backward(
            normed, packed, grad_segment, qkv_weight, out_weight
        )
        unused, norm_back = jax.vjp(layer_norm, own_of(segment_rows).astype(jnp.float32))
        grad_in_rows = grad_mixed + norm_back(own_of(grad_normed))[0]
        return (grad_in_rows, grad_packed[WIN:], grad_segment[WIN:])

    def quiet_second(extended, grad_rims, grad_mixed, normed, packed):
        return (
            jnp.zeros((row_count, model_width), jnp.float32),
            jnp.zeros((row_count, 3 * model_width), jnp.bfloat16),
            jnp.zeros((row_count, model_width), jnp.bfloat16),
        )

    def backward_phase(first_section, phase_state, skip_grads):

        def retreat(step_index, loop_state):
            inbox_grads, returned, grad_store = loop_state
            position = first_section + half_count - 1 - section_index
            slot_index = step_index - position
            active = (
                (position >= 0)
                & (position < half_count)
                & (slot_index >= 0)
                & (slot_index < micro_count)
            )
            slot_clip = jnp.clip(slot_index, 0, micro_count - 1)
            grad_input = inbox_grads[slot_clip] + skip_grads[slot_clip].astype(jnp.float32)
            extended = saved_inputs[slot_clip]
            first_parts = lax.cond(active, backward_first, quiet_first, extended, grad_input)
            grad_mixed, normed_two, grad_lifted, hidden, grad_rounded, normed, packed, attended = (
                first_parts
            )
            grad_rims = with_rims(grad_mixed.astype(jnp.bfloat16))
            grad_in_rows, grad_packed, grad_window = lax.cond(
                active,
                backward_second,
                quiet_second,
                extended,
                grad_rims,
                grad_mixed,
                normed,
                packed,
            )
            pieces = (
                normed[WIN:],
                grad_packed,
                attended[WIN:],
                grad_window,
                normed_two,
                grad_lifted,
                grad_rounded,
                hidden,
            )
            grad_store = tuple(
                (
                    stack.at[slot_clip].set(jnp.where(active, piece, stack[slot_clip]))
                    for stack, piece in zip(grad_store, pieces)
                )
            )
            sent_back = grad_in_rows.astype(jnp.bfloat16)
            returned = returned.at[slot_clip].set(jnp.where(active, sent_back, returned[slot_clip]))
            incoming = passed_along(sent_back, "section", -1)
            sender = position - 1
            sent_slot = step_index - sender
            arrived = (
                (sender >= 0) & (sender < half_count) & (sent_slot >= 0) & (sent_slot < micro_count)
            )
            sent_clip = jnp.clip(sent_slot, 0, micro_count - 1)
            inbox_grads = inbox_grads.at[sent_clip].set(
                jnp.where(arrived, incoming.astype(jnp.float32), inbox_grads[sent_clip])
            )
            return (inbox_grads, returned, grad_store)

        return lax.fori_loop(0, half_count + micro_count - 1, retreat, phase_state)

    store_start = (
        jnp.zeros((micro_count, row_count, model_width), jnp.bfloat16),
        jnp.zeros((micro_count, row_count, 3 * model_width), jnp.bfloat16),
        jnp.zeros((micro_count, row_count, model_width), jnp.bfloat16),
        jnp.zeros((micro_count, row_count, model_width), jnp.bfloat16),
        jnp.zeros((micro_count, row_count, model_width), jnp.bfloat16),
        jnp.zeros((micro_count, row_count, hidden_width), jnp.bfloat16),
        jnp.zeros((micro_count, row_count, model_width), jnp.bfloat16),
        jnp.zeros((micro_count, row_count, hidden_width), jnp.bfloat16),
    )
    phase_state = backward_phase(half_count, (head_grads, blank_rows, store_start), blank_rows)
    skip_grads = mirrored(phase_state[1])
    inbox_grads, returned, grad_store = backward_phase(0, phase_state, skip_grads)

    def stacked(left_rows, right_rows):
        return lax.dot_general(
            left_rows, right_rows, (((0, 1), (0, 1)), ((), ())), preferred_element_type=jnp.float32
        )

    summed = lax.psum_scatter(
        jnp.concatenate(
            [
                stacked(grad_store[0], grad_store[1]),
                stacked(grad_store[2], grad_store[3]),
                stacked(grad_store[4], grad_store[5]),
                stacked(grad_store[6], grad_store[7]),
            ],
            axis=1,
        ).astype(jnp.bfloat16),
        "tok",
        scatter_dimension=0,
        tiled=True,
    ).astype(jnp.float32)
    grad_qkv = summed[:, : 3 * model_width][None]
    grad_out = summed[:, 3 * model_width : 4 * model_width][None]
    grad_up = summed[:, 4 * model_width : 4 * model_width + hidden_width][None]
    grad_down = summed[:, 4 * model_width + hidden_width :][None]
    return (grad_qkv, grad_out, grad_up, grad_down)


def solution(mesh):
    placed = (
        P(None, "tok", None),
        P("section"),
        P("section", None, None),
        P("section", None, None),
        P("section", None, None),
        P("section", None, None),
        P(),
        P(None, "tok", None),
        P(None, "tok", None),
        P(None, "tok"),
        P(None, "tok"),
    )
    return jax.shard_map(
        body,
        mesh=mesh,
        in_specs=placed,
        out_specs=(
            P("section", "tok", None),
            P("section", "tok", None),
            P("section", "tok", None),
            P("section", "tok", None),
        ),
        check_vma=False,
    )
```

profile of v0, /device:TPU:35, one launch (start us, length us, event | category | flops | bytes accessed | tf_op | source)
XLA Modules:
  0.0 2451.4 jit_solution(3221428386178554336)
XLA Ops:
  9.8 227.6 %while.127 = (s32[]{:T(128)}, bf16[2,128,512]{2,1,0:T(8,128)(2,1)S(1)}, bf16[2,384,512]{2,1,0:T(8,128)(2,1)}, bf16[2,128,512]{2,1,0:T(8,128)(2,1)S(1)}, s32[]{:T...) while((s32[]{:T(128)}, ...), condition=%wide.region_12.13_spmd, body=%wide.region_0.12_spmd.sunk | while | flops 1152250240 | bytes 33995968 | solution.py:223
  25.3 7.7 collective-permute-done.2
  43.5 12.9 conditional.12
  72.0 12.9 conditional.12
  104.1 14.8 collective-permute-start.2
  153.3 11.2 collective-permute-start.2
  198.8 14.3 collective-permute-start.2
  239.0 8.9 collective-permute-start.13
  247.9 6.5 collective-permute-done.13
  254.4 21.1 collective-permute-start.14
  281.3 5.8 collective-permute-start.15
  289.5 8.1 collective-permute-done.15
  297.7 205.9 %while.128 = (s32[]{:T(128)}, bf16[2,128,512]{2,1,0:T(8,128)(2,1)S(1)}, bf16[2,384,512]{2,1,0:T(8,128)(2,1)}, bf16[2,128,512]{2,1,0:T(8,128)(2,1)S(1)}, s32[]{:T...) while((s32[]{:T(128)}, ...), condition=%wide.region_25.26_spmd, body=%wide.region_13.25_spmd.sunk | while | flops 1152512384 | bytes 34127048 | solution.py:223
  419.8 15.8 collective-permute-start.5
  450.9 22.8 collective-permute-start.5
  489.1 8.8 collective-permute-start.5
  514.4 365.4 %while.129 = (s32[]{:T(128)}, f32[2,128,512]{2,1,0:T(8,128)}, bf16[2,128,512]{2,1,0:T(8,128)(2,1)}, bf16[2,128,512]{2,1,0:T(8,128)(2,1)}, bf16[2,128,1536]{2,1,0...) while((s32[]{:T(128)}, f32[2,128,512]{2,1,0:T(8,128)}, ...), condition=%wide.region_56.57_spmd, body=%wide.region_30.56_spmd.sunk | while | flops 2145527552 | bytes 178293456 | solution.py:342
  515.9 6.7 conditional.14
  556.7 6.7 conditional.14
  595.0 6.7 conditional.14
  635.9 6.7 conditional.14
  676.1 6.7 conditional.14
  716.9 6.7 conditional.14
  757.0 6.7 conditional.14
  798.2 6.7 conditional.14
  839.4 6.7 conditional.14
  881.6 16.4 collective-permute-start.17
  898.0 6.5 collective-permute-done.17
  904.5 533.3 %collective-permute-start.18 = (bf16[2,128,512]{2,1,0:T(8,128)(2,1)S(1)}, bf16[2,128,512]{2,1,0:T(8,128)(2,1)S(1)}, u32[]{:S(2)}, u32[]{:S(2)}) collective-permute-start(bf16[2,128,512]{2,1,0:T(8,128)(2,1)S(1)} %collective-permute-done.17), channel_id=1, source_target_pairs={{0,64},{64,0},{16,80},{80,16},{32,96},{96,32},{48,112},{112,48},{1... | collective-permute-start | bytes 786440 | tf_op jit(solution)/shard_map/ppermute | solution.py:41
  1437.8 6.0 collective-permute-done.18
  1447.6 6.6 collective-permute-done.19
  1454.2 883.1 %while.130 = (s32[]{:T(128)}, f32[2,128,512]{2,1,0:T(8,128)}, bf16[2,128,512]{2,1,0:T(8,128)(2,1)}, bf16[2,128,1536]{2,1,0:T(8,128)(2,1)}, bf16[2,128,512]{2,1,0...) while((s32[]{:T(128)}, f32[2,128,512]{2,1,0:T(8,128)}, ...), condition=%wide.region_83.84_spmd, body=%wide.region_57.83_spmd.sunk | while | flops 2145724160 | bytes 176982864 | solution.py:342
  1455.9 6.6 conditional.16
  1496.4 6.6 conditional.16
  1503.1 11.5 collective-permute-start.9
  1540.9 6.6 conditional.16
  1577.5 6.6 conditional.16
  1614.6 6.6 conditional.16
  1651.7 6.6 conditional.16
  1687.0 348.5 %collective-permute-done.11 = bf16[128,512]{1,0:T(8,128)(2,1)S(1)} collective-permute-done((bf16[128,512]{1,0:T(8,128)(2,1)}, bf16[128,512]{1,0:T(8,128)(2,1)S(1)}, u32[]{:S(2)}, u32[]{:S(2)}) %collective-permute-start.11) | collective-permute-done | bytes 131104 | tf_op jit(solution)/shard_map/while/body/eval_jaxpr/ppermute | solution.py:47
  2038.6 31.3 %conditional.16 = (f32[128,512]{1,0:T(8,128)}, bf16[128,512]{1,0:T(8,128)(2,1)}, bf16[128,2048]{1,0:T(8,128)(2,1)}, bf16[128,2048]{1,0:T(8,128)(2,1)}, bf16[128,...) conditional(s32[]{:T(128)} %convert_element_type.594, ...), branch_computations={%region_59.59_spmd, %region_60.69_spmd} | conditional | flops 1422062720 | bytes 52744016 | solution.py:297
  2070.0 5.7 collective-permute-start.9
  2092.8 35.3 %conditional.17 = (bf16[128,512]{1,0:T(8,128)(2,1)}, bf16[128,1536]{1,0:T(8,128)(2,1)}, bf16[128,512]{1,0:T(8,128)(2,1)}) conditional(s32[]{:T(128)} %convert_element_type.594, () %tuple.512, (s32[]{:T(128)}, bf16[384,512]{1,0:T(8,128)(2,1)}, bf16[512,512]{1,0:T(8,128)(2,1)S(1)}, bf16[256,1536]{1,0:T(8,128)(2,1)}, ...), branch_computations={%region_70.70_spmd, %region_71.81_spmd} | conditional | flops 720188032 | bytes 75868856 | solution.py:302
  2143.3 31.3 %conditional.16 = (f32[128,512]{1,0:T(8,128)}, bf16[128,512]{1,0:T(8,128)(2,1)}, bf16[128,2048]{1,0:T(8,128)(2,1)}, bf16[128,2048]{1,0:T(8,128)(2,1)}, bf16[128,...) conditional(s32[]{:T(128)} %convert_element_type.594, ...), branch_computations={%region_59.59_spmd, %region_60.69_spmd} | conditional | flops 1422062720 | bytes 52744016 | solution.py:297
  2197.5 35.3 %conditional.17 = (bf16[128,512]{1,0:T(8,128)(2,1)}, bf16[128,1536]{1,0:T(8,128)(2,1)}, bf16[128,512]{1,0:T(8,128)(2,1)}) conditional(s32[]{:T(128)} %convert_element_type.594, () %tuple.512, (s32[]{:T(128)}, bf16[384,512]{1,0:T(8,128)(2,1)}, bf16[512,512]{1,0:T(8,128)(2,1)S(1)}, bf16[256,1536]{1,0:T(8,128)(2,1)}, ...), branch_computations={%region_70.70_spmd, %region_71.81_spmd} | conditional | flops 720188032 | bytes 75868856 | solution.py:302
  2243.1 6.6 conditional.16
  2271.4 59.4 %collective-permute-start.11 = (bf16[128,512]{1,0:T(8,128)(2,1)}, bf16[128,512]{1,0:T(8,128)(2,1)S(1)}, u32[]{:S(2)}, u32[]{:S(2)}) collective-permute-start(bf16[128,512]{1,0:T(8,128)(2,1)} %get-tuple-element.3161), channel_id=1, source_target_pairs={{16,0},{32,16},{48,32},{64,48},{80,64},{96,80},{112,96},{128,112},... | collective-permute-start | bytes 393224 | tf_op jit(solution)/shard_map/while/body/eval_jaxpr/ppermute | solution.py:47
  2346.2 95.0 %reduce-scatter.2.cloned.1.call-done = bf16[32,6144]{1,0:T(8,128)(2,1)} async-done(((bf16[512,6144]{1,0:T(8,128)(2,1)}), bf16[32,6144]{1,0:T(8,128)(2,1)}) %reduce-scatter.2.cloned.1.call-update) | async-done | bytes 393232 | tf_op jit(solution)/shard_map/reduce_scatter | solution.py:363
  (1995 shorter events, 1217.9 us)
Async XLA Ops:
  7.2 2434.0 %reduce-scatter.2.cloned.1.call-start = ((), (), s32[]{:S(2)}) async-start(), calls=%async_computation.1 | async-start | bytes 6684672 | tf_op jit(solution)/shard_map/reduce_scatter | solution.py:363
  16.4 16.6 collective-permute-start.2
  104.1 19.1 collective-permute-start.2
  153.3 15.4 collective-permute-start.2
  198.8 18.6 collective-permute-start.2
  239.0 15.4 collective-permute-start.13
  254.4 26.8 %collective-permute-start.14 = (bf16[2,128,512]{2,1,0:T(8,128)(2,1)S(1)}, bf16[2,128,512]{2,1,0:T(8,128)(2,1)S(1)}, u32[]{:S(2)}, u32[]{:S(2)}) collective-permute-start(bf16[2,128,512]{2,1,0:T(8,128)(2,1)S(1)} %collective-permute-done.13), channel_id=1, source_target_pairs={{0,64},{64,0},{16,80},{80,16},{32,96},{96,32},{48,112},{112,48},{1... | collective-permute-start | bytes 786440 | tf_op jit(solution)/shard_map/ppermute | solution.py:41
  281.3 16.4 collective-permute-start.15
  419.8 19.9 collective-permute-start.5
  450.9 27.0 %collective-permute-start.5 = (bf16[128,512]{1,0:T(8,128)(2,1)S(1)}, bf16[128,512]{1,0:T(8,128)(2,1)S(1)}, u32[]{:S(2)}, u32[]{:S(2)}) collective-permute-start(bf16[128,512]{1,0:T(8,128)(2,1)S(1)} %get-tuple-element.3506), channel_id=1, source_target_pairs={{0,16},{16,32},{32,48},{48,64},{64,80},{80,96},{96,112},{112,128},... | collective-permute-start | bytes 393224 | tf_op jit(solution)/shard_map/while/body/eval_jaxpr/ppermute | solution.py:47
  489.1 13.0 collective-permute-start.5
  522.5 15.9 collective-permute-start.6
  526.5 11.9 collective-permute-start.7
  563.4 13.9 collective-permute-start.6
  601.6 16.5 collective-permute-start.6
  642.6 15.5 collective-permute-start.6
  682.7 15.5 collective-permute-start.6
  702.1 12.2 collective-permute-start.8
  723.5 15.5 collective-permute-start.6
  763.7 15.5 collective-permute-start.6
  783.1 12.6 collective-permute-start.8
  804.9 15.5 collective-permute-start.6
  824.3 12.6 collective-permute-start.8
  846.1 15.5 collective-permute-start.6
  865.5 12.6 collective-permute-start.8
  881.6 22.9 collective-permute-start.17
  904.5 539.2 %collective-permute-start.18 = (bf16[2,128,512]{2,1,0:T(8,128)(2,1)S(1)}, bf16[2,128,512]{2,1,0:T(8,128)(2,1)S(1)}, u32[]{:S(2)}, u32[]{:S(2)}) collective-permute-start(bf16[2,128,512]{2,1,0:T(8,128)(2,1)S(1)} %collective-permute-done.17), channel_id=1, source_target_pairs={{0,64},{64,0},{16,80},{80,16},{32,96},{96,32},{48,112},{112,48},{1... | collective-permute-start | bytes 786440 | tf_op jit(solution)/shard_map/ppermute | solution.py:41
  1462.6 17.3 collective-permute-start.10
  1462.6 17.3 collective-permute-start.9
  1503.1 23.8 collective-permute-start.10
  1503.1 23.8 collective-permute-start.9
  1547.6 15.9 collective-permute-start.10
  1547.6 15.9 collective-permute-start.9
  1584.2 16.1 collective-permute-start.10
  1584.2 16.1 collective-permute-start.9
  1621.2 16.2 collective-permute-start.10
  1621.2 16.2 collective-permute-start.9
  1658.4 17.7 collective-permute-start.10
  1658.4 17.7 collective-permute-start.9
  1680.0 355.5 %collective-permute-start.11 = (bf16[128,512]{1,0:T(8,128)(2,1)}, bf16[128,512]{1,0:T(8,128)(2,1)S(1)}, u32[]{:S(2)}, u32[]{:S(2)}) collective-permute-start(bf16[128,512]{1,0:T(8,128)(2,1)} %get-tuple-element.3161), channel_id=1, source_target_pairs={{16,0},{32,16},{48,32},{64,48},{80,64},{96,80},{112,96},{128,112},... | collective-permute-start | bytes 393224 | tf_op jit(solution)/shard_map/while/body/eval_jaxpr/ppermute | solution.py:47
  2069.9 21.0 collective-permute-start.10
  2070.0 21.0 collective-permute-start.9
  2128.1 12.2 collective-permute-start.11
  2174.6 21.0 collective-permute-start.10
  2174.6 21.0 collective-permute-start.9
  2249.7 17.7 collective-permute-start.10
  2249.7 17.7 collective-permute-start.9
  2271.4 64.4 %collective-permute-start.11 = (bf16[128,512]{1,0:T(8,128)(2,1)}, bf16[128,512]{1,0:T(8,128)(2,1)S(1)}, u32[]{:S(2)}, u32[]{:S(2)}) collective-permute-start(bf16[128,512]{1,0:T(8,128)(2,1)} %get-tuple-element.3161), channel_id=1, source_target_pairs={{16,0},{32,16},{48,32},{64,48},{80,64},{96,80},{112,96},{128,112},... | collective-permute-start | bytes 393224 | tf_op jit(solution)/shard_map/while/body/eval_jaxpr/ppermute | solution.py:47
  (499 other events, 4330.7 us)
Sparse Core Ops, SparseCore 0:
  2346.3 94.8 reduce-scatter.1
where the time goes:
time: 2490 us; the launch traced here: 2450 us
  starting transfers between devices  957 us (38%)
  waiting for transfers between devices  566 us (23%)
  local copies, waits for them, and re-layouts  423 us (17%)
  other arithmetic  410 us (16%)
  matrix products  62 us (2%)
    ppermute x8, starting transfers between devices, from_partner(): return lax.ppermute(block, axis, route)  589 us
    ppermute x36, waiting for transfers between devices, passed_along(): return lax.ppermute(block, axis, route)  388 us
    ppermute x36, starting transfers between devices, passed_along(): return lax.ppermute(block, axis, route)  224 us
    scatter x90, other arithmetic, retreat(): stack.at[slot_clip].set(jnp.where(active, piece, stack[slot_clip]))  155 us
    another operation x218, local copies, waits for them, and re-layouts  147 us
    ppermute x36, starting transfers between devices, with_halo(): lax.ppermute(head, axis, [((i + 1) % count, i) for i in range(count)])  141 us
    reduce_scatter x1, waiting for transfers between devices, body(): lax.psum_scatter(jnp.concatenate([stacked(grad_store[0], grad_store[1]),...  95 us
    dynamic_slice x144, local copies, waits for them, and re-layouts, retreat(): stack[slot_clip]  87.3 us
  transfers between devices with their start and end apart: 117, of which 53 were waited for; matrix products, arithmetic and copies ran while one was open for 16% of the time, Pallas kernels for 0%

commit v1 on v0

v1 whole, which is shorter than its diff:
```python
import math

import jax
import jax.numpy as jnp
from jax import lax
from jax.experimental import pallas as pl
from jax.experimental.pallas import tpu as pltpu
from jax.sharding import PartitionSpec as P

HEAD_DIM = 32
WIN = 128
LANES = 128
GROUP = LANES // HEAD_DIM

norm_eps = 1e-05
logit_scale = 10.0
floor_share = 0.75
decay_base = 0.8
norm_floor = floor_share * math.sqrt(HEAD_DIM)

F32 = jnp.float32
BF16 = jnp.bfloat16
VMEM_LIMIT = 48 * 1024 * 1024

SLOT = 512
X_AT, QKV_AT, LEFT_AT, RIGHT_AT, Z_AT, GX_AT, LOW_SLOTS = 0, 1, 4, 11, 20, 21, 22
LEFT_SLOTS, RIGHT_SLOTS = 7, 9
Y_AT, U_AT, WIDE_SLOTS = 0, 1, 5
LOW_STORE, WIDE_STORE = 224, 112

NN = (((1,), (0,)), ((), ()))
NT = (((1,), (1,)), ((), ()))
TN = (((0,), (0,)), ((), ()))


def dot(left, right, dims=NN):
    return lax.dot_general(left, right, dims, preferred_element_type=F32)


def norm_parts(values):
    center = values - jnp.mean(values, axis=-1, keepdims=True)
    scale = lax.rsqrt(jnp.mean(center * center, axis=-1, keepdims=True) + norm_eps)
    return center * scale, scale


def norm_back(normed, scale, grad):
    grad_mean = jnp.mean(grad, axis=-1, keepdims=True)
    grad_dot = jnp.mean(grad * normed, axis=-1, keepdims=True)
    return scale * (grad - grad_mean - normed * grad_dot)


def joined(first, second, start):
    both = jnp.concatenate([first.astype(F32), second.astype(F32)], axis=0)
    return pltpu.roll(both, lax.rem(2 * WIN - start, 2 * WIN), 0)[:WIN]


def head_sum(values):
    width = values.shape[1]
    rows = lax.broadcasted_iota(jnp.int32, (LANES, LANES), 0) // HEAD_DIM
    cols = lax.broadcasted_iota(jnp.int32, (LANES, LANES), 1) // HEAD_DIM
    same = (rows == cols).astype(BF16)
    high = values.astype(BF16)
    low = (values - high.astype(F32)).astype(BF16)
    parts = []
    for at in range(0, width, LANES):
        parts.append(dot(high[:, at : at + LANES], same) + dot(low[:, at : at + LANES], same))
    return jnp.concatenate(parts, axis=1)


def spread_heads(rows):
    head = lax.broadcasted_iota(jnp.int32, rows.shape, 1) // HEAD_DIM
    zero = jnp.zeros_like(rows)
    return jnp.concatenate([jnp.where(head == h, rows, zero) for h in range(GROUP)], axis=0)


def gather_heads(stacked):
    head = lax.broadcasted_iota(jnp.int32, (WIN, LANES), 1) // HEAD_DIM
    result = stacked[:WIN]
    for h in range(1, GROUP):
        result = jnp.where(head == h, stacked[h * WIN : (h + 1) * WIN], result)
    return result


def unit_rows(rows):
    length = jnp.sqrt(head_sum(rows * rows))
    inverse = 1.0 / jnp.maximum(length, norm_floor)
    return inverse, length > norm_floor


def gelu_parts(lifted):
    root = math.sqrt(2.0 / math.pi)
    square = lifted * lifted
    bend = jnp.tanh(root * lifted * (1.0 + 0.044715 * square))
    return square, bend, root


def weight_views(refs):
    first, up, down = refs
    split = 3 * first.shape[0]
    views = [first.at[:, pl.ds(0, split)], first.at[:, pl.ds(split, first.shape[1] - split)]]
    return views + [up, down]


def fetch(pairs, own, sems):
    for index, (mine, other, into) in enumerate(pairs):

        @pl.when(own == 1)
        def _():
            pltpu.make_async_copy(mine, into, sems.at[index]).start()

        @pl.when(own == 0)
        def _():
            pltpu.make_async_copy(other, into, sems.at[index]).start()

    def arrived(index):
        pltpu.make_async_copy(pairs[index][0], pairs[index][2], sems.at[index]).wait()

    return arrived


def forward_kernel(mode, section, *refs):
    info_ref = refs[0]

    @pl.when(info_ref[section, 2] == 1)
    def _():
        forward_section(mode, section, *refs)


def forward_section(mode, section, *refs):
    refs = list(refs)
    info_ref, cur_ref, nxt_ref = refs[:3]
    refs = refs[3:]
    skip_ref = refs.pop(0) if mode == "skip" else None
    mine, other = weight_views(refs[:3]), weight_views(refs[3:6])
    low_store, wide_store, z_ref = refs[8:11]
    held = refs[11:15]
    x_ref, qkv_ref, left_ref, y_ref, u_ref, sems, out_sems = refs[15:]
    arrived = fetch(list(zip(mine, other, held)), info_ref[section, 1], sems)
    w_qkv, w_out, w_up, w_down = held
    low_base, wide_base = section % 2 * LOW_SLOTS, section % 2 * WIDE_SLOTS
    out_copies = []

    def keep(room, store, at):
        goal = store.at[pl.ds(at, room.shape[0])]
        copy = pltpu.make_async_copy(room, goal, out_sems.at[len(out_copies)])
        copy.start()
        out_copies.append(copy)

    x = joined(cur_ref[...], nxt_ref[...], info_ref[section, 0])
    if mode == "skip":
        x = (x + skip_ref[...].astype(F32)).astype(BF16).astype(F32)
    if mode == "double":
        x = x + x
    x_ref[0] = x.astype(BF16)
    keep(x_ref, low_store, low_base + X_AT)
    n1 = norm_parts(x)[0].astype(BF16)
    left_ref[0] = n1
    arrived(0)
    q, k, v = [dot(n1, w_qkv[:, at : at + SLOT]).astype(BF16) for at in (0, SLOT, 2 * SLOT)]
    qkv_ref[0] = q
    qkv_ref[1] = k
    qkv_ref[2] = v
    keep(qkv_ref, low_store, low_base + QKV_AT)
    q = q.astype(F32)
    k = k.astype(F32)
    qh = (q * (logit_scale * unit_rows(q)[0])).astype(BF16)
    kh = (k * unit_rows(k)[0]).astype(BF16)
    ones = jnp.ones((WIN, LANES), BF16)
    attended = []
    for at in range(0, SLOT, LANES):
        scores = dot(spread_heads(qh[:, at : at + LANES]), kh[:, at : at + LANES], NT)
        weights = jnp.exp(scores).astype(BF16)
        mixed = dot(weights, jnp.concatenate([v[:, at : at + LANES], ones], axis=1))
        attended.append(gather_heads(mixed[:, :LANES] / mixed[:, LANES:]))
    att = jnp.concatenate(attended, axis=1).astype(BF16)
    left_ref[1] = att
    arrived(1)
    y = x + dot(att, w_out[...])
    y_ref[0] = y
    keep(y_ref, wide_store, wide_base + Y_AT)
    n2 = norm_parts(y)[0].astype(BF16)
    left_ref[2] = n2
    arrived(2)
    for index in range(LEFT_SLOTS - 3):
        u = dot(n2, w_up[:, index * SLOT : (index + 1) * SLOT])
        u_ref[index] = u
        bend = gelu_parts(u)[1]
        left_ref[3 + index] = (0.5 * u * (1.0 + bend)).astype(BF16)
    keep(u_ref, wide_store, wide_base + U_AT)
    keep(left_ref, low_store, low_base + LEFT_AT)
    arrived(3)
    z = y
    for index in range(LEFT_SLOTS - 3):
        z = z + dot(left_ref[3 + index], w_down[:, index * SLOT : (index + 1) * SLOT], NT)
    z_ref[...] = z.astype(BF16)
    posted = pltpu.make_async_copy(z_ref, low_store.at[low_base + Z_AT], out_sems.at[5])
    posted.start()
    for copy in out_copies + [posted]:
        copy.wait()


def backward_kernel(mode, last, section, *refs):
    info_ref = refs[0]

    @pl.when(info_ref[section, 2] == 1)
    def _():
        backward_section(mode, last, section, *refs)


def backward_section(mode, last, section, *refs):
    refs = list(refs)
    info_ref = refs.pop(0)
    if mode == "head":
        z_ref, aim_ref, head_ref = refs[:3]
        refs = refs[3:]
    else:
        cur_ref, prv_ref = refs[:2]
        refs = refs[2:]
    skip_ref = refs.pop(0) if mode == "skip" else None
    mine, other = weight_views(refs[:3]), weight_views(refs[3:6])
    low_store, wide_store, gx_ref = refs[8:11]
    held = refs[11:15]
    x_ref, qkv_ref, right_ref, y_ref, u_ref, sems, in_sems, out_sem = refs[15:]
    low_base, wide_base = section % 2 * LOW_SLOTS, section % 2 * WIDE_SLOTS
    in_copies = [
        pltpu.make_async_copy(store.at[pl.ds(at, room.shape[0])], room, in_sems.at[index])
        for index, (room, store, at) in enumerate(
            [
                (x_ref, low_store, low_base + X_AT),
                (y_ref, wide_store, wide_base + Y_AT),
                (u_ref, wide_store, wide_base + U_AT),
                (qkv_ref, low_store, low_base + QKV_AT),
            ]
        )
    ]
    pairs = list(zip(mine, other, held))
    arrived = fetch(pairs[::-1], info_ref[section, 1], sems)
    for index in (2, 1, 3, 0):
        in_copies[index].start()
    w_qkv, w_out, w_up, w_down = held
    hidden_slots = u_ref.shape[0]

    if mode == "head":
        normed, scale = norm_parts(z_ref[...].astype(F32))
        channels = head_ref.shape[1]
        predicted = dot(normed.astype(BF16), head_ref[...])
        target = aim_ref[:, :channels].astype(F32)
        bucket = aim_ref[:, channels:].astype(F32)
        decay = jnp.exp(bucket * math.log(decay_base))
        loss_scale = 1.0 / math.sqrt(2 * 16 * WIN)
        grad_pred = (decay * (predicted - target) * loss_scale).astype(BF16)
        dz = norm_back(normed, scale, dot(grad_pred, head_ref[...], NT))
    else:
        dz = joined(prv_ref[...], cur_ref[...], WIN - info_ref[section, 3])
        if mode == "skip":
            dz = dz + skip_ref[...].astype(F32)
        if mode == "double":
            dz = dz + dz
    g_m = dz.astype(BF16)
    right_ref[4 + hidden_slots] = g_m
    arrived(0)
    in_copies[2].wait()
    for index in range(hidden_slots):
        dh = dot(g_m, w_down[:, index * SLOT : (index + 1) * SLOT])
        u = u_ref[index]
        square, bend, root = gelu_parts(u)
        slope = 0.5 * (1.0 + bend) + (0.5 * root) * u * (1.0 - bend * bend) * (
            1.0 + 3 * 0.044715 * square
        )
        right_ref[4 + index] = (slope * dh).astype(BF16)
    arrived(1)
    dn2 = dot(right_ref[4], w_up[:, :SLOT], NT)
    for index in range(1, hidden_slots):
        dn2 = dn2 + dot(right_ref[4 + index], w_up[:, index * SLOT : (index + 1) * SLOT], NT)
    in_copies[1].wait()
    normed, scale = norm_parts(y_ref[0])
    dy = dz + norm_back(normed, scale, dn2)
    g_a = dy.astype(BF16)
    right_ref[3] = g_a
    arrived(2)
    da = dot(g_a, w_out[...], NT).astype(BF16)

    in_copies[3].wait()
    q = qkv_ref[0].astype(F32)
    k = qkv_ref[1].astype(F32)
    q_inv, q_free = unit_rows(q)
    k_inv, k_free = unit_rows(k)
    qu = q * q_inv
    ku = k * k_inv
    qh = (logit_scale * qu).astype(BF16)
    kh = ku.astype(BF16)
    ones = jnp.ones((WIN, LANES), BF16)
    dq_parts, dk_parts = [], []
    for at in range(0, SLOT, LANES):
        kg = kh[:, at : at + LANES]
        vg = qkv_ref[2, :, at : at + LANES]
        queries = spread_heads(qh[:, at : at + LANES])
        weights = jnp.exp(dot(queries, kg, NT))
        probs = weights / dot(weights.astype(BF16), ones)
        probs_low = probs.astype(BF16)
        grads = spread_heads(da[:, at : at + LANES])
        dp = dot(grads, vg, NT)
        ds = (probs * (dp - dot((probs * dp).astype(BF16), ones))).astype(BF16)
        right_ref[2, :, at : at + LANES] = dot(probs_low, grads, TN).astype(BF16)
        dq_parts.append(gather_heads(dot(ds, kg)))
        dk_parts.append(dot(ds, queries, TN))
    dqh = logit_scale * jnp.concatenate(dq_parts, axis=1)
    dkh = jnp.concatenate(dk_parts, axis=1)
    dq = q_inv * (dqh - jnp.where(q_free, qu * head_sum(qu * dqh), 0.0))
    dk = k_inv * (dkh - jnp.where(k_free, ku * head_sum(ku * dkh), 0.0))
    right_ref[0] = dq.astype(BF16)
    right_ref[1] = dk.astype(BF16)
    right_goal = low_store.at[pl.ds(low_base + RIGHT_AT, RIGHT_SLOTS)]
    out_copy = pltpu.make_async_copy(right_ref, right_goal, out_sem.at[0])
    out_copy.start()
    arrived(3)
    in_copies[0].wait()
    if last:
        gx_ref[...] = g_a
    else:
        dn1 = dot(right_ref[0], w_qkv[:, :SLOT], NT)
        for index in (1, 2):
            dn1 = dn1 + dot(right_ref[index], w_qkv[:, index * SLOT : (index + 1) * SLOT], NT)
        normed, scale = norm_parts(x_ref[0].astype(F32))
        gx_ref[...] = (dy + norm_back(normed, scale, dn1)).astype(BF16)
    posted = pltpu.make_async_copy(gx_ref, low_store.at[low_base + GX_AT], out_sem.at[1])
    posted.start()
    out_copy.wait()
    posted.wait()


def pick_kernel(ranges, *refs):
    store_ref = refs[1]
    outs, sems = refs[2:-1], refs[-1]
    copies = []
    for index, (at, count) in enumerate(ranges):
        source = store_ref.at[pl.ds(at, count)]
        copies.append(pltpu.make_async_copy(source, outs[index], sems.at[index]))
        copies[-1].start()
    for copy in copies:
        copy.wait()


def weight_kernel(inner, *refs):
    info_ref, store_ref = refs[:2]
    received = refs[2:6]
    near_refs, far_refs = refs[6 : 6 + inner], refs[6 + inner : 6 + 2 * inner]
    left, right, room, sems = refs[6 + 2 * inner :]
    copies = []
    for into, at, count, got in ((left, LEFT_AT, LEFT_SLOTS, 0), (right, RIGHT_AT, RIGHT_SLOTS, 1)):
        for index in range(count):
            columns = pl.ds(index * SLOT, SLOT)
            for part in range(2):
                goal = into.at[pl.ds(part * WIN, WIN), columns]
                sem = sems.at[len(copies)]
                for side in range(2):

                    @pl.when(info_ref[0] == side)
                    def _():
                        if part == 0:
                            source = store_ref.at[side * LOW_SLOTS + at + index]
                        else:
                            source = received[2 * got + side].at[index]
                        pltpu.make_async_copy(source, goal, sem).start()

                copies.append(pltpu.make_async_copy(store_ref.at[at + index], goal, sem))
    for copy in copies:
        copy.wait()
    width, step = room.shape
    hidden = right.shape[1] - 5 * width
    total = 4 * width + 2 * hidden
    outer = near_refs[0].shape[0]
    strip = near_refs[0].shape[1]
    split = near_refs[0].shape[2]
    for at in range(0, total, step):
        if at < 3 * width:
            first, second = left[:, :width], right[:, at : at + step]
        elif at < 4 * width:
            first, second = left[:, width : 2 * width], right[:, at : at + step]
        elif at < 4 * width + hidden:
            first, second = left[:, 2 * width : 3 * width], right[:, at : at + step]
        else:
            start = 3 * width + at - 4 * width - hidden
            first, second = right[:, 4 * width + hidden :], left[:, start : start + step]
        room[...] = dot(first, second, TN).astype(BF16)
        for distance in range(inner):
            if at < split:
                column = lax.rem(info_ref[1] + distance, inner)
            else:
                column = lax.rem(info_ref[2] + distance, outer)
            for line in range(outer):
                if at < split:
                    owner = line * inner + column
                    near_refs[distance][line, :, at : at + step] = room[
                        pl.ds(owner * strip, strip), :
                    ]
                else:
                    owner = column * inner + line
                    far_refs[distance][line, :, at - split : at - split + step] = room[
                        pl.ds(owner * strip, strip), :
                    ]


VMEM = pl.BlockSpec(memory_space=pltpu.VMEM)
SMEM = pl.BlockSpec(memory_space=pltpu.SMEM)
HBM = pl.BlockSpec(memory_space=pltpu.HBM)


def body(tokens, offsets, w_qkv, w_out, w_up, w_down, w_head, era5t, era5, flags, buckets):
    section_count = lax.axis_size("section")
    tok_count = lax.axis_size("tok")
    pair_count = section_count // 2
    half_pairs = pair_count // 2
    section_index = lax.axis_index("section")
    tok_index = lax.axis_index("tok")
    pair_index = section_index // 2
    core_index = section_index % 2
    micro_count, row_count, width = tokens.shape
    hidden = w_up.shape[2]
    mine = (jnp.concatenate([w_qkv[0], w_out[0]], axis=1), w_up[0], w_down[0])

    def place(section, tok):
        return section * tok_count + tok % tok_count

    def moved(block, route):
        return lax.ppermute(block, ("section", "tok"), route)

    def hop(block, low_pair, step, tok_shift):
        route = []
        for pair in range(pair_count - 1):
            if pair % 2 == low_pair % 2:
                for core in range(2):
                    for tok in range(tok_count):
                        low, high = 2 * pair + core, 2 * pair + 2 + core
                        origin, goal = (low, high) if step > 0 else (high, low)
                        route.append((place(origin, tok + tok_shift), place(goal, tok)))
        return moved(block, route)

    def along(block, tok_shift, sections):
        route = []
        for section in sections:
            for tok in range(tok_count):
                route.append((place(section, tok + tok_shift), place(section, tok)))
        return moved(block, route)

    def mirror(block, pairs):
        route = []
        for one in pairs:
            for goal in (pair_count - 1 - one,):
                for core in range(2):
                    for tok in range(tok_count):
                        origin = 2 * (pair_count - 1 - goal) + core
                        route.append((place(origin, tok), place(2 * goal + core, tok)))
        return moved(block, sorted(route))

    outer_pairs = [pair for pair in range(pair_count) if pair not in (half_pairs - 1, half_pairs)]

    def swap(block, origins):
        route = [
            (place(section, tok), place(section ^ 1, tok))
            for section in range(section_count)
            if section % 2 in origins
            for tok in range(tok_count)
        ]
        return moved(block, route)

    everyone = range(section_count)
    last_encoder = section_count // 2 - 1
    encoders = range(last_encoder - 1)
    inner_encoders = range(last_encoder - 1, last_encoder + 1)
    inner_decoders = range(last_encoder + 1, last_encoder + 3)
    decoders = range(last_encoder + 3, section_count)

    def far_along(block, blocks, limit, sign, sections):
        bit = 1
        while bit <= limit:
            shifted = along(block, sign * bit, sections)
            block = jnp.where((blocks // bit) % 2 == 1, shifted, block)
            bit *= 2
        return block

    def together(*arrays):
        return lax.optimization_barrier(arrays)

    table = lax.all_gather(offsets, "section").reshape(section_count)
    order = jnp.arange(section_count)
    before = jnp.where(order == 0, 0, jnp.roll(table, 1))
    shifts = (table - before + WIN) % WIN
    start = jnp.sum(jnp.where(order[:, None] >= order[None, :], shifts[None, :], 0), axis=1)

    other = tuple(swap(weight, (0, 1)) for weight in mine)

    info = jnp.stack(
        [
            shifts,
            (core_index == order % 2).astype(jnp.int32),
            (pair_index == order // 2).astype(jnp.int32),
            jnp.roll(shifts, -1),
        ],
        axis=1,
    ).astype(jnp.int32)

    weight_rooms = [
        pltpu.VMEM(weight.shape[1:], BF16) for weight in (w_qkv, w_out, w_up, w_down)
    ]
    weight_sems = pltpu.SemaphoreType.DMA((4,))
    rows_bf = jax.ShapeDtypeStruct((WIN, width), BF16)
    store_shapes = (
        jax.ShapeDtypeStruct((LOW_STORE, WIN, SLOT), BF16),
        jax.ShapeDtypeStruct((WIDE_STORE, WIN, SLOT), F32),
    )
    channels = era5.shape[2]
    hidden_slots = hidden // SLOT

    def room(count, dtype):
        return pltpu.VMEM((count, WIN, SLOT), dtype)

    params = pltpu.CompilerParams(vmem_limit_bytes=VMEM_LIMIT)

    def section_call(kernel, name, inputs, stores, rooms, sems):
        inputs = [info, *inputs]
        first = len(inputs) + 6
        result = pl.pallas_call(
            kernel,
            out_shape=store_shapes + (rows_bf,),
            in_specs=[SMEM] + [VMEM] * (len(inputs) - 1) + [HBM] * 8,
            out_specs=(HBM, HBM, VMEM),
            input_output_aliases={first: 0, first + 1: 1},
            scratch_shapes=weight_rooms
            + rooms
            + [room(1, F32), room(hidden_slots, F32), weight_sems]
            + [pltpu.SemaphoreType.DMA((count,)) for count in sems],
            compiler_params=params,
            name=name,
        )(*inputs, *mine, *other, *stores)
        return tuple(result[:2]), result[2]

    def forward(section, cur, nxt, skip, stores):
        if section < section_count // 2:
            mode = "plain"
        else:
            mode = "double" if section == section_count // 2 else "skip"
        return section_call(
            lambda *refs: forward_kernel(mode, section, *refs),
            "forward_" + mode,
            [cur, nxt] + ([skip] if mode == "skip" else []),
            stores,
            [room(1, BF16), room(3, BF16), room(LEFT_SLOTS, BF16)],
            (6,),
        )

    def backward(section, sources, skip, stores):
        if section == section_count - 1:
            mode = "head"
        elif section >= section_count // 2:
            mode = "plain"
        else:
            mode = "double" if section == section_count // 2 - 1 else "skip"
        return section_call(
            lambda *refs: backward_kernel(mode, section == 0, section, *refs),
            "backward_" + mode,
            [*sources] + ([skip] if mode == "skip" else []),
            stores,
            [room(1, BF16), room(3, BF16), room(RIGHT_SLOTS, BF16)],
            (4, 2),
        )

    def picked(stores, *ranges):
        result = pl.pallas_call(
            lambda *refs: pick_kernel(ranges, *refs),
            out_shape=(store_shapes[0],)
            + tuple(jax.ShapeDtypeStruct((count, WIN, SLOT), BF16) for _, count in ranges),
            in_specs=[HBM],
            out_specs=(HBM,) + (VMEM,) * len(ranges),
            input_output_aliases={0: 0},
            scratch_shapes=[pltpu.SemaphoreType.DMA((len(ranges),))],
            name="pick",
        )(stores[0])
        return (result[0], stores[1]), result[1:]

    def unwritten():
        return pl.pallas_call(
            lambda *refs: None,
            out_shape=store_shapes,
            out_specs=(HBM,) * 2,
            name="unwritten",
        )()

    cur = lax.dynamic_index_in_dim(tokens, core_index, 0, False)
    nxt = along(cur, 1, everyone)
    stores = unwritten()
    chosen = jnp.repeat(
        lax.dynamic_index_in_dim(flags, core_index, 0, False), row_count // flags.shape[1]
    )
    target = jnp.where(
        (chosen == 1)[:, None],
        lax.dynamic_index_in_dim(era5t, core_index, 0, False),
        lax.dynamic_index_in_dim(era5, core_index, 0, False),
    )
    bucket = lax.dynamic_index_in_dim(buckets, core_index, 0, False).astype(BF16)
    bucket = jnp.broadcast_to(bucket[:, None], target.shape)
    aim_here = jnp.stack([target, bucket])

    low_reach = start[section_count - 1 - 2 * pair_index] - start[2 * pair_index]
    high_reach = start[section_count - 2 - 2 * pair_index] - start[2 * pair_index + 1]
    reaches = [jnp.abs(low_reach), jnp.abs(high_reach)]
    reaches_seen = [
        jnp.where(pair_index < half_pairs, reaches[slot], reaches[1 - slot]) for slot in range(2)
    ]
    target_reach = start[section_count - 1]

    def cut(first, second, at):
        return lax.dynamic_slice_in_dim(jnp.concatenate([first, second], axis=0), at, WIN, 0)

    def long_shift(blocks, counts, limit, sign, sections):
        near = far_along(blocks, counts, limit, sign, sections)
        return near, along(near, sign, sections)

    def short_shift(block, count, limit, sign, sections):
        blocks = [block]
        for _ in range(limit + 1):
            blocks.append(along(blocks[-1], sign, sections))
        near, beside = blocks[0], blocks[1]
        for index in range(1, limit + 1):
            near = jnp.where(count == index, blocks[index], near)
            beside = jnp.where(count == index, blocks[index + 1], beside)
        return near, beside

    skips = {}
    aim = None
    for pair in range(pair_count):
        low, high = 2 * pair, 2 * pair + 1
        stores, z_low = forward(low, cur, nxt, skips.get(low), stores)
        nxt = along(z_low, 1, everyone)
        stores, z_high = forward(high, z_low, nxt, skips.get(high), stores)
        if pair < pair_count - 1:
            nxt = hop(z_high, pair, 1, 1)
            cur = hop(z_high, pair, 1, 0)
        if pair == half_pairs - 1:
            reach = start[low + 3] - start[low]
            near, beside = short_shift(
                mirror(z_low, (pair,)), reach // WIN, 2, 1, inner_decoders
            )
            skips[low + 3] = cut(near, beside, reach % WIN)
            cur, nxt, skips[low + 3] = together(cur, nxt, skips[low + 3])
            stores, posts = picked(stores, (Z_AT, 1), (LOW_SLOTS + Z_AT, 1))
            post = jnp.concatenate([jnp.concatenate(posts, axis=0), aim_here], axis=2)
            cur, nxt, post = together(cur, nxt, post)
            counts = [
                jnp.concatenate(
                    [
                        jnp.full((1, 1, width), each // WIN),
                        jnp.full((1, 1, channels), target_reach // WIN),
                    ],
                    axis=2,
                )
                for each in reaches_seen
            ]
            near, beside = long_shift(
                mirror(post, outer_pairs),
                jnp.concatenate(counts, axis=0),
                tok_count - 1,
                1,
                decoders,
            )
            outer_skip = [
                cut(near[slot, :, :width], beside[slot, :, :width], reaches_seen[slot] % WIN)
                for slot in range(2)
            ]
            aim = jnp.concatenate(
                [
                    cut(near[slot, :, width:], beside[slot, :, width:], target_reach % WIN)
                    for slot in range(2)
                ],
                axis=1,
            )
            for goal in range(half_pairs + 1, pair_count):
                skips[2 * goal + 1], skips[2 * goal] = outer_skip

    skips = {}
    sources = (z_high, aim, w_head)
    for pair in range(pair_count - 1, -1, -1):
        low, high = 2 * pair, 2 * pair + 1
        stores, gx_high = backward(high, sources, skips.get(high), stores)
        sources = (gx_high, along(gx_high, -1, everyone))
        stores, gx_low = backward(low, sources, skips.get(low), stores)
        if pair > 0:
            prv = hop(gx_low, pair - 1, -1, -1)
            cur = hop(gx_low, pair - 1, -1, 0)
            sources = (cur, prv)
        if pair == half_pairs:
            reach = start[high] - start[high - 3]
            near, beside = short_shift(
                mirror(gx_high, (pair,)), reach // WIN, 2, -1, inner_encoders
            )
            skips[high - 3] = cut(beside, near, WIN - reach % WIN)
            cur, prv, skips[high - 3] = together(cur, prv, skips[high - 3])
            stores, posts = picked(stores, (LOW_SLOTS + GX_AT, 1), (GX_AT, 1))
            cur, prv, post = together(cur, prv, jnp.concatenate(posts, axis=0))
            sources = (cur, prv)
            counts = jnp.stack([each // WIN for each in reaches_seen])[:, None, None]
            near, beside = long_shift(
                mirror(post, outer_pairs), counts, tok_count - 2, -1, encoders
            )
            outer_skip = [
                cut(beside[slot], near[slot], WIN - reaches_seen[slot] % WIN) for slot in range(2)
            ]
            for goal in range(half_pairs - 1):
                skips[2 * goal], skips[2 * goal + 1] = outer_skip
        if pair == half_pairs - 1:
            stores, lefts = picked(
                stores, (LEFT_AT, LEFT_SLOTS), (LOW_SLOTS + LEFT_AT, LEFT_SLOTS)
            )
            left_low = swap(lefts[0], (1,))
            left_high = swap(lefts[1], (0,))
            cur, prv, left_low, left_high = together(cur, prv, left_low, left_high)
            sources = (cur, prv)

    stores, rights = picked(
        stores, (RIGHT_AT, RIGHT_SLOTS), (LOW_SLOTS + RIGHT_AT, RIGHT_SLOTS)
    )
    right_high = swap(rights[1], (0,))
    right_low = swap(rights[0], (1,))
    total = 4 * width + 2 * hidden
    inner = 4
    outer = tok_count // inner
    strip = width // tok_count
    split = 4 * width + hidden
    tok_in, tok_out = tok_index % inner, tok_index // inner
    step = width
    parts = pl.pallas_call(
        lambda *refs: weight_kernel(inner, *refs),
        out_shape=[jax.ShapeDtypeStruct((outer, strip, split), BF16)] * inner
        + [jax.ShapeDtypeStruct((inner, strip, total - split), BF16)] * outer,
        in_specs=[SMEM] + [HBM] * 5,
        out_specs=[VMEM] * (inner + outer),
        scratch_shapes=[
            pltpu.VMEM((2 * WIN, LEFT_SLOTS * SLOT), BF16),
            pltpu.VMEM((2 * WIN, RIGHT_SLOTS * SLOT), BF16),
            pltpu.VMEM((width, step), BF16),
            pltpu.SemaphoreType.DMA((2 * (LEFT_SLOTS + RIGHT_SLOTS),)),
        ],
        compiler_params=params,
        name="weight_grads",
    )(
        jnp.stack([core_index, tok_in, tok_out]).astype(jnp.int32),
        stores[0],
        left_low,
        left_high,
        right_low,
        right_high,
    )
    near_parts, far_parts = parts[:inner], parts[inner:]

    def ring(block, distance, inside):
        route = []
        for tok in range(tok_count):
            far, near = tok // inner, tok % inner
            if inside:
                goal = far * inner + (near + distance) % inner
            else:
                goal = (far + distance) % outer * inner + near
            route.append((tok, goal))
        return lax.ppermute(block, "tok", route)

    def piece(array, index):
        return lax.dynamic_index_in_dim(array, index, 0, False)

    def first_stage(pieces, inside):
        summed = pieces[0].astype(F32)
        for distance in range(1, len(pieces)):
            summed = summed + ring(pieces[distance], distance, inside).astype(F32)
        return summed.astype(BF16)

    def second_stage(summed, position, size, inside):
        result = piece(summed, position).astype(F32)
        for distance in range(1, size):
            sent = piece(summed, (position + distance) % size)
            result = result + ring(sent, distance, inside).astype(F32)
        return result

    near_sums = first_stage(near_parts, True)
    far_sums = first_stage(far_parts, False)
    near_sums, far_sums = together(near_sums, far_sums)
    near_result = second_stage(near_sums, tok_out, outer, False)
    far_result = second_stage(far_sums, tok_in, inner, True)
    grad_qkv = near_result[:, : 3 * width][None]
    grad_out = near_result[:, 3 * width : 4 * width][None]
    grad_up = near_result[:, 4 * width :][None]
    grad_down = far_result[None]
    return (grad_qkv, grad_out, grad_up, grad_down)


def solution(mesh):
    placed = (
        P(None, "tok", None),
        P("section"),
        P("section", None, None),
        P("section", None, None),
        P("section", None, None),
        P("section", None, None),
        P(),
        P(None, "tok", None),
        P(None, "tok", None),
        P(None, "tok"),
        P(None, "tok"),
    )
    return jax.shard_map(
        body,
        mesh=mesh,
        in_specs=placed,
        out_specs=(
            P("section", "tok", None),
            P("section", "tok", None),
            P("section", "tok", None),
            P("section", "tok", None),
        ),
        check_vma=False,
    )
```

time: 2490 us -> 761 us (0.31); the launches traced: 2450 us -> 752 us
  starting transfers between devices: 957 us -> 274 us
  local copies, waits for them, and re-layouts: 423 us -> 27 us
  other arithmetic: 410 us -> 14.9 us
  waiting for transfers between devices: 566 us -> 276 us
  Pallas kernels: 0 us -> 134 us
  matrix products: 62 us -> 0 us
    ppermute x116 -> x84, starting transfers between devices: 957 us -> 274 us  [the longest x72 245 us: moved(): return lax.ppermute(block, ('section', 'tok'), route)]
    scatter x162 -> x0, other arithmetic: 275 us -> none  [the longest x90 155 us: retreat(): stack.at[slot_clip].set(jnp.where(active, piece, stack[slot_clip]))]
    ppermute x116 -> x84, waiting for transfers between devices: 471 us -> 276 us  [the longest x72 217 us: moved(): return lax.ppermute(block, ('section', 'tok'), route)]
    another operation x218 -> x2, local copies, waits for them, and re-layouts: 147 us -> 0.17 us  [the longest x1 0.09 us: body(): jnp.stack([shifts, (core_index == order % 2).astype(jnp.int32), (pair_ind...]
    pallas_call x0 -> x38, Pallas kernels: none -> 134 us  [the longest x32 118 us: section_call(): pl.pallas_call(kernel, out_shape=store_shapes + (rows_bf,), in_specs=[SME...]
    dynamic_slice x198 -> x0, local copies, waits for them, and re-layouts: 125 us -> none  [the longest x144 87.3 us: retreat(): stack[slot_clip]]
    reduce_scatter x1 -> x0, waiting for transfers between devices: 95 us -> none  [body(): lax.psum_scatter(jnp.concatenate([stacked(grad_store[0], grad_store[1]),...]
    while x738 -> x0, local copies, waits for them, and re-layouts: 80.4 us -> none
  transfers between devices with their start and end apart: 117 -> 84, of which waited for: 53 -> 39; matrix products, arithmetic and copies ran while one was open for 16% -> 2% of each run, Pallas kernels for 0% -> 4%
where the time goes in v1:
time: 761 us; the launch traced here: 752 us
  waiting for transfers between devices  276 us (36%)
  starting transfers between devices  274 us (36%)
  Pallas kernels  134 us (18%)
  local copies, waits for them, and re-layouts  27 us (4%)
  blocking collectives  16.1 us (2%)
  other arithmetic  14.9 us (2%)
  between operations  9.76 us (1%)
    ppermute x72, starting transfers between devices, moved(): return lax.ppermute(block, ('section', 'tok'), route)  245 us
    ppermute x72, waiting for transfers between devices, moved(): return lax.ppermute(block, ('section', 'tok'), route)  217 us
    pallas_call x32, Pallas kernels, section_call(): pl.pallas_call(kernel, out_shape=store_shapes + (rows_bf,), in_specs=[SME...  118 us
    ppermute x12, waiting for transfers between devices, ring(): return lax.ppermute(block, 'tok', route)  58.6 us
    ppermute x12, starting transfers between devices, ring(): return lax.ppermute(block, 'tok', route)  29.2 us
    unnamed x39, local copies, waits for them, and re-layouts  18.1 us
    unnamed x1, blocking collectives  16.1 us
  transfers between devices with their start and end apart: 84, of which 39 were waited for; matrix products, arithmetic and copies ran while one was open for 2% of the time, Pallas kernels for 4%

profile of v1, /device:TPU:35, one launch (start us, length us, event | category | flops | bytes accessed | tf_op | source)
XLA Modules:
  0.0 752.0 jit_solution(14162913108770172805)
XLA Ops:
  6.8 16.1 %all-reduce.2 = s32[16]{0:T(128)S(1)} all-reduce(s32[16]{0:T(128)S(1)} %dynamic-update-slice), channel_id=2, replica_groups=mesh['section'=16,'tok'=16] {'section'}, use_global_device_ids=true, to_apply=%add.2 | all-reduce | flops 16 | bytes 128
  26.9 6.1 forward_plain.8
  38.2 5.5 forward_plain.9
  48.3 8.6 %forward_plain.10 = (bf16[224,128,512]{2,1,0:T(8,128)(2,1)}, f32[112,128,512]{2,1,0:T(8,128)}, bf16[128,512]{1,0:T(8,128)(2,1)S(1)}) custom-call(s32[16,4]{1,0:T(8,128)S(1)} %copy.149.refs_0_, bf16[128,512]{1,0:T(8,128)(2,1)S(1)} %collective-permute-done.5.refs_1_, ...), custom_call_target="tpu_custom_call", output_to_operand_aliasing={{0}: (9, {}), {1}: (10, {})} | custom-call | tf_op jit(solution)/shard_map/forward_plain/pallas_call | solution.py:523
  68.8 12.8 %collective-permute-start.11 = (bf16[128,512]{1,0:T(8,128)(2,1)S(1)}, bf16[128,512]{1,0:T(8,128)(2,1)S(1)}, u32[]{:S(2)}, u32[]{:S(2)}) collective-permute-start(bf16[128,512]{1,0:T(8,128)(2,1)S(1)} %get-tuple-element.155), channel_id=1, source_target_pairs={{0,32},{1,33},{2,34},{3,35},{4,36},{5,37},{6,38},{7,39},{8,40},{9,... | collective-permute-start | bytes 393224 | tf_op jit(solution)/shard_map/ppermute | solution.py:426
  81.6 6.1 collective-permute-start.12
  89.7 8.1 %forward_plain.14 = (bf16[224,128,512]{2,1,0:T(8,128)(2,1)}, f32[112,128,512]{2,1,0:T(8,128)}, bf16[128,512]{1,0:T(8,128)(2,1)S(1)}) custom-call(s32[16,4]{1,0:T(8,128)S(1)} %copy.149.refs_0_, bf16[128,512]{1,0:T(8,128)(2,1)S(1)} %collective-permute-done.11.refs_1_, ...), custom_call_target="tpu_custom_call", output_to_operand_aliasing={{0}: (9, {}), {1}: (10, {})} | custom-call | tf_op jit(solution)/shard_map/forward_plain/pallas_call | solution.py:523
  100.2 4.1 collective-permute-start.13
  115.7 15.4 %collective-permute-done.23 = bf16[2,128,640]{2,1,0:T(8,128)(2,1)S(1)} collective-permute-done((bf16[2,128,640]{2,1,0:T(8,128)(2,1)S(1)}, bf16[2,128,640]{2,1,0:T(8,128)(2,1)S(1)}, u32[]{:S(2)}, u32[]{:S(2)}) %collective-permute-start.23) | collective-permute-done | bytes 327712 | tf_op jit(solution)/shard_map/ppermute | solution.py:426
  147.2 8.8 %forward_skip.7 = (bf16[224,128,512]{2,1,0:T(8,128)(2,1)}, f32[112,128,512]{2,1,0:T(8,128)}, bf16[128,512]{1,0:T(8,128)(2,1)S(1)}) custom-call(s32[16,4]{1,0:T(8,128)S(1)} %copy.149.refs_0_, bf16[128,512]{1,0:T(8,128)(2,1)S(1)} %get-tuple-element.171.refs_1_, ...), custom_call_target="tpu_custom_call", output_to_operand_aliasing={{0}: (10, {}), {1}: (11, {})} | custom-call | tf_op jit(solution)/shard_map/forward_skip/pallas_call | solution.py:523
  156.1 12.8 %collective-permute-start.21 = (bf16[128,512]{1,0:T(8,128)(2,1)S(1)}, bf16[128,512]{1,0:T(8,128)(2,1)S(1)}, u32[]{:S(2)}, u32[]{:S(2)}) collective-permute-start(bf16[128,512]{1,0:T(8,128)(2,1)S(1)} %get-tuple-element.175), channel_id=1, source_target_pairs={{0,32},{1,33},{2,34},{3,35},{4,36},{5,37},{6,38},{7,39},{8,40},{9,... | collective-permute-start | bytes 393224 | tf_op jit(solution)/shard_map/ppermute | solution.py:426
  190.3 9.8 %forward_skip.11 = (bf16[224,128,512]{2,1,0:T(8,128)(2,1)}, f32[112,128,512]{2,1,0:T(8,128)}, bf16[128,512]{1,0:T(8,128)(2,1)S(1)}) custom-call(s32[16,4]{1,0:T(8,128)S(1)} %copy.149.refs_0_, bf16[128,512]{1,0:T(8,128)(2,1)S(1)} %get-tuple-element.185.refs_1_, ...), custom_call_target="tpu_custom_call", output_to_operand_aliasing={{0}: (10, {}), {1}: (11, {})} | custom-call | tf_op jit(solution)/shard_map/forward_skip/pallas_call | solution.py:523
  200.0 24.9 %collective-permute-start.33 = (bf16[128,512]{1,0:T(8,128)(2,1)S(1)}, bf16[128,512]{1,0:T(8,128)(2,1)S(1)}, u32[]{:S(2)}, u32[]{:S(2)}) collective-permute-start(bf16[128,512]{1,0:T(8,128)(2,1)S(1)} %get-tuple-element.188), channel_id=1, source_target_pairs={{0,32},{1,33},{2,34},{3,35},{4,36},{5,37},{6,38},{7,39},{8,40},{9,... | collective-permute-start | bytes 393224 | tf_op jit(solution)/shard_map/ppermute | solution.py:426
  236.8 4.2 collective-permute-done.36.refs_2_
  244.4 4.3 collective-permute-done.37.refs_1_
  248.8 5.0 collective-permute-done.38.refs_2_
  254.6 4.0 collective-permute-done.39.refs_2_
  258.6 8.2 %backward_plain.9 = (bf16[224,128,512]{2,1,0:T(8,128)(2,1)}, f32[112,128,512]{2,1,0:T(8,128)}, bf16[128,512]{1,0:T(8,128)(2,1)S(1)}) custom-call(s32[16,4]{1,0:T(8,128)S(1)} %copy.149.refs_0_, bf16[128,512]{1,0:T(8,128)(2,1)S(1)} %get-tuple-element.203.refs_1_, ...), custom_call_target="tpu_custom_call", output_to_operand_aliasing={{0}: (9, {}), {1}: (10, {})} | custom-call | tf_op jit(solution)/shard_map/backward_plain/pallas_call | solution.py:523
  269.1 5.9 collective-permute-done.42.refs_2_
  278.4 42.1 %collective-permute-done.43.refs_1_ = bf16[128,512]{1,0:T(8,128)(2,1)S(1)} collective-permute-done((bf16[128,512]{1,0:T(8,128)(2,1)S(1)}, bf16[128,512]{1,0:T(8,128)(2,1)S(1)}, u32[]{:S(2)}, u32[]{:S(2)}) %collective-permute-start.43) | collective-permute-done | bytes 131104 | tf_op jit(solution)/shard_map/ppermute | solution.py:426
  320.5 6.8 collective-permute-done.44.refs_2_
  327.3 9.5 %backward_plain.12 = (bf16[224,128,512]{2,1,0:T(8,128)(2,1)}, f32[112,128,512]{2,1,0:T(8,128)}, bf16[128,512]{1,0:T(8,128)(2,1)S(1)}) custom-call(s32[16,4]{1,0:T(8,128)S(1)} %copy.149.refs_0_, bf16[128,512]{1,0:T(8,128)(2,1)S(1)} %collective-permute-done.43.refs_1_, ...), custom_call_target="tpu_custom_call", output_to_operand_aliasing={{0}: (9, {}), {1}: (10, {})} | custom-call | tf_op jit(solution)/shard_map/backward_plain/pallas_call | solution.py:523
  349.7 48.7 %collective-permute-start.57 = (bf16[2,128,512]{2,1,0:T(8,128)(2,1)S(1)}, bf16[2,128,512]{2,1,0:T(8,128)(2,1)S(1)}, u32[]{:S(2)}, u32[]{:S(2)}) collective-permute-start(bf16[2,128,512]{2,1,0:T(8,128)(2,1)S(1)} %pad_maximum_fusion.1), channel_id=1, source_target_pairs={{0,224},{1,225},{2,226},{3,227},{4,228},{5,229},{6,230},{7,231},{8... | collective-permute-start | bytes 786440 | tf_op jit(solution)/shard_map/ppermute | solution.py:426
  402.1 6.9 collective-permute-start.58
  409.2 6.8 collective-permute-done.58
  428.2 9.5 %backward_skip.7 = (bf16[224,128,512]{2,1,0:T(8,128)(2,1)}, f32[112,128,512]{2,1,0:T(8,128)}, bf16[128,512]{1,0:T(8,128)(2,1)}) custom-call(s32[16,4]{1,0:T(8,128)S(1)} %copy.149.refs_0_, bf16[128,512]{1,0:T(8,128)(2,1)S(1)} %get-tuple-element.228.refs_1_, ...), custom_call_target="tpu_custom_call", output_to_operand_aliasing={{0}: (10, {}), {1}: (11, {})} | custom-call | tf_op jit(solution)/shard_map/backward_skip/pallas_call | solution.py:523
  440.5 33.8 %collective-permute-start.55 = (bf16[7,128,512]{2,1,0:T(8,128)(2,1)}, bf16[7,128,512]{2,1,0:T(8,128)(2,1)S(1)}, u32[]{:S(2)}, u32[]{:S(2)}) collective-permute-start(bf16[7,128,512]{2,1,0:T(8,128)(2,1)} %get-tuple-element.234), channel_id=1, source_target_pairs={{16,0},{17,1},{18,2},{19,3},{20,4},{21,5},{22,6},{23,7},{24,8},{25... | collective-permute-start | bytes 2752520 | tf_op jit(solution)/shard_map/ppermute | solution.py:426
  476.6 17.1 %collective-permute-start.61 = (bf16[2,128,512]{2,1,0:T(8,128)(2,1)S(1)}, bf16[2,128,512]{2,1,0:T(8,128)(2,1)S(1)}, u32[]{:S(2)}, u32[]{:S(2)}) collective-permute-start(bf16[2,128,512]{2,1,0:T(8,128)(2,1)S(1)} %broadcast_select_fusion.6), channel_id=1, source_target_pairs={{8,0},{9,1},{10,2},{11,3},{12,4},{13,5},{14,6},{15,7},{0,8},{1,9},... | collective-permute-start | bytes 786440 | tf_op jit(solution)/shard_map/ppermute | solution.py:426
  496.3 6.9 collective-permute-done.61
  506.9 9.7 %collective-permute-done.53.refs_1_ = bf16[128,512]{1,0:T(8,128)(2,1)S(1)} collective-permute-done((bf16[128,512]{1,0:T(8,128)(2,1)}, bf16[128,512]{1,0:T(8,128)(2,1)S(1)}, u32[]{:S(2)}, u32[]{:S(2)}) %collective-permute-start.53) | collective-permute-done | bytes 131104 | tf_op jit(solution)/shard_map/ppermute | solution.py:426
  516.5 4.5 collective-permute-done.54.refs_2_
  535.6 8.8 %backward_skip.10 = (bf16[224,128,512]{2,1,0:T(8,128)(2,1)}, f32[112,128,512]{2,1,0:T(8,128)}, bf16[128,512]{1,0:T(8,128)(2,1)S(1)}) custom-call(s32[16,4]{1,0:T(8,128)S(1)} %copy.149.refs_0_, bf16[128,512]{1,0:T(8,128)(2,1)S(1)} %collective-permute-done.64.refs_1_, ...), custom_call_target="tpu_custom_call", output_to_operand_aliasing={{0}: (10, {}), {1}: (11, {})} | custom-call | tf_op jit(solution)/shard_map/backward_skip/pallas_call | solution.py:523
  544.4 5.0 collective-permute-done.66.refs_2_
  552.8 52.9 %collective-permute-done.67.refs_1_ = bf16[128,512]{1,0:T(8,128)(2,1)S(1)} collective-permute-done((bf16[128,512]{1,0:T(8,128)(2,1)S(1)}, bf16[128,512]{1,0:T(8,128)(2,1)S(1)}, u32[]{:S(2)}, u32[]{:S(2)}) %collective-permute-start.67) | collective-permute-done | bytes 131104 | tf_op jit(solution)/shard_map/ppermute | solution.py:426
  605.7 4.0 collective-permute-done.68.refs_2_
  609.7 8.8 %backward_skip.12 = (bf16[224,128,512]{2,1,0:T(8,128)(2,1)}, f32[112,128,512]{2,1,0:T(8,128)}, bf16[128,512]{1,0:T(8,128)(2,1)S(1)}) custom-call(s32[16,4]{1,0:T(8,128)S(1)} %copy.149.refs_0_, bf16[128,512]{1,0:T(8,128)(2,1)S(1)} %collective-permute-done.67.refs_1_, ...), custom_call_target="tpu_custom_call", output_to_operand_aliasing={{0}: (10, {}), {1}: (11, {})} | custom-call | tf_op jit(solution)/shard_map/backward_skip/pallas_call | solution.py:523
  618.6 3.8 collective-permute-done.69.refs_2_
  622.4 10.3 %backward_skip.13 = (bf16[224,128,512]{2,1,0:T(8,128)(2,1)}, f32[112,128,512]{2,1,0:T(8,128)}, bf16[128,512]{1,0:T(8,128)(2,1)}) custom-call(s32[16,4]{1,0:T(8,128)S(1)} %copy.149.refs_0_, bf16[128,512]{1,0:T(8,128)(2,1)S(1)} %get-tuple-element.253.refs_1_, ...), custom_call_target="tpu_custom_call", output_to_operand_aliasing={{0}: (10, {}), {1}: (11, {})} | custom-call | tf_op jit(solution)/shard_map/backward_skip/pallas_call | solution.py:523
  635.8 8.9 %collective-permute-start.70 = (bf16[9,128,512]{2,1,0:T(8,128)(2,1)}, bf16[9,128,512]{2,1,0:T(8,128)(2,1)S(1)}, u32[]{:S(2)}, u32[]{:S(2)}) collective-permute-start(bf16[9,128,512]{2,1,0:T(8,128)(2,1)} %get-tuple-element.260), channel_id=1, source_target_pairs={{16,0},{17,1},{18,2},{19,3},{20,4},{21,5},{22,6},{23,7},{24,8},{25... | collective-permute-start | bytes 3538952 | tf_op jit(solution)/shard_map/ppermute | solution.py:426
  649.8 6.9 weight_grads.1
  657.0 4.5 collective-permute-start.73
  661.9 10.4 %collective-permute-start.76 = (bf16[4,32,2048]{2,1,0:T(8,128)(2,1)}, bf16[4,32,2048]{2,1,0:T(8,128)(2,1)}, u32[]{:S(2)}, u32[]{:S(2)}) collective-permute-start(bf16[4,32,2048]{2,1,0:T(8,128)(2,1)} %get-tuple-element.268), channel_id=1, source_target_pairs={{0,8},{1,9},{2,10},{3,11},{4,12},{5,13},{6,14},{7,15},{8,0},{9,1},... | collective-permute-start | bytes 1572872 | tf_op jit(solution)/shard_map/ppermute | solution.py:764
  672.3 4.3 collective-permute-done.75
  679.7 25.9 %collective-permute-done.76 = bf16[4,32,2048]{2,1,0:T(8,128)(2,1)} collective-permute-done((bf16[4,32,2048]{2,1,0:T(8,128)(2,1)}, bf16[4,32,2048]{2,1,0:T(8,128)(2,1)}, u32[]{:S(2)}, u32[]{:S(2)}) %collective-permute-start.76) | collective-permute-done | bytes 524320 | tf_op jit(solution)/shard_map/ppermute | solution.py:764
  705.6 6.8 collective-permute-done.77
  716.5 6.1 collective-permute-start.82
  729.6 14.8 %collective-permute-done.79 = bf16[32,4096]{1,0:T(8,128)(2,1)S(1)} collective-permute-done((bf16[32,4096]{1,0:T(8,128)(2,1)S(1)}, bf16[32,4096]{1,0:T(8,128)(2,1)S(1)}, u32[]{:S(2)}, u32[]{:S(2)}) %collective-permute-start.79) | collective-permute-done | bytes 262176 | tf_op jit(solution)/shard_map/ppermute | solution.py:764
  744.5 5.0 collective-permute-done.80
  (263 shorter events, 182.2 us)
Async XLA Ops:
  2.5 22.7 %collective-permute-start.1 = (bf16[512,2048]{1,0:T(8,128)(2,1)S(1)}, bf16[512,2048]{1,0:T(8,128)(2,1)}, u32[]{:S(2)}, u32[]{:S(2)}) collective-permute-start(bf16[512,2048]{1,0:T(8,128)(2,1)S(1)} %pad_maximum_fusion.refs_3_.refs_4_), channel_id=1, source_target_pairs={{0,16},{1,17},{2,18},{3,19},{4,20},{5,21},{6,22},{7,23},{8,24},{9,... | collective-permute-start | bytes 6291464 | tf_op jit(solution)/shard_map/ppermute | solution.py:426
  3.3 22.0 %collective-permute-start.2 = (bf16[512,2048]{1,0:T(8,128)(2,1)}, bf16[512,2048]{1,0:T(8,128)(2,1)}, u32[]{:S(2)}, u32[]{:S(2)}) collective-permute-start(bf16[512,2048]{1,0:T(8,128)(2,1)} %bitcast.80), channel_id=1, source_target_pairs={{0,16},{1,17},{2,18},{3,19},{4,20},{5,21},{6,22},{7,23},{8,24},{9,... | collective-permute-start | bytes 6291464 | tf_op jit(solution)/shard_map/ppermute | solution.py:426
  3.4 21.9 %collective-permute-start.3 = (bf16[512,2048]{1,0:T(8,128)(2,1)}, bf16[512,2048]{1,0:T(8,128)(2,1)}, u32[]{:S(2)}, u32[]{:S(2)}) collective-permute-start(bf16[512,2048]{1,0:T(8,128)(2,1)} %bitcast.113), channel_id=1, source_target_pairs={{0,16},{1,17},{2,18},{3,19},{4,20},{5,21},{6,22},{7,23},{8,24},{9,... | collective-permute-start | bytes 6291464 | tf_op jit(solution)/shard_map/ppermute | solution.py:426
  3.8 21.4 %collective-permute-start = (bf16[128,512]{1,0:T(8,128)(2,1)S(1)}, bf16[128,512]{1,0:T(8,128)(2,1)S(1)}, u32[]{:S(2)}, u32[]{:S(2)}) collective-permute-start(bf16[128,512]{1,0:T(8,128)(2,1)S(1)} %dynamic-slice_bitcast_fusion.6.refs_1_), channel_id=1, source_target_pairs={{1,0},{2,1},{3,2},{4,3},{5,4},{6,5},{7,6},{8,7},{9,8},{10,9},{11,1... | collective-permute-start | bytes 393224 | tf_op jit(solution)/shard_map/ppermute | solution.py:426
  33.0 5.3 collective-permute-start.4
  68.8 18.9 %collective-permute-start.11 = (bf16[128,512]{1,0:T(8,128)(2,1)S(1)}, bf16[128,512]{1,0:T(8,128)(2,1)S(1)}, u32[]{:S(2)}, u32[]{:S(2)}) collective-permute-start(bf16[128,512]{1,0:T(8,128)(2,1)S(1)} %get-tuple-element.155), channel_id=1, source_target_pairs={{0,32},{1,33},{2,34},{3,35},{4,36},{5,37},{6,38},{7,39},{8,40},{9,... | collective-permute-start | bytes 393224 | tf_op jit(solution)/shard_map/ppermute | solution.py:426
  81.6 8.0 %collective-permute-start.12 = (bf16[128,512]{1,0:T(8,128)(2,1)S(1)}, bf16[128,512]{1,0:T(8,128)(2,1)S(1)}, u32[]{:S(2)}, u32[]{:S(2)}) collective-permute-start(bf16[128,512]{1,0:T(8,128)(2,1)S(1)} %get-tuple-element.155), channel_id=1, source_target_pairs={{1,32},{2,33},{3,34},{4,35},{5,36},{6,37},{7,38},{8,39},{9,40},{10... | collective-permute-start | bytes 393224 | tf_op jit(solution)/shard_map/ppermute | solution.py:426
  99.4 5.6 collective-permute-start.18
  100.2 6.8 collective-permute-start.13
  105.0 8.5 %collective-permute-start.19 = (bf16[128,512]{1,0:T(8,128)(2,1)S(1)}, bf16[128,512]{1,0:T(8,128)(2,1)S(1)}, u32[]{:S(2)}, u32[]{:S(2)}) collective-permute-start(bf16[128,512]{1,0:T(8,128)(2,1)S(1)} %collective-permute-done.18), channel_id=1, source_target_pairs={{129,128},{130,129},{131,130},{132,131},{133,132},{134,133},{135,1... | collective-permute-start | bytes 393224 | tf_op jit(solution)/shard_map/ppermute | solution.py:426
  113.8 17.3 %collective-permute-start.23 = (bf16[2,128,640]{2,1,0:T(8,128)(2,1)S(1)}, bf16[2,128,640]{2,1,0:T(8,128)(2,1)S(1)}, u32[]{:S(2)}, u32[]{:S(2)}) collective-permute-start(bf16[2,128,640]{2,1,0:T(8,128)(2,1)S(1)} %maximum_maximum_fusion), channel_id=1, source_target_pairs={{0,224},{1,225},{2,226},{3,227},{4,228},{5,229},{6,230},{7,231},{8... | collective-permute-start | bytes 983048 | tf_op jit(solution)/shard_map/ppermute | solution.py:426
  131.1 6.0 collective-permute-start.24
  143.1 27.6 %collective-permute-start.28 = (bf16[2,128,640]{2,1,0:T(8,128)(2,1)S(1)}, bf16[2,128,640]{2,1,0:T(8,128)(2,1)}, u32[]{:S(2)}, u32[]{:S(2)}) collective-permute-start(bf16[2,128,640]{2,1,0:T(8,128)(2,1)S(1)} %broadcast_select_fusion.3), channel_id=1, source_target_pairs={{161,160},{162,161},{163,162},{164,163},{165,164},{166,165},{167,1... | collective-permute-start | bytes 983048 | tf_op jit(solution)/shard_map/ppermute | solution.py:426
  156.1 15.8 %collective-permute-start.21 = (bf16[128,512]{1,0:T(8,128)(2,1)S(1)}, bf16[128,512]{1,0:T(8,128)(2,1)S(1)}, u32[]{:S(2)}, u32[]{:S(2)}) collective-permute-start(bf16[128,512]{1,0:T(8,128)(2,1)S(1)} %get-tuple-element.175), channel_id=1, source_target_pairs={{0,32},{1,33},{2,34},{3,35},{4,36},{5,37},{6,38},{7,39},{8,40},{9,... | collective-permute-start | bytes 393224 | tf_op jit(solution)/shard_map/ppermute | solution.py:426
  173.4 5.7 collective-permute-start.29
  200.0 28.5 %collective-permute-start.33 = (bf16[128,512]{1,0:T(8,128)(2,1)S(1)}, bf16[128,512]{1,0:T(8,128)(2,1)S(1)}, u32[]{:S(2)}, u32[]{:S(2)}) collective-permute-start(bf16[128,512]{1,0:T(8,128)(2,1)S(1)} %get-tuple-element.188), channel_id=1, source_target_pairs={{0,32},{1,33},{2,34},{3,35},{4,36},{5,37},{6,38},{7,39},{8,40},{9,... | collective-permute-start | bytes 393224 | tf_op jit(solution)/shard_map/ppermute | solution.py:426
  241.8 6.9 collective-permute-start.37
  243.1 10.6 %collective-permute-start.38 = (bf16[128,512]{1,0:T(8,128)(2,1)S(1)}, bf16[128,512]{1,0:T(8,128)(2,1)S(1)}, u32[]{:S(2)}, u32[]{:S(2)}) collective-permute-start(bf16[128,512]{1,0:T(8,128)(2,1)S(1)} %get-tuple-element.200), channel_id=1, source_target_pairs={{47,0},{32,1},{33,2},{34,3},{35,4},{36,5},{37,6},{38,7},{39,8},{40... | collective-permute-start | bytes 393224 | tf_op jit(solution)/shard_map/ppermute | solution.py:426
  269.0 6.0 collective-permute-start.42
  275.8 44.7 %collective-permute-start.43 = (bf16[128,512]{1,0:T(8,128)(2,1)S(1)}, bf16[128,512]{1,0:T(8,128)(2,1)S(1)}, u32[]{:S(2)}, u32[]{:S(2)}) collective-permute-start(bf16[128,512]{1,0:T(8,128)(2,1)S(1)} %get-tuple-element.212), channel_id=1, source_target_pairs={{32,0},{33,1},{34,2},{35,3},{36,4},{37,5},{38,6},{39,7},{40,8},{41... | collective-permute-start | bytes 393224 | tf_op jit(solution)/shard_map/ppermute | solution.py:426
  277.1 50.2 %collective-permute-start.44 = (bf16[128,512]{1,0:T(8,128)(2,1)S(1)}, bf16[128,512]{1,0:T(8,128)(2,1)S(1)}, u32[]{:S(2)}, u32[]{:S(2)}) collective-permute-start(bf16[128,512]{1,0:T(8,128)(2,1)S(1)} %get-tuple-element.212), channel_id=1, source_target_pairs={{47,0},{32,1},{33,2},{34,3},{35,4},{36,5},{37,6},{38,7},{39,8},{40... | collective-permute-start | bytes 393224 | tf_op jit(solution)/shard_map/ppermute | solution.py:426
  338.9 10.5 %collective-permute-start.51 = (bf16[128,512]{1,0:T(8,128)(2,1)S(1)}, bf16[128,512]{1,0:T(8,128)(2,1)S(1)}, u32[]{:S(2)}, u32[]{:S(2)}) collective-permute-start(bf16[128,512]{1,0:T(8,128)(2,1)S(1)} %collective-permute-done.50), channel_id=1, source_target_pairs={{111,96},{96,97},{97,98},{98,99},{99,100},{100,101},{101,102},{102... | collective-permute-start | bytes 393224 | tf_op jit(solution)/shard_map/ppermute | solution.py:426
  349.7 52.4 %collective-permute-start.57 = (bf16[2,128,512]{2,1,0:T(8,128)(2,1)S(1)}, bf16[2,128,512]{2,1,0:T(8,128)(2,1)S(1)}, u32[]{:S(2)}, u32[]{:S(2)}) collective-permute-start(bf16[2,128,512]{2,1,0:T(8,128)(2,1)S(1)} %pad_maximum_fusion.1), channel_id=1, source_target_pairs={{0,224},{1,225},{2,226},{3,227},{4,228},{5,229},{6,230},{7,231},{8... | collective-permute-start | bytes 786440 | tf_op jit(solution)/shard_map/ppermute | solution.py:426
  402.1 13.8 %collective-permute-start.58 = (bf16[2,128,512]{2,1,0:T(8,128)(2,1)S(1)}, bf16[2,128,512]{2,1,0:T(8,128)(2,1)S(1)}, u32[]{:S(2)}, u32[]{:S(2)}) collective-permute-start(bf16[2,128,512]{2,1,0:T(8,128)(2,1)S(1)} %collective-permute-done.57), channel_id=1, source_target_pairs={{15,0},{0,1},{1,2},{2,3},{3,4},{4,5},{5,6},{6,7},{7,8},{8,9},{9,10... | collective-permute-start | bytes 786440 | tf_op jit(solution)/shard_map/ppermute | solution.py:426
  416.1 9.8 %collective-permute-start.59 = (bf16[2,128,512]{2,1,0:T(8,128)(2,1)S(1)}, bf16[2,128,512]{2,1,0:T(8,128)(2,1)S(1)}, u32[]{:S(2)}, u32[]{:S(2)}) collective-permute-start(bf16[2,128,512]{2,1,0:T(8,128)(2,1)S(1)} %broadcast_select_fusion.4), channel_id=1, source_target_pairs={{14,0},{15,1},{0,2},{1,3},{2,4},{3,5},{4,6},{5,7},{6,8},{7,9},{8,1... | collective-permute-start | bytes 786440 | tf_op jit(solution)/shard_map/ppermute | solution.py:426
  421.4 6.8 collective-permute-start.52
  426.0 49.6 %collective-permute-start.60 = (bf16[2,128,512]{2,1,0:T(8,128)(2,1)S(1)}, bf16[2,128,512]{2,1,0:T(8,128)(2,1)}, u32[]{:S(2)}, u32[]{:S(2)}) collective-permute-start(bf16[2,128,512]{2,1,0:T(8,128)(2,1)S(1)} %broadcast_select_fusion.5), channel_id=1, source_target_pairs={{12,0},{13,1},{14,2},{15,3},{0,4},{1,5},{2,6},{3,7},{4,8},{5,9},{6... | collective-permute-start | bytes 786440 | tf_op jit(solution)/shard_map/ppermute | solution.py:426
  440.5 80.6 %collective-permute-start.55 = (bf16[7,128,512]{2,1,0:T(8,128)(2,1)}, bf16[7,128,512]{2,1,0:T(8,128)(2,1)S(1)}, u32[]{:S(2)}, u32[]{:S(2)}) collective-permute-start(bf16[7,128,512]{2,1,0:T(8,128)(2,1)} %get-tuple-element.234), channel_id=1, source_target_pairs={{16,0},{17,1},{18,2},{19,3},{20,4},{21,5},{22,6},{23,7},{24,8},{25... | collective-permute-start | bytes 2752520 | tf_op jit(solution)/shard_map/ppermute | solution.py:426
  474.2 46.8 %collective-permute-start.56 = (bf16[7,128,512]{2,1,0:T(8,128)(2,1)}, bf16[7,128,512]{2,1,0:T(8,128)(2,1)}, u32[]{:S(2)}, u32[]{:S(2)}) collective-permute-start(bf16[7,128,512]{2,1,0:T(8,128)(2,1)} %get-tuple-element.235), channel_id=1, source_target_pairs={{0,16},{1,17},{2,18},{3,19},{4,20},{5,21},{6,22},{7,23},{8,24},{9,... | collective-permute-start | bytes 2752520 | tf_op jit(solution)/shard_map/ppermute | solution.py:426
  476.6 26.6 %collective-permute-start.61 = (bf16[2,128,512]{2,1,0:T(8,128)(2,1)S(1)}, bf16[2,128,512]{2,1,0:T(8,128)(2,1)S(1)}, u32[]{:S(2)}, u32[]{:S(2)}) collective-permute-start(bf16[2,128,512]{2,1,0:T(8,128)(2,1)S(1)} %broadcast_select_fusion.6), channel_id=1, source_target_pairs={{8,0},{9,1},{10,2},{11,3},{12,4},{13,5},{14,6},{15,7},{0,8},{1,9},... | collective-permute-start | bytes 786440 | tf_op jit(solution)/shard_map/ppermute | solution.py:426
  493.7 22.8 %collective-permute-start.53 = (bf16[128,512]{1,0:T(8,128)(2,1)}, bf16[128,512]{1,0:T(8,128)(2,1)S(1)}, u32[]{:S(2)}, u32[]{:S(2)}) collective-permute-start(bf16[128,512]{1,0:T(8,128)(2,1)} %get-tuple-element.232), channel_id=1, source_target_pairs={{32,0},{33,1},{34,2},{35,3},{36,4},{37,5},{38,6},{39,7},{40,8},{41... | collective-permute-start | bytes 393224 | tf_op jit(solution)/shard_map/ppermute | solution.py:426
  495.0 26.0 %collective-permute-start.54 = (bf16[128,512]{1,0:T(8,128)(2,1)}, bf16[128,512]{1,0:T(8,128)(2,1)S(1)}, u32[]{:S(2)}, u32[]{:S(2)}) collective-permute-start(bf16[128,512]{1,0:T(8,128)(2,1)} %get-tuple-element.232), channel_id=1, source_target_pairs={{47,0},{32,1},{33,2},{34,3},{35,4},{36,5},{37,6},{38,7},{39,8},{40... | collective-permute-start | bytes 393224 | tf_op jit(solution)/shard_map/ppermute | solution.py:426
  504.0 18.7 %collective-permute-start.62 = (bf16[2,128,512]{2,1,0:T(8,128)(2,1)}, bf16[2,128,512]{2,1,0:T(8,128)(2,1)}, u32[]{:S(2)}, u32[]{:S(2)}) collective-permute-start(bf16[2,128,512]{2,1,0:T(8,128)(2,1)} %broadcast_select_fusion.7), channel_id=1, source_target_pairs={{15,0},{0,1},{1,2},{2,3},{3,4},{4,5},{5,6},{6,7},{7,8},{8,9},{9,10... | collective-permute-start | bytes 786440 | tf_op jit(solution)/shard_map/ppermute | solution.py:426
  550.2 55.5 %collective-permute-start.67 = (bf16[128,512]{1,0:T(8,128)(2,1)S(1)}, bf16[128,512]{1,0:T(8,128)(2,1)S(1)}, u32[]{:S(2)}, u32[]{:S(2)}) collective-permute-start(bf16[128,512]{1,0:T(8,128)(2,1)S(1)} %get-tuple-element.250), channel_id=1, source_target_pairs={{32,0},{33,1},{34,2},{35,3},{36,4},{37,5},{38,6},{39,7},{40,8},{41... | collective-permute-start | bytes 393224 | tf_op jit(solution)/shard_map/ppermute | solution.py:426
  551.5 58.2 %collective-permute-start.68 = (bf16[128,512]{1,0:T(8,128)(2,1)S(1)}, bf16[128,512]{1,0:T(8,128)(2,1)S(1)}, u32[]{:S(2)}, u32[]{:S(2)}) collective-permute-start(bf16[128,512]{1,0:T(8,128)(2,1)S(1)} %get-tuple-element.250), channel_id=1, source_target_pairs={{47,0},{32,1},{33,2},{34,3},{35,4},{36,5},{37,6},{38,7},{39,8},{40... | collective-permute-start | bytes 393224 | tf_op jit(solution)/shard_map/ppermute | solution.py:426
  635.8 11.5 %collective-permute-start.70 = (bf16[9,128,512]{2,1,0:T(8,128)(2,1)}, bf16[9,128,512]{2,1,0:T(8,128)(2,1)S(1)}, u32[]{:S(2)}, u32[]{:S(2)}) collective-permute-start(bf16[9,128,512]{2,1,0:T(8,128)(2,1)} %get-tuple-element.260), channel_id=1, source_target_pairs={{16,0},{17,1},{18,2},{19,3},{20,4},{21,5},{22,6},{23,7},{24,8},{25... | collective-permute-start | bytes 3538952 | tf_op jit(solution)/shard_map/ppermute | solution.py:426
  656.8 19.9 %collective-permute-start.75 = (bf16[4,32,2048]{2,1,0:T(8,128)(2,1)S(1)}, bf16[4,32,2048]{2,1,0:T(8,128)(2,1)}, u32[]{:S(2)}, u32[]{:S(2)}) collective-permute-start(bf16[4,32,2048]{2,1,0:T(8,128)(2,1)S(1)} %get-tuple-element.267), channel_id=1, source_target_pairs={{0,4},{1,5},{2,6},{3,7},{4,8},{5,9},{6,10},{7,11},{8,12},{9,13},{1... | collective-permute-start | bytes 1572872 | tf_op jit(solution)/shard_map/ppermute | solution.py:764
  656.9 57.3 %collective-permute-start.72 = (bf16[4,32,4096]{2,1,0:T(8,128)(2,1)}, bf16[4,32,4096]{2,1,0:T(8,128)(2,1)S(1)}, u32[]{:S(2)}, u32[]{:S(2)}) collective-permute-start(bf16[4,32,4096]{2,1,0:T(8,128)(2,1)} %get-tuple-element.263), channel_id=1, source_target_pairs={{0,1},{1,2},{2,3},{3,0},{4,5},{5,6},{6,7},{7,4},{8,9},{9,10},{10,1... | collective-permute-start | bytes 3145736 | tf_op jit(solution)/shard_map/ppermute | solution.py:764
  657.0 57.2 %collective-permute-start.73 = (bf16[4,32,4096]{2,1,0:T(8,128)(2,1)}, bf16[4,32,4096]{2,1,0:T(8,128)(2,1)}, u32[]{:S(2)}, u32[]{:S(2)}) collective-permute-start(bf16[4,32,4096]{2,1,0:T(8,128)(2,1)} %get-tuple-element.264), channel_id=1, source_target_pairs={{0,2},{1,3},{2,0},{3,1},{4,6},{5,7},{6,4},{7,5},{8,10},{9,11},{10,... | collective-permute-start | bytes 3145736 | tf_op jit(solution)/shard_map/ppermute | solution.py:764
  661.5 52.7 %collective-permute-start.74 = (bf16[4,32,4096]{2,1,0:T(8,128)(2,1)}, bf16[4,32,4096]{2,1,0:T(8,128)(2,1)}, u32[]{:S(2)}, u32[]{:S(2)}) collective-permute-start(bf16[4,32,4096]{2,1,0:T(8,128)(2,1)} %get-tuple-element.265), channel_id=1, source_target_pairs={{0,3},{1,0},{2,1},{3,2},{4,7},{5,4},{6,5},{7,6},{8,11},{9,8},{10,9... | collective-permute-start | bytes 3145736 | tf_op jit(solution)/shard_map/ppermute | solution.py:764
  661.9 43.7 %collective-permute-start.76 = (bf16[4,32,2048]{2,1,0:T(8,128)(2,1)}, bf16[4,32,2048]{2,1,0:T(8,128)(2,1)}, u32[]{:S(2)}, u32[]{:S(2)}) collective-permute-start(bf16[4,32,2048]{2,1,0:T(8,128)(2,1)} %get-tuple-element.268), channel_id=1, source_target_pairs={{0,8},{1,9},{2,10},{3,11},{4,12},{5,13},{6,14},{7,15},{8,0},{9,1},... | collective-permute-start | bytes 1572872 | tf_op jit(solution)/shard_map/ppermute | solution.py:764
  676.6 35.8 %collective-permute-start.77 = (bf16[4,32,2048]{2,1,0:T(8,128)(2,1)S(1)}, bf16[4,32,2048]{2,1,0:T(8,128)(2,1)}, u32[]{:S(2)}, u32[]{:S(2)}) collective-permute-start(bf16[4,32,2048]{2,1,0:T(8,128)(2,1)S(1)} %get-tuple-element.269), channel_id=1, source_target_pairs={{0,12},{1,13},{2,14},{3,15},{4,0},{5,1},{6,2},{7,3},{8,4},{9,5},{1... | collective-permute-start | bytes 1572872 | tf_op jit(solution)/shard_map/ppermute | solution.py:764
  716.4 9.3 %collective-permute-start.81 = (bf16[32,2048]{1,0:T(8,128)(2,1)S(1)}, bf16[32,2048]{1,0:T(8,128)(2,1)S(1)}, u32[]{:S(2)}, u32[]{:S(2)}) collective-permute-start(bf16[32,2048]{1,0:T(8,128)(2,1)S(1)} %get-tuple-element.277), channel_id=1, source_target_pairs={{0,1},{1,2},{2,3},{3,0},{4,5},{5,6},{6,7},{7,4},{8,9},{9,10},{10,1... | collective-permute-start | bytes 393224 | tf_op jit(solution)/shard_map/ppermute | solution.py:764
  716.5 10.6 %collective-permute-start.82 = (bf16[32,2048]{1,0:T(8,128)(2,1)S(1)}, bf16[32,2048]{1,0:T(8,128)(2,1)S(1)}, u32[]{:S(2)}, u32[]{:S(2)}) collective-permute-start(bf16[32,2048]{1,0:T(8,128)(2,1)S(1)} %get-tuple-element.279), channel_id=1, source_target_pairs={{0,2},{1,3},{2,0},{3,1},{4,6},{5,7},{6,4},{7,5},{8,10},{9,11},{10,... | collective-permute-start | bytes 393224 | tf_op jit(solution)/shard_map/ppermute | solution.py:764
  722.6 6.3 collective-permute-start.83
  722.7 7.0 collective-permute-start.78
  722.7 21.7 %collective-permute-start.79 = (bf16[32,4096]{1,0:T(8,128)(2,1)S(1)}, bf16[32,4096]{1,0:T(8,128)(2,1)S(1)}, u32[]{:S(2)}, u32[]{:S(2)}) collective-permute-start(bf16[32,4096]{1,0:T(8,128)(2,1)S(1)} %get-tuple-element.276), channel_id=1, source_target_pairs={{0,8},{1,9},{2,10},{3,11},{4,12},{5,13},{6,14},{7,15},{8,0},{9,1},... | collective-permute-start | bytes 786440 | tf_op jit(solution)/shard_map/ppermute | solution.py:764
  725.8 23.7 %collective-permute-start.80 = (bf16[32,4096]{1,0:T(8,128)(2,1)S(1)}, bf16[32,4096]{1,0:T(8,128)(2,1)S(1)}, u32[]{:S(2)}, u32[]{:S(2)}) collective-permute-start(bf16[32,4096]{1,0:T(8,128)(2,1)S(1)} %get-tuple-element.275), channel_id=1, source_target_pairs={{0,12},{1,13},{2,14},{3,15},{4,0},{5,1},{6,2},{7,3},{8,4},{9,5},{1... | collective-permute-start | bytes 786440 | tf_op jit(solution)/shard_map/ppermute | solution.py:764
  (54 other events, 288.1 us)

commit v2 on v1

--- a/solution.py
+++ b/solution.py
@@ -128,7 +128,7 @@
 
 def forward_section(mode, section, *refs):
     refs = list(refs)
-    info_ref, cur_ref, nxt_ref = refs[:3]
+    info_ref, first_ref, second_ref = refs[:3]
     refs = refs[3:]
     skip_ref = refs.pop(0) if mode == "skip" else None
     mine, other = weight_views(refs[:3]), weight_views(refs[3:6])
@@ -146,7 +146,7 @@
         copy.start()
         out_copies.append(copy)
 
-    x = joined(cur_ref[...], nxt_ref[...], info_ref[section, 0])
+    x = joined(first_ref[...], second_ref[...], info_ref[section, 0])
     if mode == "skip":
         x = (x + skip_ref[...].astype(F32)).astype(BF16).astype(F32)
     if mode == "double":
@@ -214,7 +214,7 @@
         z_ref, aim_ref, head_ref = refs[:3]
         refs = refs[3:]
     else:
-        cur_ref, prv_ref = refs[:2]
+        first_ref, second_ref = refs[:2]
         refs = refs[2:]
     skip_ref = refs.pop(0) if mode == "skip" else None
     mine, other = weight_views(refs[:3]), weight_views(refs[3:6])
@@ -251,7 +251,7 @@
         grad_pred = (decay * (predicted - target) * loss_scale).astype(BF16)
         dz = norm_back(normed, scale, dot(grad_pred, head_ref[...], NT))
     else:
-        dz = joined(prv_ref[...], cur_ref[...], WIN - info_ref[section, 3])
+        dz = joined(first_ref[...], second_ref[...], info_ref[section, 3])
         if mode == "skip":
             dz = dz + skip_ref[...].astype(F32)
         if mode == "double":
@@ -330,11 +330,12 @@
 
 
 def pick_kernel(ranges, *refs):
-    store_ref = refs[1]
-    outs, sems = refs[2:-1], refs[-1]
+    core_ref, store_ref = refs[:2]
+    outs, sems = refs[3:-1], refs[-1]
     copies = []
-    for index, (at, count) in enumerate(ranges):
-        source = store_ref.at[pl.ds(at, count)]
+    for index, (at, count, given) in enumerate(ranges):
+        base = at + (1 - core_ref[0]) * LOW_SLOTS if given else at
+        source = store_ref.at[pl.ds(base, count)]
         copies.append(pltpu.make_async_copy(source, outs[index], sems.at[index]))
         copies[-1].start()
     for copy in copies:
@@ -343,9 +344,9 @@
 
 def weight_kernel(inner, *refs):
     info_ref, store_ref = refs[:2]
-    received = refs[2:6]
-    near_refs, far_refs = refs[6 : 6 + inner], refs[6 + inner : 6 + 2 * inner]
-    left, right, room, sems = refs[6 + 2 * inner :]
+    received = refs[2:4]
+    groups = [refs[4 + group * inner : 4 + (group + 1) * inner] for group in range(3)]
+    left, right, room, sems = refs[4 + 3 * inner :]
     copies = []
     for into, at, count, got in ((left, LEFT_AT, LEFT_SLOTS, 0), (right, RIGHT_AT, RIGHT_SLOTS, 1)):
         for index in range(count):
@@ -353,25 +354,18 @@
             for part in range(2):
                 goal = into.at[pl.ds(part * WIN, WIN), columns]
                 sem = sems.at[len(copies)]
-                for side in range(2):
-
-                    @pl.when(info_ref[0] == side)
-                    def _():
-                        if part == 0:
-                            source = store_ref.at[side * LOW_SLOTS + at + index]
-                        else:
-                            source = received[2 * got + side].at[index]
-                        pltpu.make_async_copy(source, goal, sem).start()
-
-                copies.append(pltpu.make_async_copy(store_ref.at[at + index], goal, sem))
+                if part == 0:
+                    source = store_ref.at[info_ref[0] * LOW_SLOTS + at + index]
+                else:
+                    source = received[got].at[index]
+                copies.append(pltpu.make_async_copy(source, goal, sem))
+                copies[-1].start()
     for copy in copies:
         copy.wait()
     width, step = room.shape
     hidden = right.shape[1] - 5 * width
     total = 4 * width + 2 * hidden
-    outer = near_refs[0].shape[0]
-    strip = near_refs[0].shape[1]
-    split = near_refs[0].shape[2]
+    outer, strip, group_width = groups[0][0].shape
     for at in range(0, total, step):
         if at < 3 * width:
             first, second = left[:, :width], right[:, at : at + step]
@@ -383,22 +377,13 @@
             start = 3 * width + at - 4 * width - hidden
             first, second = right[:, 4 * width + hidden :], left[:, start : start + step]
         room[...] = dot(first, second, TN).astype(BF16)
+        group = at // group_width
+        columns = slice(at % group_width, at % group_width + step)
         for distance in range(inner):
-            if at < split:
-                column = lax.rem(info_ref[1] + distance, inner)
-            else:
-                column = lax.rem(info_ref[2] + distance, outer)
+            place = lax.rem(info_ref[1 if group < 2 else 2] + distance, inner)
             for line in range(outer):
-                if at < split:
-                    owner = line * inner + column
-                    near_refs[distance][line, :, at : at + step] = room[
-                        pl.ds(owner * strip, strip), :
-                    ]
-                else:
-                    owner = column * inner + line
-                    far_refs[distance][line, :, at - split : at - split + step] = room[
-                        pl.ds(owner * strip, strip), :
-                    ]
+                owner = line * inner + place if group < 2 else place * inner + line
+                groups[group][distance][line, :, columns] = room[pl.ds(owner * strip, strip), :]
 
 
 VMEM = pl.BlockSpec(memory_space=pltpu.VMEM)
@@ -426,15 +411,16 @@
         return lax.ppermute(block, ("section", "tok"), route)
 
     def hop(block, low_pair, step, tok_shift):
+        middle = half_pairs - 1
         route = []
         for pair in range(pair_count - 1):
-            if pair % 2 == low_pair % 2:
+            if (pair > middle) - (pair < middle) == (low_pair > middle) - (low_pair < middle):
                 for core in range(2):
                     for tok in range(tok_count):
                         low, high = 2 * pair + core, 2 * pair + 2 + core
                         origin, goal = (low, high) if step > 0 else (high, low)
                         route.append((place(origin, tok + tok_shift), place(goal, tok)))
-        return moved(block, route)
+        return moved(block, sorted(route))
 
     def along(block, tok_shift, sections):
         route = []
@@ -443,41 +429,35 @@
                 route.append((place(section, tok + tok_shift), place(section, tok)))
         return moved(block, route)
 
-    def mirror(block, pairs):
-        route = []
-        for one in pairs:
-            for goal in (pair_count - 1 - one,):
-                for core in range(2):
-                    for tok in range(tok_count):
-                        origin = 2 * (pair_count - 1 - goal) + core
-                        route.append((place(origin, tok), place(2 * goal + core, tok)))
-        return moved(block, sorted(route))
-
-    outer_pairs = [pair for pair in range(pair_count) if pair not in (half_pairs - 1, half_pairs)]
-
-    def swap(block, origins):
+    def swap(block):
         route = [
             (place(section, tok), place(section ^ 1, tok))
             for section in range(section_count)
-            if section % 2 in origins
             for tok in range(tok_count)
         ]
         return moved(block, route)
 
+    def across(block, pairs, offsets, sign):
+        blocks = []
+        for offset in offsets:
+            route = []
+            for pair in pairs:
+                shift = offset * sign if pair < half_pairs else -offset * sign
+                for core in range(2):
+                    for tok in range(tok_count):
+                        goal = place(2 * (pair_count - 1 - pair) + core, tok)
+                        route.append((place(2 * pair + core, tok + shift), goal))
+            blocks.append(moved(block, sorted(route)))
+        return blocks
+
     everyone = range(section_count)
-    last_encoder = section_count // 2 - 1
-    encoders = range(last_encoder - 1)
-    inner_encoders = range(last_encoder - 1, last_encoder + 1)
-    inner_decoders = range(last_encoder + 1, last_encoder + 3)
-    decoders = range(last_encoder + 3, section_count)
-
-    def far_along(block, blocks, limit, sign, sections):
+    def far_along(blocks, counts):
         bit = 1
-        while bit <= limit:
-            shifted = along(block, sign * bit, sections)
-            block = jnp.where((blocks // bit) % 2 == 1, shifted, block)
+        while bit < tok_count:
+            shifted = along(blocks, bit, everyone)
+            blocks = jnp.where((counts % tok_count // bit) % 2 == 1, shifted, blocks)
             bit *= 2
-        return block
+        return blocks
 
     def together(*arrays):
         return lax.optimization_barrier(arrays)
@@ -485,17 +465,20 @@
     table = lax.all_gather(offsets, "section").reshape(section_count)
     order = jnp.arange(section_count)
     before = jnp.where(order == 0, 0, jnp.roll(table, 1))
-    shifts = (table - before + WIN) % WIN
-    start = jnp.sum(jnp.where(order[:, None] >= order[None, :], shifts[None, :], 0), axis=1)
-
-    other = tuple(swap(weight, (0, 1)) for weight in mine)
+    turn = section_count // 2
+    moves = jnp.where(
+        order <= turn, (table - before + WIN) % WIN, -((before - table + WIN) % WIN)
+    )
+    start = jnp.sum(jnp.where(order[:, None] >= order[None, :], moves[None, :], 0), axis=1)
+
+    other = [swap(weight) for weight in mine]
 
     info = jnp.stack(
         [
-            shifts,
+            jnp.where(order <= turn, moves, WIN + moves),
             (core_index == order % 2).astype(jnp.int32),
             (pair_index == order // 2).astype(jnp.int32),
-            jnp.roll(shifts, -1),
+            jnp.roll(jnp.where(order <= turn, WIN - moves, -moves), -1),
         ],
         axis=1,
     ).astype(jnp.int32)
@@ -535,7 +518,7 @@
         )(*inputs, *mine, *other, *stores)
         return tuple(result[:2]), result[2]
 
-    def forward(section, cur, nxt, skip, stores):
+    def forward(section, sources, skip, stores):
         if section < section_count // 2:
             mode = "plain"
         else:
@@ -543,7 +526,7 @@
         return section_call(
             lambda *refs: forward_kernel(mode, section, *refs),
             "forward_" + mode,
-            [cur, nxt] + ([skip] if mode == "skip" else []),
+            [*sources] + ([skip] if mode == "skip" else []),
             stores,
             [room(1, BF16), room(3, BF16), room(LEFT_SLOTS, BF16)],
             (6,),
@@ -565,17 +548,19 @@
             (4, 2),
         )
 
+    core_scalar = core_index[None].astype(jnp.int32)
+
     def picked(stores, *ranges):
         result = pl.pallas_call(
             lambda *refs: pick_kernel(ranges, *refs),
             out_shape=(store_shapes[0],)
-            + tuple(jax.ShapeDtypeStruct((count, WIN, SLOT), BF16) for _, count in ranges),
-            in_specs=[HBM],
+            + tuple(jax.ShapeDtypeStruct((count, WIN, SLOT), BF16) for _, count, _ in ranges),
+            in_specs=[SMEM, HBM],
             out_specs=(HBM,) + (VMEM,) * len(ranges),
-            input_output_aliases={0: 0},
+            input_output_aliases={1: 0},
             scratch_shapes=[pltpu.SemaphoreType.DMA((len(ranges),))],
             name="pick",
-        )(stores[0])
+        )(core_scalar, stores[0])
         return (result[0], stores[1]), result[1:]
 
     def unwritten():
@@ -587,7 +572,7 @@
         )()
 
     cur = lax.dynamic_index_in_dim(tokens, core_index, 0, False)
-    nxt = along(cur, 1, everyone)
+    sources = (cur, along(cur, 1, everyone))
     stores = unwritten()
     chosen = jnp.repeat(
         lax.dynamic_index_in_dim(flags, core_index, 0, False), row_count // flags.shape[1]
@@ -599,141 +584,115 @@
     )
     bucket = lax.dynamic_index_in_dim(buckets, core_index, 0, False).astype(BF16)
     bucket = jnp.broadcast_to(bucket[:, None], target.shape)
-    aim_here = jnp.stack([target, bucket])
-
-    low_reach = start[section_count - 1 - 2 * pair_index] - start[2 * pair_index]
-    high_reach = start[section_count - 2 - 2 * pair_index] - start[2 * pair_index + 1]
-    reaches = [jnp.abs(low_reach), jnp.abs(high_reach)]
-    reaches_seen = [
-        jnp.where(pair_index < half_pairs, reaches[slot], reaches[1 - slot]) for slot in range(2)
+    aims = lax.all_gather(jnp.concatenate([target, bucket], axis=1), "tok", axis=0, tiled=True)
+    slab = tok_count * row_count
+    aims = jnp.concatenate([aims, aims[:WIN]], axis=0)
+    first_row = (tok_index * row_count + start[section_count - 1] + 2 * slab) % slab
+    aim = lax.dynamic_slice_in_dim(aims, first_row, WIN, 0)
+
+    outer = jnp.arange(2 * (half_pairs - 1))
+    reaches = start[section_count - 1 - outer] - start[outer]
+    nearer = jnp.minimum(pair_index, pair_count - 1 - pair_index)
+    own = [
+        start[section_count - 1 - 2 * nearer - slot] - start[2 * nearer + slot] for slot in range(2)
     ]
-    target_reach = start[section_count - 1]
-
-    def cut(first, second, at):
-        return lax.dynamic_slice_in_dim(jnp.concatenate([first, second], axis=0), at, WIN, 0)
-
-    def long_shift(blocks, counts, limit, sign, sections):
-        near = far_along(blocks, counts, limit, sign, sections)
-        return near, along(near, sign, sections)
-
-    def short_shift(block, count, limit, sign, sections):
-        blocks = [block]
-        for _ in range(limit + 1):
-            blocks.append(along(blocks[-1], sign, sections))
+    outer_encoders = range(half_pairs - 1)
+    outer_pairs = [*outer_encoders, *range(half_pairs + 1, pair_count)]
+    lowest, beyond = -2, 3
+
+    def between(blocks, lowest, reach):
+        count = jnp.floor_divide(reach, WIN)
         near, beside = blocks[0], blocks[1]
-        for index in range(1, limit + 1):
-            near = jnp.where(count == index, blocks[index], near)
-            beside = jnp.where(count == index, blocks[index + 1], beside)
-        return near, beside
+        for index in range(1, len(blocks) - 1):
+            near = jnp.where(count == lowest + index, blocks[index], near)
+            beside = jnp.where(count == lowest + index, blocks[index + 1], beside)
+        both = jnp.concatenate([near, beside], axis=0)
+        return lax.dynamic_slice_in_dim(both, reach % WIN, WIN, 0)
+
+    def outer_skips(stores, places, sign):
+        stores, posts = picked(stores, *[(at, 1, False) for at in places])
+        post = jnp.concatenate(posts, axis=0)
+        counts = jnp.floor_divide(sign * reaches, WIN)
+        bottom, top = (lowest, beyond) if sign > 0 else (-beyond, -lowest)
+        far = jnp.any((counts < bottom) | (counts >= top))
+        own_reach = jnp.stack([sign * each for each in own])
+        own_count = jnp.floor_divide(own_reach, WIN)
+        turned = jnp.where((own_count < bottom) | (own_count >= top), own_count, 0)
+        post = lax.cond(
+            far, lambda rows: far_along(rows, turned[:, None, None]), lambda rows: rows, post
+        )
+        blocks = across(post, outer_pairs, range(bottom, top + 1), sign)
+        left = own_reach - turned * WIN
+        return stores, [
+            between([block[slot] for block in blocks], bottom, left[slot]) for slot in range(2)
+        ]
+
+    def forward_sources(block, neighbour, goal):
+        return (block, neighbour) if goal <= turn else (neighbour, block)
+
+    def backward_sources(block, neighbour, origin):
+        return (neighbour, block) if origin <= turn else (block, neighbour)
+
+    def step_to(goal):
+        return 1 if goal <= turn else -1
 
     skips = {}
-    aim = None
     for pair in range(pair_count):
         low, high = 2 * pair, 2 * pair + 1
-        stores, z_low = forward(low, cur, nxt, skips.get(low), stores)
-        nxt = along(z_low, 1, everyone)
-        stores, z_high = forward(high, z_low, nxt, skips.get(high), stores)
+        stores, z_low = forward(low, sources, skips.get(low), stores)
+        neighbour = along(z_low, step_to(high), everyone)
+        if pair == half_pairs - 1:
+            inner = across(z_low, (pair,), range(-1, 3), 1)
+            stores, rows = outer_skips(stores, (Z_AT, LOW_SLOTS + Z_AT), 1)
+            neighbour, *rows = together(neighbour, *rows)
+            for goal in range(half_pairs + 1, pair_count):
+                skips[2 * goal + 1], skips[2 * goal] = rows
+        sources = forward_sources(z_low, neighbour, high)
+        stores, z_high = forward(high, sources, skips.get(high), stores)
+        if pair == half_pairs - 1:
+            z_high, *inner = together(z_high, *inner)
+            skips[low + 3] = between(inner, -1, start[low + 3] - start[low])
         if pair < pair_count - 1:
-            nxt = hop(z_high, pair, 1, 1)
-            cur = hop(z_high, pair, 1, 0)
-        if pair == half_pairs - 1:
-            reach = start[low + 3] - start[low]
-            near, beside = short_shift(
-                mirror(z_low, (pair,)), reach // WIN, 2, 1, inner_decoders
-            )
-            skips[low + 3] = cut(near, beside, reach % WIN)
-            cur, nxt, skips[low + 3] = together(cur, nxt, skips[low + 3])
-            stores, posts = picked(stores, (Z_AT, 1), (LOW_SLOTS + Z_AT, 1))
-            post = jnp.concatenate([jnp.concatenate(posts, axis=0), aim_here], axis=2)
-            cur, nxt, post = together(cur, nxt, post)
-            counts = [
-                jnp.concatenate(
-                    [
-                        jnp.full((1, 1, width), each // WIN),
-                        jnp.full((1, 1, channels), target_reach // WIN),
-                    ],
-                    axis=2,
-                )
-                for each in reaches_seen
-            ]
-            near, beside = long_shift(
-                mirror(post, outer_pairs),
-                jnp.concatenate(counts, axis=0),
-                tok_count - 1,
-                1,
-                decoders,
-            )
-            outer_skip = [
-                cut(near[slot, :, :width], beside[slot, :, :width], reaches_seen[slot] % WIN)
-                for slot in range(2)
-            ]
-            aim = jnp.concatenate(
-                [
-                    cut(near[slot, :, width:], beside[slot, :, width:], target_reach % WIN)
-                    for slot in range(2)
-                ],
-                axis=1,
-            )
-            for goal in range(half_pairs + 1, pair_count):
-                skips[2 * goal + 1], skips[2 * goal] = outer_skip
+            neighbour = hop(z_high, pair, 1, step_to(high + 1))
+            sources = forward_sources(hop(z_high, pair, 1, 0), neighbour, high + 1)
 
     skips = {}
     sources = (z_high, aim, w_head)
     for pair in range(pair_count - 1, -1, -1):
         low, high = 2 * pair, 2 * pair + 1
         stores, gx_high = backward(high, sources, skips.get(high), stores)
-        sources = (gx_high, along(gx_high, -1, everyone))
+        neighbour = along(gx_high, -step_to(high), everyone)
+        if pair == half_pairs:
+            inner = across(gx_high, (pair,), range(-2, 2), -1)
+            stores, rows = outer_skips(stores, (LOW_SLOTS + GX_AT, GX_AT), -1)
+            neighbour, *rows = together(neighbour, *rows)
+            for goal in outer_encoders:
+                skips[2 * goal], skips[2 * goal + 1] = rows
+        sources = backward_sources(gx_high, neighbour, high)
         stores, gx_low = backward(low, sources, skips.get(low), stores)
+        if pair == half_pairs:
+            gx_low, *inner = together(gx_low, *inner)
+            skips[high - 3] = between(inner, -2, start[high - 3] - start[high])
         if pair > 0:
-            prv = hop(gx_low, pair - 1, -1, -1)
-            cur = hop(gx_low, pair - 1, -1, 0)
-            sources = (cur, prv)
-        if pair == half_pairs:
-            reach = start[high] - start[high - 3]
-            near, beside = short_shift(
-                mirror(gx_high, (pair,)), reach // WIN, 2, -1, inner_encoders
-            )
-            skips[high - 3] = cut(beside, near, WIN - reach % WIN)
-            cur, prv, skips[high - 3] = together(cur, prv, skips[high - 3])
-            stores, posts = picked(stores, (LOW_SLOTS + GX_AT, 1), (GX_AT, 1))
-            cur, prv, post = together(cur, prv, jnp.concatenate(posts, axis=0))
-            sources = (cur, prv)
-            counts = jnp.stack([each // WIN for each in reaches_seen])[:, None, None]
-            near, beside = long_shift(
-                mirror(post, outer_pairs), counts, tok_count - 2, -1, encoders
-            )
-            outer_skip = [
-                cut(beside[slot], near[slot], WIN - reaches_seen[slot] % WIN) for slot in range(2)
-            ]
-            for goal in range(half_pairs - 1):
-                skips[2 * goal], skips[2 * goal + 1] = outer_skip
+            neighbour = hop(gx_low, pair - 1, -1, -step_to(low))
+            sources = backward_sources(hop(gx_low, pair - 1, -1, 0), neighbour, low)
         if pair == half_pairs - 1:
-            stores, lefts = picked(
-                stores, (LEFT_AT, LEFT_SLOTS), (LOW_SLOTS + LEFT_AT, LEFT_SLOTS)
-            )
-            left_low = swap(lefts[0], (1,))
-            left_high = swap(lefts[1], (0,))
-            cur, prv, left_low, left_high = together(cur, prv, left_low, left_high)
-            sources = (cur, prv)
-
-    stores, rights = picked(
-        stores, (RIGHT_AT, RIGHT_SLOTS), (LOW_SLOTS + RIGHT_AT, RIGHT_SLOTS)
-    )
-    right_high = swap(rights[1], (0,))
-    right_low = swap(rights[0], (1,))
+            stores, given = picked(stores, (LEFT_AT, LEFT_SLOTS, True))
+            *sources, left_other = together(*sources, swap(given[0]))
+
+    stores, given = picked(stores, (RIGHT_AT, RIGHT_SLOTS, True))
+    right_other = swap(given[0])
     total = 4 * width + 2 * hidden
     inner = 4
     outer = tok_count // inner
     strip = width // tok_count
-    split = 4 * width + hidden
     tok_in, tok_out = tok_index % inner, tok_index // inner
     step = width
     parts = pl.pallas_call(
         lambda *refs: weight_kernel(inner, *refs),
-        out_shape=[jax.ShapeDtypeStruct((outer, strip, split), BF16)] * inner
-        + [jax.ShapeDtypeStruct((inner, strip, total - split), BF16)] * outer,
-        in_specs=[SMEM] + [HBM] * 5,
-        out_specs=[VMEM] * (inner + outer),
+        out_shape=[jax.ShapeDtypeStruct((outer, strip, hidden), BF16)] * (3 * inner),
+        in_specs=[SMEM] + [HBM] * 3,
+        out_specs=[VMEM] * (3 * inner),
         scratch_shapes=[
             pltpu.VMEM((2 * WIN, LEFT_SLOTS * SLOT), BF16),
             pltpu.VMEM((2 * WIN, RIGHT_SLOTS * SLOT), BF16),
@@ -745,12 +704,12 @@
     )(
         jnp.stack([core_index, tok_in, tok_out]).astype(jnp.int32),
         stores[0],
-        left_low,
-        left_high,
-        right_low,
-        right_high,
+        left_other,
+        right_other,
     )
-    near_parts, far_parts = parts[:inner], parts[inner:]
+    early_parts, late_parts, far_parts = [
+        parts[group * inner : (group + 1) * inner] for group in range(3)
+    ]
 
     def ring(block, distance, inside):
         route = []
@@ -779,14 +738,18 @@
             result = result + ring(sent, distance, inside).astype(F32)
         return result
 
-    near_sums = first_stage(near_parts, True)
+    early_sums = first_stage(early_parts, True)
     far_sums = first_stage(far_parts, False)
-    near_sums, far_sums = together(near_sums, far_sums)
-    near_result = second_stage(near_sums, tok_out, outer, False)
+    waiting, *late_parts = together(early_sums, *late_parts)
+    late_sums = first_stage(late_parts, True)
+    early_sums, far_sums = together(waiting, far_sums)
+    early_result = second_stage(early_sums, tok_out, outer, False)
+    early_result, late_sums, far_sums = together(early_result, late_sums, far_sums)
+    late_result = second_stage(late_sums, tok_out, outer, False)
     far_result = second_stage(far_sums, tok_in, inner, True)
-    grad_qkv = near_result[:, : 3 * width][None]
-    grad_out = near_result[:, 3 * width : 4 * width][None]
-    grad_up = near_result[:, 4 * width :][None]
+    grad_qkv = early_result[:, : 3 * width][None]
+    grad_out = early_result[:, 3 * width :][None]
+    grad_up = late_result[None]
     grad_down = far_result[None]
     return (grad_qkv, grad_out, grad_up, grad_down)
 

time: 761 us -> 807 us (1.060)
  between operations: 9.76 us -> 34.4 us
  starting transfers between devices: 274 us -> 288 us
  local copies, waits for them, and re-layouts: 27 us -> 35.3 us
    ppermute x72 -> x70, waiting for transfers between devices: 217 us -> 204 us  [moved(): return lax.ppermute(block, ('section', 'tok'), route)]
    ppermute x72 -> x70, starting transfers between devices: 245 us -> 254 us  [moved(): return lax.ppermute(block, ('section', 'tok'), route)]
    ppermute x12 -> x18, waiting for transfers between devices: 58.6 us -> 66.2 us  [ring(): return lax.ppermute(block, 'tok', route)]
    unnamed x39 -> x77, local copies, waits for them, and re-layouts: 18.1 us -> 25.1 us
    ppermute x12 -> x18, starting transfers between devices: 29.2 us -> 33.3 us  [ring(): return lax.ppermute(block, 'tok', route)]
  transfers between devices with their start and end apart: 84 -> 89, of which waited for: 39 -> 36; matrix products, arithmetic and copies ran while one was open for 2% -> 3% of each run, Pallas kernels for 4% -> 2%
where the time goes in v2:
time: 807 us; the launch traced here: 794 us
  starting transfers between devices  288 us (36%)
  waiting for transfers between devices  270 us (33%)
  Pallas kernels  131 us (16%)
  local copies, waits for them, and re-layouts  35.3 us (4%)
  between operations  34.4 us (4%)
  other arithmetic  19.5 us (2%)
  blocking collectives  16.1 us (2%)
    ppermute x70, starting transfers between devices, moved(): return lax.ppermute(block, ('section', 'tok'), route)  254 us
    ppermute x70, waiting for transfers between devices, moved(): return lax.ppermute(block, ('section', 'tok'), route)  204 us
    pallas_call x32, Pallas kernels, section_call(): pl.pallas_call(kernel, out_shape=store_shapes + (rows_bf,), in_specs=[SME...  117 us
    ppermute x18, waiting for transfers between devices, ring(): return lax.ppermute(block, 'tok', route)  66.2 us
    ppermute x18, starting transfers between devices, ring(): return lax.ppermute(block, 'tok', route)  33.3 us
    unnamed x77, local copies, waits for them, and re-layouts  25.1 us
  transfers between devices with their start and end apart: 89, of which 36 were waited for; matrix products, arithmetic and copies ran while one was open for 3% of the time, Pallas kernels for 2%

profile of v2, /device:TPU:35, one launch (start us, length us, event | category | flops | bytes accessed | tf_op | source)
XLA Modules:
  0.0 794.1 jit_solution(17653240591357465515)
XLA Ops:
  13.4 16.1 %all-reduce = s32[16]{0:T(128)S(1)} all-reduce(s32[16]{0:T(128)S(1)} %dynamic-update-slice), channel_id=2, replica_groups=mesh['section'=16,'tok'=16] {'section'}, use_global_device_ids=true, to_apply=%add | all-reduce | flops 16 | bytes 128
  33.4 6.1 forward_plain.8
  44.8 5.5 forward_plain.9
  54.9 8.8 %forward_plain.10 = (bf16[224,128,512]{2,1,0:T(8,128)(2,1)}, f32[112,128,512]{2,1,0:T(8,128)}, bf16[128,512]{1,0:T(8,128)(2,1)S(1)}) custom-call(s32[16,4]{1,0:T(8,128)S(1)} %copy.154.refs_0_, bf16[128,512]{1,0:T(8,128)(2,1)S(1)} %collective-permute-done.13.refs_1_, ...), custom_call_target="tpu_custom_call", output_to_operand_aliasing={{0}: (9, {}), {1}: (10, {})} | custom-call | tf_op jit(solution)/shard_map/forward_plain/pallas_call | solution.py:506
  68.4 9.9 %collective-permute-start.16 = (bf16[128,512]{1,0:T(8,128)(2,1)S(1)}, bf16[128,512]{1,0:T(8,128)(2,1)S(1)}, u32[]{:S(2)}, u32[]{:S(2)}) collective-permute-start(bf16[128,512]{1,0:T(8,128)(2,1)S(1)} %get-tuple-element.182), channel_id=1, source_target_pairs={{0,32},{1,33},{2,34},{3,35},{4,36},{5,37},{6,38},{7,39},{8,40},{9,... | collective-permute-start | bytes 393224 | tf_op jit(solution)/shard_map/ppermute | solution.py:411
  78.3 3.6 collective-permute-start.17
  86.2 4.1 collective-permute-start.18
  97.3 12.6 %collective-permute-start.20 = (bf16[128,512]{1,0:T(8,128)(2,1)S(1)}, bf16[128,512]{1,0:T(8,128)(2,1)S(1)}, u32[]{:S(2)}, u32[]{:S(2)}) collective-permute-start(bf16[128,512]{1,0:T(8,128)(2,1)S(1)} %get-tuple-element.188), channel_id=1, source_target_pairs={{0,47},{1,32},{2,33},{3,34},{4,35},{5,36},{6,37},{7,38},{8,39},{9,... | collective-permute-start | bytes 393224 | tf_op jit(solution)/shard_map/ppermute | solution.py:411
  115.6 9.7 %forward_plain.14 = (bf16[224,128,512]{2,1,0:T(8,128)(2,1)}, f32[112,128,512]{2,1,0:T(8,128)}, bf16[128,512]{1,0:T(8,128)(2,1)S(1)}) custom-call(s32[16,4]{1,0:T(8,128)S(1)} %copy.154.refs_0_, bf16[128,512]{1,0:T(8,128)(2,1)S(1)} %collective-permute-done.19.refs_1_, ...), custom_call_target="tpu_custom_call", output_to_operand_aliasing={{0}: (9, {}), {1}: (10, {})} | custom-call | tf_op jit(solution)/shard_map/forward_plain/pallas_call | solution.py:506
  132.3 11.6 %collective-permute-start.23 = (bf16[2,128,512]{2,1,0:T(8,128)(2,1)}, bf16[2,128,512]{2,1,0:T(8,128)(2,1)S(1)}, u32[]{:S(2)}, u32[]{:S(2)}) collective-permute-start(bf16[2,128,512]{2,1,0:T(8,128)(2,1)} %get-tuple-element.372), channel_id=1, source_target_pairs={{0,239},{1,224},{2,225},{3,226},{4,227},{5,228},{6,229},{7,230},{8... | collective-permute-start | bytes 786440 | tf_op jit(solution)/shard_map/ppermute | solution.py:411
  145.8 9.9 %collective-permute-start.25 = (bf16[2,128,512]{2,1,0:T(8,128)(2,1)}, bf16[2,128,512]{2,1,0:T(8,128)(2,1)S(1)}, u32[]{:S(2)}, u32[]{:S(2)}) collective-permute-start(bf16[2,128,512]{2,1,0:T(8,128)(2,1)} %get-tuple-element.372), channel_id=1, source_target_pairs={{0,225},{1,226},{2,227},{3,228},{4,229},{5,230},{6,231},{7,232},{8... | collective-permute-start | bytes 786440 | tf_op jit(solution)/shard_map/ppermute | solution.py:411
  158.5 51.6 %collective-permute-done.22 = bf16[2,128,512]{2,1,0:T(8,128)(2,1)S(1)} collective-permute-done((bf16[2,128,512]{2,1,0:T(8,128)(2,1)}, bf16[2,128,512]{2,1,0:T(8,128)(2,1)S(1)}, u32[]{:S(2)}, u32[]{:S(2)}) %collective-permute-start.22) | collective-permute-done | bytes 262176 | tf_op jit(solution)/shard_map/ppermute | solution.py:411
  221.8 7.1 collective-permute-done.26
  239.0 4.2 collective-permute-done.34.refs_1_
  246.2 4.2 collective-permute-done.37.refs_1_
  252.5 8.9 %forward_skip.10 = (bf16[224,128,512]{2,1,0:T(8,128)(2,1)}, f32[112,128,512]{2,1,0:T(8,128)}, bf16[128,512]{1,0:T(8,128)(2,1)S(1)}) custom-call(s32[16,4]{1,0:T(8,128)S(1)} %copy.154.refs_0_, bf16[128,512]{1,0:T(8,128)(2,1)S(1)} %collective-permute-done.38.refs_1_, ...), custom_call_target="tpu_custom_call", output_to_operand_aliasing={{0}: (10, {}), {1}: (11, {})} | custom-call | tf_op jit(solution)/shard_map/forward_skip/pallas_call | solution.py:506
  261.5 4.7 collective-permute-done.40.refs_1_
  277.6 8.6 %backward_head.1 = (bf16[224,128,512]{2,1,0:T(8,128)(2,1)}, f32[112,128,512]{2,1,0:T(8,128)}, bf16[128,512]{1,0:T(8,128)(2,1)S(1)}) custom-call(s32[16,4]{1,0:T(8,128)S(1)} %copy.154.refs_0_, bf16[128,512]{1,0:T(8,128)(2,1)S(1)} %get-tuple-element.229.refs_1_, bf16[128,256]{1,0:T(8,128)(2,1)S(1)} %fusion.50.refs_2_, ...), custom_call_target="tpu_custom_call", output_to_operand_aliasing={{0}: (10, {}), {1}: (11, {})} | custom-call | tf_op jit(solution)/shard_map/backward_head/pallas_call | solution.py:506
  286.1 3.6 collective-permute-start.44
  298.5 8.3 %backward_plain.9 = (bf16[224,128,512]{2,1,0:T(8,128)(2,1)}, f32[112,128,512]{2,1,0:T(8,128)}, bf16[128,512]{1,0:T(8,128)(2,1)S(1)}) custom-call(s32[16,4]{1,0:T(8,128)S(1)} %copy.154.refs_0_, bf16[128,512]{1,0:T(8,128)(2,1)S(1)} %get-tuple-element.238.refs_1_, ...), custom_call_target="tpu_custom_call", output_to_operand_aliasing={{0}: (9, {}), {1}: (10, {})} | custom-call | tf_op jit(solution)/shard_map/backward_plain/pallas_call | solution.py:506
  318.9 8.4 %backward_plain.12 = (bf16[224,128,512]{2,1,0:T(8,128)(2,1)}, f32[112,128,512]{2,1,0:T(8,128)}, bf16[128,512]{1,0:T(8,128)(2,1)S(1)}) custom-call(s32[16,4]{1,0:T(8,128)S(1)} %copy.154.refs_0_, bf16[128,512]{1,0:T(8,128)(2,1)S(1)} %collective-permute-done.51.refs_1_, ...), custom_call_target="tpu_custom_call", output_to_operand_aliasing={{0}: (9, {}), {1}: (10, {})} | custom-call | tf_op jit(solution)/shard_map/backward_plain/pallas_call | solution.py:506
  332.2 105.3 %collective-permute-start.54 = (bf16[2,128,512]{2,1,0:T(8,128)(2,1)}, bf16[2,128,512]{2,1,0:T(8,128)(2,1)S(1)}, u32[]{:S(2)}, u32[]{:S(2)}) collective-permute-start(bf16[2,128,512]{2,1,0:T(8,128)(2,1)} %get-tuple-element.373), channel_id=1, source_target_pairs={{0,225},{1,226},{2,227},{3,228},{4,229},{5,230},{6,231},{7,232},{8... | collective-permute-start | bytes 786440 | tf_op jit(solution)/shard_map/ppermute | solution.py:411
  440.1 10.3 %collective-permute-start.56 = (bf16[2,128,512]{2,1,0:T(8,128)(2,1)}, bf16[2,128,512]{2,1,0:T(8,128)(2,1)S(1)}, u32[]{:S(2)}, u32[]{:S(2)}) collective-permute-start(bf16[2,128,512]{2,1,0:T(8,128)(2,1)} %get-tuple-element.373), channel_id=1, source_target_pairs={{0,239},{1,224},{2,225},{3,226},{4,227},{5,228},{6,229},{7,230},{8... | collective-permute-start | bytes 786440 | tf_op jit(solution)/shard_map/ppermute | solution.py:411
  450.4 5.3 collective-permute-start.57
  455.8 6.5 collective-permute-start.59
  462.2 5.5 collective-permute-start.58
  475.1 55.5 %collective-permute-done.57 = bf16[2,128,512]{2,1,0:T(8,128)(2,1)S(1)} collective-permute-done((bf16[2,128,512]{2,1,0:T(8,128)(2,1)}, bf16[2,128,512]{2,1,0:T(8,128)(2,1)S(1)}, u32[]{:S(2)}, u32[]{:S(2)}) %collective-permute-start.57) | collective-permute-done | bytes 262176 | tf_op jit(solution)/shard_map/ppermute | solution.py:411
  541.7 9.1 %backward_double.1 = (bf16[224,128,512]{2,1,0:T(8,128)(2,1)}, f32[112,128,512]{2,1,0:T(8,128)}, bf16[128,512]{1,0:T(8,128)(2,1)S(1)}) custom-call(s32[16,4]{1,0:T(8,128)S(1)} %copy.154.refs_0_, bf16[128,512]{1,0:T(8,128)(2,1)S(1)} %collective-permute-done.64.refs_1_, ...), custom_call_target="tpu_custom_call", output_to_operand_aliasing={{0}: (9, {}), {1}: (10, {})} | custom-call | tf_op jit(solution)/shard_map/backward_double/pallas_call | solution.py:506
  550.8 3.7 collective-permute-start.66
  563.9 5.3 collective-permute-done.67.refs_1_
  579.8 8.4 %backward_skip.9 = (bf16[224,128,512]{2,1,0:T(8,128)(2,1)}, f32[112,128,512]{2,1,0:T(8,128)}, bf16[128,512]{1,0:T(8,128)(2,1)S(1)}) custom-call(s32[16,4]{1,0:T(8,128)S(1)} %copy.154.refs_0_, bf16[128,512]{1,0:T(8,128)(2,1)S(1)} %collective-permute-done.70.refs_1_, ...), custom_call_target="tpu_custom_call", output_to_operand_aliasing={{0}: (10, {}), {1}: (11, {})} | custom-call | tf_op jit(solution)/shard_map/backward_skip/pallas_call | solution.py:506
  590.8 4.4 collective-permute-done.71.refs_1_
  595.2 3.5 collective-permute-done.72.refs_2_
  607.3 27.7 %collective-permute-done.74.refs_1_ = bf16[128,512]{1,0:T(8,128)(2,1)S(1)} collective-permute-done((bf16[128,512]{1,0:T(8,128)(2,1)S(1)}, bf16[128,512]{1,0:T(8,128)(2,1)S(1)}, u32[]{:S(2)}, u32[]{:S(2)}) %collective-permute-start.74) | collective-permute-done | bytes 131104 | tf_op jit(solution)/shard_map/ppermute | solution.py:411
  636.2 9.7 %backward_skip.12 = (bf16[224,128,512]{2,1,0:T(8,128)(2,1)}, f32[112,128,512]{2,1,0:T(8,128)}, bf16[128,512]{1,0:T(8,128)(2,1)S(1)}) custom-call(s32[16,4]{1,0:T(8,128)S(1)} %copy.154.refs_0_, bf16[128,512]{1,0:T(8,128)(2,1)S(1)} %collective-permute-done.74.refs_1_, ...), custom_call_target="tpu_custom_call", output_to_operand_aliasing={{0}: (10, {}), {1}: (11, {})} | custom-call | tf_op jit(solution)/shard_map/backward_skip/pallas_call | solution.py:506
  646.0 4.6 collective-permute-done.76.refs_1_
  650.6 9.8 %backward_skip.13 = (bf16[224,128,512]{2,1,0:T(8,128)(2,1)}, f32[112,128,512]{2,1,0:T(8,128)}, bf16[128,512]{1,0:T(8,128)(2,1)}) custom-call(s32[16,4]{1,0:T(8,128)S(1)} %copy.154.refs_0_, bf16[128,512]{1,0:T(8,128)(2,1)S(1)} %collective-permute-done.76.refs_1_, ...), custom_call_target="tpu_custom_call", output_to_operand_aliasing={{0}: (10, {}), {1}: (11, {})} | custom-call | tf_op jit(solution)/shard_map/backward_skip/pallas_call | solution.py:506
  662.8 3.6 collective-permute-start.77
  670.2 6.6 weight_grads.1
  676.8 5.0 collective-permute-start.79
  683.2 6.8 collective-permute-start.82
  693.0 6.3 collective-permute-start.83
  699.3 6.5 collective-permute-done.80
  707.5 20.1 %collective-permute-done.82 = bf16[4,32,2048]{2,1,0:T(8,128)(2,1)} collective-permute-done((bf16[4,32,2048]{2,1,0:T(8,128)(2,1)}, bf16[4,32,2048]{2,1,0:T(8,128)(2,1)}, u32[]{:S(2)}, u32[]{:S(2)}) %collective-permute-start.82) | collective-permute-done | bytes 524320 | tf_op jit(solution)/shard_map/ppermute | solution.py:723
  727.6 6.9 collective-permute-done.83
  746.1 4.5 collective-permute-done.87
  752.7 14.1 %collective-permute-done.89 = bf16[4,32,2048]{2,1,0:T(8,128)(2,1)} collective-permute-done((bf16[4,32,2048]{2,1,0:T(8,128)(2,1)S(1)}, bf16[4,32,2048]{2,1,0:T(8,128)(2,1)}, u32[]{:S(2)}, u32[]{:S(2)}) %collective-permute-start.89) | collective-permute-done | bytes 524320 | tf_op jit(solution)/shard_map/ppermute | solution.py:723
  777.4 5.3 collective-permute-done.91
  (308 shorter events, 192.1 us)
Async XLA Ops:
  7.2 262.7 %all-gather.3.cloned.1.call-start = ((), (), s32[]{:S(2)}) async-start(), calls=%async_computation | async-start | bytes 1114112 | tf_op jit(solution)/shard_map/all_gather | solution.py:587
  9.1 22.7 %collective-permute-start.9 = (bf16[512,2048]{1,0:T(8,128)(2,1)S(1)}, bf16[512,2048]{1,0:T(8,128)(2,1)}, u32[]{:S(2)}, u32[]{:S(2)}) collective-permute-start(bf16[512,2048]{1,0:T(8,128)(2,1)S(1)} %pad_maximum_fusion.refs_3_.refs_4_), channel_id=1, source_target_pairs={{0,16},{1,17},{2,18},{3,19},{4,20},{5,21},{6,22},{7,23},{8,24},{9,... | collective-permute-start | bytes 6291464 | tf_op jit(solution)/shard_map/ppermute | solution.py:411
  9.9 22.0 %collective-permute-start.10 = (bf16[512,2048]{1,0:T(8,128)(2,1)}, bf16[512,2048]{1,0:T(8,128)(2,1)}, u32[]{:S(2)}, u32[]{:S(2)}) collective-permute-start(bf16[512,2048]{1,0:T(8,128)(2,1)} %bitcast.231), channel_id=1, source_target_pairs={{0,16},{1,17},{2,18},{3,19},{4,20},{5,21},{6,22},{7,23},{8,24},{9,... | collective-permute-start | bytes 6291464 | tf_op jit(solution)/shard_map/ppermute | solution.py:411
  10.0 21.9 %collective-permute-start.11 = (bf16[512,2048]{1,0:T(8,128)(2,1)}, bf16[512,2048]{1,0:T(8,128)(2,1)}, u32[]{:S(2)}, u32[]{:S(2)}) collective-permute-start(bf16[512,2048]{1,0:T(8,128)(2,1)} %bitcast.264), channel_id=1, source_target_pairs={{0,16},{1,17},{2,18},{3,19},{4,20},{5,21},{6,22},{7,23},{8,24},{9,... | collective-permute-start | bytes 6291464 | tf_op jit(solution)/shard_map/ppermute | solution.py:411
  10.4 21.4 %collective-permute-start.8 = (bf16[128,512]{1,0:T(8,128)(2,1)S(1)}, bf16[128,512]{1,0:T(8,128)(2,1)S(1)}, u32[]{:S(2)}, u32[]{:S(2)}) collective-permute-start(bf16[128,512]{1,0:T(8,128)(2,1)S(1)} %dynamic-slice_bitcast_fusion.9.refs_1_), channel_id=1, source_target_pairs={{1,0},{2,1},{3,2},{4,3},{5,4},{6,5},{7,6},{8,7},{9,8},{10,9},{11,1... | collective-permute-start | bytes 393224 | tf_op jit(solution)/shard_map/ppermute | solution.py:411
  68.4 14.3 %collective-permute-start.16 = (bf16[128,512]{1,0:T(8,128)(2,1)S(1)}, bf16[128,512]{1,0:T(8,128)(2,1)S(1)}, u32[]{:S(2)}, u32[]{:S(2)}) collective-permute-start(bf16[128,512]{1,0:T(8,128)(2,1)S(1)} %get-tuple-element.182), channel_id=1, source_target_pairs={{0,32},{1,33},{2,34},{3,35},{4,36},{5,37},{6,38},{7,39},{8,40},{9,... | collective-permute-start | bytes 393224 | tf_op jit(solution)/shard_map/ppermute | solution.py:411
  95.1 19.0 %collective-permute-start.19 = (bf16[128,512]{1,0:T(8,128)(2,1)S(1)}, bf16[128,512]{1,0:T(8,128)(2,1)S(1)}, u32[]{:S(2)}, u32[]{:S(2)}) collective-permute-start(bf16[128,512]{1,0:T(8,128)(2,1)S(1)} %get-tuple-element.188), channel_id=1, source_target_pairs={{0,32},{1,33},{2,34},{3,35},{4,36},{5,37},{6,38},{7,39},{8,40},{9,... | collective-permute-start | bytes 393224 | tf_op jit(solution)/shard_map/ppermute | solution.py:411
  97.3 16.8 %collective-permute-start.20 = (bf16[128,512]{1,0:T(8,128)(2,1)S(1)}, bf16[128,512]{1,0:T(8,128)(2,1)S(1)}, u32[]{:S(2)}, u32[]{:S(2)}) collective-permute-start(bf16[128,512]{1,0:T(8,128)(2,1)S(1)} %get-tuple-element.188), channel_id=1, source_target_pairs={{0,47},{1,32},{2,33},{3,34},{4,35},{5,36},{6,37},{7,38},{8,39},{9,... | collective-permute-start | bytes 393224 | tf_op jit(solution)/shard_map/ppermute | solution.py:411
  130.3 79.8 %collective-permute-start.22 = (bf16[2,128,512]{2,1,0:T(8,128)(2,1)}, bf16[2,128,512]{2,1,0:T(8,128)(2,1)S(1)}, u32[]{:S(2)}, u32[]{:S(2)}) collective-permute-start(bf16[2,128,512]{2,1,0:T(8,128)(2,1)} %get-tuple-element.372), channel_id=1, source_target_pairs={{0,238},{1,239},{2,224},{3,225},{4,226},{5,227},{6,228},{7,229},{8... | collective-permute-start | bytes 786440 | tf_op jit(solution)/shard_map/ppermute | solution.py:411
  132.3 85.6 %collective-permute-start.23 = (bf16[2,128,512]{2,1,0:T(8,128)(2,1)}, bf16[2,128,512]{2,1,0:T(8,128)(2,1)S(1)}, u32[]{:S(2)}, u32[]{:S(2)}) collective-permute-start(bf16[2,128,512]{2,1,0:T(8,128)(2,1)} %get-tuple-element.372), channel_id=1, source_target_pairs={{0,239},{1,224},{2,225},{3,226},{4,227},{5,228},{6,229},{7,230},{8... | collective-permute-start | bytes 786440 | tf_op jit(solution)/shard_map/ppermute | solution.py:411
  143.9 74.8 %collective-permute-start.24 = (bf16[2,128,512]{2,1,0:T(8,128)(2,1)}, bf16[2,128,512]{2,1,0:T(8,128)(2,1)S(1)}, u32[]{:S(2)}, u32[]{:S(2)}) collective-permute-start(bf16[2,128,512]{2,1,0:T(8,128)(2,1)} %get-tuple-element.372), channel_id=1, source_target_pairs={{0,224},{1,225},{2,226},{3,227},{4,228},{5,229},{6,230},{7,231},{8... | collective-permute-start | bytes 786440 | tf_op jit(solution)/shard_map/ppermute | solution.py:411
  145.8 73.6 %collective-permute-start.25 = (bf16[2,128,512]{2,1,0:T(8,128)(2,1)}, bf16[2,128,512]{2,1,0:T(8,128)(2,1)S(1)}, u32[]{:S(2)}, u32[]{:S(2)}) collective-permute-start(bf16[2,128,512]{2,1,0:T(8,128)(2,1)} %get-tuple-element.372), channel_id=1, source_target_pairs={{0,225},{1,226},{2,227},{3,228},{4,229},{5,230},{6,231},{7,232},{8... | collective-permute-start | bytes 786440 | tf_op jit(solution)/shard_map/ppermute | solution.py:411
  155.8 64.3 %collective-permute-start.27 = (bf16[2,128,512]{2,1,0:T(8,128)(2,1)}, bf16[2,128,512]{2,1,0:T(8,128)(2,1)}, u32[]{:S(2)}, u32[]{:S(2)}) collective-permute-start(bf16[2,128,512]{2,1,0:T(8,128)(2,1)} %get-tuple-element.372), channel_id=1, source_target_pairs={{0,237},{1,238},{2,239},{3,224},{4,225},{5,226},{6,227},{7,228},{8... | collective-permute-start | bytes 786440 | tf_op jit(solution)/shard_map/ppermute | solution.py:411
  210.1 18.8 %collective-permute-start.26 = (bf16[2,128,512]{2,1,0:T(8,128)(2,1)}, bf16[2,128,512]{2,1,0:T(8,128)(2,1)}, u32[]{:S(2)}, u32[]{:S(2)}) collective-permute-start(bf16[2,128,512]{2,1,0:T(8,128)(2,1)} %get-tuple-element.372), channel_id=1, source_target_pairs={{0,226},{1,227},{2,228},{3,229},{4,230},{5,231},{6,232},{7,233},{8... | collective-permute-start | bytes 786440 | tf_op jit(solution)/shard_map/ppermute | solution.py:411
  217.9 13.1 %collective-permute-start.21 = (bf16[128,512]{1,0:T(8,128)(2,1)S(1)}, bf16[128,512]{1,0:T(8,128)(2,1)S(1)}, u32[]{:S(2)}, u32[]{:S(2)}) collective-permute-start(bf16[128,512]{1,0:T(8,128)(2,1)S(1)} %get-tuple-element.191.refs_1_), channel_id=1, source_target_pairs={{1,0},{2,1},{3,2},{4,3},{5,4},{6,5},{7,6},{8,7},{9,8},{10,9},{11,1... | collective-permute-start | bytes 393224 | tf_op jit(solution)/shard_map/ppermute | solution.py:411
  218.7 14.6 %collective-permute-start.28 = (bf16[128,512]{1,0:T(8,128)(2,1)S(1)}, bf16[128,512]{1,0:T(8,128)(2,1)S(1)}, u32[]{:S(2)}, u32[]{:S(2)}) collective-permute-start(bf16[128,512]{1,0:T(8,128)(2,1)S(1)} %get-tuple-element.191.refs_1_), channel_id=1, source_target_pairs={{96,129},{97,130},{98,131},{99,132},{100,133},{101,134},{102,135},... | collective-permute-start | bytes 393224 | tf_op jit(solution)/shard_map/ppermute | solution.py:411
  219.4 14.0 %collective-permute-start.29 = (bf16[128,512]{1,0:T(8,128)(2,1)S(1)}, bf16[128,512]{1,0:T(8,128)(2,1)S(1)}, u32[]{:S(2)}, u32[]{:S(2)}) collective-permute-start(bf16[128,512]{1,0:T(8,128)(2,1)S(1)} %get-tuple-element.191.refs_1_), channel_id=1, source_target_pairs={{96,128},{97,129},{98,130},{99,131},{100,132},{101,133},{102,134},... | collective-permute-start | bytes 393224 | tf_op jit(solution)/shard_map/ppermute | solution.py:411
  220.1 13.3 %collective-permute-start.30 = (bf16[128,512]{1,0:T(8,128)(2,1)S(1)}, bf16[128,512]{1,0:T(8,128)(2,1)S(1)}, u32[]{:S(2)}, u32[]{:S(2)}) collective-permute-start(bf16[128,512]{1,0:T(8,128)(2,1)S(1)} %get-tuple-element.191.refs_1_), channel_id=1, source_target_pairs={{96,143},{97,128},{98,129},{99,130},{100,131},{101,132},{102,133},... | collective-permute-start | bytes 393224 | tf_op jit(solution)/shard_map/ppermute | solution.py:411
  332.2 130.0 %collective-permute-start.54 = (bf16[2,128,512]{2,1,0:T(8,128)(2,1)}, bf16[2,128,512]{2,1,0:T(8,128)(2,1)S(1)}, u32[]{:S(2)}, u32[]{:S(2)}) collective-permute-start(bf16[2,128,512]{2,1,0:T(8,128)(2,1)} %get-tuple-element.373), channel_id=1, source_target_pairs={{0,225},{1,226},{2,227},{3,228},{4,229},{5,230},{6,231},{7,232},{8... | collective-permute-start | bytes 786440 | tf_op jit(solution)/shard_map/ppermute | solution.py:411
  437.5 36.0 %collective-permute-start.55 = (bf16[2,128,512]{2,1,0:T(8,128)(2,1)}, bf16[2,128,512]{2,1,0:T(8,128)(2,1)S(1)}, u32[]{:S(2)}, u32[]{:S(2)}) collective-permute-start(bf16[2,128,512]{2,1,0:T(8,128)(2,1)} %get-tuple-element.373), channel_id=1, source_target_pairs={{0,224},{1,225},{2,226},{3,227},{4,228},{5,229},{6,230},{7,231},{8... | collective-permute-start | bytes 786440 | tf_op jit(solution)/shard_map/ppermute | solution.py:411
  440.1 34.2 %collective-permute-start.56 = (bf16[2,128,512]{2,1,0:T(8,128)(2,1)}, bf16[2,128,512]{2,1,0:T(8,128)(2,1)S(1)}, u32[]{:S(2)}, u32[]{:S(2)}) collective-permute-start(bf16[2,128,512]{2,1,0:T(8,128)(2,1)} %get-tuple-element.373), channel_id=1, source_target_pairs={{0,239},{1,224},{2,225},{3,226},{4,227},{5,228},{6,229},{7,230},{8... | collective-permute-start | bytes 786440 | tf_op jit(solution)/shard_map/ppermute | solution.py:411
  450.4 80.1 %collective-permute-start.57 = (bf16[2,128,512]{2,1,0:T(8,128)(2,1)}, bf16[2,128,512]{2,1,0:T(8,128)(2,1)S(1)}, u32[]{:S(2)}, u32[]{:S(2)}) collective-permute-start(bf16[2,128,512]{2,1,0:T(8,128)(2,1)} %get-tuple-element.373), channel_id=1, source_target_pairs={{0,238},{1,239},{2,224},{3,225},{4,226},{5,227},{6,228},{7,229},{8... | collective-permute-start | bytes 786440 | tf_op jit(solution)/shard_map/ppermute | solution.py:411
  455.8 75.4 %collective-permute-start.59 = (bf16[2,128,512]{2,1,0:T(8,128)(2,1)}, bf16[2,128,512]{2,1,0:T(8,128)(2,1)}, u32[]{:S(2)}, u32[]{:S(2)}) collective-permute-start(bf16[2,128,512]{2,1,0:T(8,128)(2,1)} %get-tuple-element.373), channel_id=1, source_target_pairs={{0,226},{1,227},{2,228},{3,229},{4,230},{5,231},{6,232},{7,233},{8... | collective-permute-start | bytes 786440 | tf_op jit(solution)/shard_map/ppermute | solution.py:411
  462.2 70.7 %collective-permute-start.58 = (bf16[2,128,512]{2,1,0:T(8,128)(2,1)}, bf16[2,128,512]{2,1,0:T(8,128)(2,1)}, u32[]{:S(2)}, u32[]{:S(2)}) collective-permute-start(bf16[2,128,512]{2,1,0:T(8,128)(2,1)} %get-tuple-element.373), channel_id=1, source_target_pairs={{0,237},{1,238},{2,239},{3,224},{4,225},{5,226},{6,227},{7,228},{8... | collective-permute-start | bytes 786440 | tf_op jit(solution)/shard_map/ppermute | solution.py:411
  473.5 61.4 %collective-permute-start.53 = (bf16[128,512]{1,0:T(8,128)(2,1)S(1)}, bf16[128,512]{1,0:T(8,128)(2,1)S(1)}, u32[]{:S(2)}, u32[]{:S(2)}) collective-permute-start(bf16[128,512]{1,0:T(8,128)(2,1)S(1)} %get-tuple-element.250.refs_1_), channel_id=1, source_target_pairs={{1,0},{2,1},{3,2},{4,3},{5,4},{6,5},{7,6},{8,7},{9,8},{10,9},{11,1... | collective-permute-start | bytes 393224 | tf_op jit(solution)/shard_map/ppermute | solution.py:411
  474.4 63.0 %collective-permute-start.60 = (bf16[128,512]{1,0:T(8,128)(2,1)S(1)}, bf16[128,512]{1,0:T(8,128)(2,1)S(1)}, u32[]{:S(2)}, u32[]{:S(2)}) collective-permute-start(bf16[128,512]{1,0:T(8,128)(2,1)S(1)} %get-tuple-element.250.refs_1_), channel_id=1, source_target_pairs={{128,98},{129,99},{130,100},{131,101},{132,102},{133,103},{134,104... | collective-permute-start | bytes 393224 | tf_op jit(solution)/shard_map/ppermute | solution.py:411
  559.7 12.5 %collective-permute-start.69 = (bf16[7,128,512]{2,1,0:T(8,128)(2,1)}, bf16[7,128,512]{2,1,0:T(8,128)(2,1)S(1)}, u32[]{:S(2)}, u32[]{:S(2)}) collective-permute-start(bf16[7,128,512]{2,1,0:T(8,128)(2,1)} %get-tuple-element.270), channel_id=1, source_target_pairs={{0,16},{1,17},{2,18},{3,19},{4,20},{5,21},{6,22},{7,23},{8,24},{9,... | collective-permute-start | bytes 2752520 | tf_op jit(solution)/shard_map/ppermute | solution.py:411
  561.3 7.9 collective-permute-start.67
  562.6 9.5 %collective-permute-start.68 = (bf16[128,512]{1,0:T(8,128)(2,1)S(1)}, bf16[128,512]{1,0:T(8,128)(2,1)S(1)}, u32[]{:S(2)}, u32[]{:S(2)}) collective-permute-start(bf16[128,512]{1,0:T(8,128)(2,1)S(1)} %get-tuple-element.268), channel_id=1, source_target_pairs={{32,0},{33,1},{34,2},{35,3},{36,4},{37,5},{38,6},{39,7},{40,8},{41... | collective-permute-start | bytes 393224 | tf_op jit(solution)/shard_map/ppermute | solution.py:411
  588.2 7.0 collective-permute-start.71
  589.5 9.2 %collective-permute-start.72 = (bf16[128,512]{1,0:T(8,128)(2,1)S(1)}, bf16[128,512]{1,0:T(8,128)(2,1)S(1)}, u32[]{:S(2)}, u32[]{:S(2)}) collective-permute-start(bf16[128,512]{1,0:T(8,128)(2,1)S(1)} %get-tuple-element.280), channel_id=1, source_target_pairs={{32,0},{33,1},{34,2},{35,3},{36,4},{37,5},{38,6},{39,7},{40,8},{41... | collective-permute-start | bytes 393224 | tf_op jit(solution)/shard_map/ppermute | solution.py:411
  604.7 30.3 %collective-permute-start.74 = (bf16[128,512]{1,0:T(8,128)(2,1)S(1)}, bf16[128,512]{1,0:T(8,128)(2,1)S(1)}, u32[]{:S(2)}, u32[]{:S(2)}) collective-permute-start(bf16[128,512]{1,0:T(8,128)(2,1)S(1)} %get-tuple-element.286), channel_id=1, source_target_pairs={{32,1},{33,2},{34,3},{35,4},{36,5},{37,6},{38,7},{39,8},{40,9},{41... | collective-permute-start | bytes 393224 | tf_op jit(solution)/shard_map/ppermute | solution.py:411
  606.0 30.3 %collective-permute-start.75 = (bf16[128,512]{1,0:T(8,128)(2,1)S(1)}, bf16[128,512]{1,0:T(8,128)(2,1)S(1)}, u32[]{:S(2)}, u32[]{:S(2)}) collective-permute-start(bf16[128,512]{1,0:T(8,128)(2,1)S(1)} %get-tuple-element.286), channel_id=1, source_target_pairs={{32,0},{33,1},{34,2},{35,3},{36,4},{37,5},{38,6},{39,7},{40,8},{41... | collective-permute-start | bytes 393224 | tf_op jit(solution)/shard_map/ppermute | solution.py:411
  676.7 15.5 %collective-permute-start.78 = (bf16[4,32,2048]{2,1,0:T(8,128)(2,1)S(1)}, bf16[4,32,2048]{2,1,0:T(8,128)(2,1)S(1)}, u32[]{:S(2)}, u32[]{:S(2)}) collective-permute-start(bf16[4,32,2048]{2,1,0:T(8,128)(2,1)S(1)} %get-tuple-element.297), channel_id=1, source_target_pairs={{0,1},{1,2},{2,3},{3,0},{4,5},{5,6},{6,7},{7,4},{8,9},{9,10},{10,1... | collective-permute-start | bytes 1572872 | tf_op jit(solution)/shard_map/ppermute | solution.py:723
  676.8 22.5 %collective-permute-start.79 = (bf16[4,32,2048]{2,1,0:T(8,128)(2,1)}, bf16[4,32,2048]{2,1,0:T(8,128)(2,1)}, u32[]{:S(2)}, u32[]{:S(2)}) collective-permute-start(bf16[4,32,2048]{2,1,0:T(8,128)(2,1)} %get-tuple-element.298), channel_id=1, source_target_pairs={{0,2},{1,3},{2,0},{3,1},{4,6},{5,7},{6,4},{7,5},{8,10},{9,11},{10,... | collective-permute-start | bytes 1572872 | tf_op jit(solution)/shard_map/ppermute | solution.py:723
  681.9 23.9 %collective-permute-start.80 = (bf16[4,32,2048]{2,1,0:T(8,128)(2,1)}, bf16[4,32,2048]{2,1,0:T(8,128)(2,1)}, u32[]{:S(2)}, u32[]{:S(2)}) collective-permute-start(bf16[4,32,2048]{2,1,0:T(8,128)(2,1)} %get-tuple-element.299), channel_id=1, source_target_pairs={{0,3},{1,0},{2,1},{3,2},{4,7},{5,4},{6,5},{7,6},{8,11},{9,8},{10,9... | collective-permute-start | bytes 1572872 | tf_op jit(solution)/shard_map/ppermute | solution.py:723
  681.9 25.6 %collective-permute-start.81 = (bf16[4,32,2048]{2,1,0:T(8,128)(2,1)}, bf16[4,32,2048]{2,1,0:T(8,128)(2,1)}, u32[]{:S(2)}, u32[]{:S(2)}) collective-permute-start(bf16[4,32,2048]{2,1,0:T(8,128)(2,1)} %get-tuple-element.306), channel_id=1, source_target_pairs={{0,4},{1,5},{2,6},{3,7},{4,8},{5,9},{6,10},{7,11},{8,12},{9,13},{1... | collective-permute-start | bytes 1572872 | tf_op jit(solution)/shard_map/ppermute | solution.py:723
  683.2 44.4 %collective-permute-start.82 = (bf16[4,32,2048]{2,1,0:T(8,128)(2,1)}, bf16[4,32,2048]{2,1,0:T(8,128)(2,1)}, u32[]{:S(2)}, u32[]{:S(2)}) collective-permute-start(bf16[4,32,2048]{2,1,0:T(8,128)(2,1)} %get-tuple-element.307), channel_id=1, source_target_pairs={{0,8},{1,9},{2,10},{3,11},{4,12},{5,13},{6,14},{7,15},{8,0},{9,1},... | collective-permute-start | bytes 1572872 | tf_op jit(solution)/shard_map/ppermute | solution.py:723
  693.0 41.5 %collective-permute-start.83 = (bf16[4,32,2048]{2,1,0:T(8,128)(2,1)}, bf16[4,32,2048]{2,1,0:T(8,128)(2,1)}, u32[]{:S(2)}, u32[]{:S(2)}) collective-permute-start(bf16[4,32,2048]{2,1,0:T(8,128)(2,1)} %get-tuple-element.308), channel_id=1, source_target_pairs={{0,12},{1,13},{2,14},{3,15},{4,0},{5,1},{6,2},{7,3},{8,4},{9,5},{1... | collective-permute-start | bytes 1572872 | tf_op jit(solution)/shard_map/ppermute | solution.py:723
  737.0 8.0 %collective-permute-start.86 = (bf16[32,2048]{1,0:T(8,128)(2,1)}, bf16[32,2048]{1,0:T(8,128)(2,1)}, u32[]{:S(2)}, u32[]{:S(2)}) collective-permute-start(bf16[32,2048]{1,0:T(8,128)(2,1)} %get-tuple-element.351), channel_id=1, source_target_pairs={{0,12},{1,13},{2,14},{3,15},{4,0},{5,1},{6,2},{7,3},{8,4},{9,5},{1... | collective-permute-start | bytes 393224 | tf_op jit(solution)/shard_map/ppermute | solution.py:723
  738.4 12.1 %collective-permute-start.87 = (bf16[4,32,2048]{2,1,0:T(8,128)(2,1)S(1)}, bf16[4,32,2048]{2,1,0:T(8,128)(2,1)S(1)}, u32[]{:S(2)}, u32[]{:S(2)}) collective-permute-start(bf16[4,32,2048]{2,1,0:T(8,128)(2,1)S(1)} %get-tuple-element.311), channel_id=1, source_target_pairs={{0,1},{1,2},{2,3},{3,0},{4,5},{5,6},{6,7},{7,4},{8,9},{9,10},{10,1... | collective-permute-start | bytes 1572872 | tf_op jit(solution)/shard_map/ppermute | solution.py:723
  741.3 11.4 %collective-permute-start.88 = (bf16[4,32,2048]{2,1,0:T(8,128)(2,1)S(1)}, bf16[4,32,2048]{2,1,0:T(8,128)(2,1)}, u32[]{:S(2)}, u32[]{:S(2)}) collective-permute-start(bf16[4,32,2048]{2,1,0:T(8,128)(2,1)S(1)} %get-tuple-element.312), channel_id=1, source_target_pairs={{0,2},{1,3},{2,0},{3,1},{4,6},{5,7},{6,4},{7,5},{8,10},{9,11},{10,... | collective-permute-start | bytes 1572872 | tf_op jit(solution)/shard_map/ppermute | solution.py:723
  742.2 24.5 %collective-permute-start.89 = (bf16[4,32,2048]{2,1,0:T(8,128)(2,1)S(1)}, bf16[4,32,2048]{2,1,0:T(8,128)(2,1)}, u32[]{:S(2)}, u32[]{:S(2)}) collective-permute-start(bf16[4,32,2048]{2,1,0:T(8,128)(2,1)S(1)} %get-tuple-element.313), channel_id=1, source_target_pairs={{0,3},{1,0},{2,1},{3,2},{4,7},{5,4},{6,5},{7,6},{8,11},{9,8},{10,9... | collective-permute-start | bytes 1572872 | tf_op jit(solution)/shard_map/ppermute | solution.py:723
  768.4 17.6 %collective-permute-start.93 = (bf16[32,2048]{1,0:T(8,128)(2,1)S(1)}, bf16[32,2048]{1,0:T(8,128)(2,1)S(1)}, u32[]{:S(2)}, u32[]{:S(2)}) collective-permute-start(bf16[32,2048]{1,0:T(8,128)(2,1)S(1)} %get-tuple-element.344), channel_id=1, source_target_pairs={{0,1},{1,2},{2,3},{3,0},{4,5},{5,6},{6,7},{7,4},{8,9},{9,10},{10,1... | collective-permute-start | bytes 393224 | tf_op jit(solution)/shard_map/ppermute | solution.py:723
  768.5 17.5 %collective-permute-start.94 = (bf16[32,2048]{1,0:T(8,128)(2,1)S(1)}, bf16[32,2048]{1,0:T(8,128)(2,1)S(1)}, u32[]{:S(2)}, u32[]{:S(2)}) collective-permute-start(bf16[32,2048]{1,0:T(8,128)(2,1)S(1)} %get-tuple-element.346), channel_id=1, source_target_pairs={{0,2},{1,3},{2,0},{3,1},{4,6},{5,7},{6,4},{7,5},{8,10},{9,11},{10,... | collective-permute-start | bytes 393224 | tf_op jit(solution)/shard_map/ppermute | solution.py:723
  772.3 10.4 %collective-permute-start.91 = (bf16[32,2048]{1,0:T(8,128)(2,1)S(1)}, bf16[32,2048]{1,0:T(8,128)(2,1)S(1)}, u32[]{:S(2)}, u32[]{:S(2)}) collective-permute-start(bf16[32,2048]{1,0:T(8,128)(2,1)S(1)} %get-tuple-element.349), channel_id=1, source_target_pairs={{0,8},{1,9},{2,10},{3,11},{4,12},{5,13},{6,14},{7,15},{8,0},{9,1},... | collective-permute-start | bytes 393224 | tf_op jit(solution)/shard_map/ppermute | solution.py:723
  774.1 11.1 %collective-permute-start.92 = (bf16[32,2048]{1,0:T(8,128)(2,1)S(1)}, bf16[32,2048]{1,0:T(8,128)(2,1)S(1)}, u32[]{:S(2)}, u32[]{:S(2)}) collective-permute-start(bf16[32,2048]{1,0:T(8,128)(2,1)S(1)} %get-tuple-element.348), channel_id=1, source_target_pairs={{0,12},{1,13},{2,14},{3,15},{4,0},{5,1},{6,2},{7,3},{8,4},{9,5},{1... | collective-permute-start | bytes 393224 | tf_op jit(solution)/shard_map/ppermute | solution.py:723
  775.4 10.6 %collective-permute-start.95 = (bf16[32,2048]{1,0:T(8,128)(2,1)S(1)}, bf16[32,2048]{1,0:T(8,128)(2,1)S(1)}, u32[]{:S(2)}, u32[]{:S(2)}) collective-permute-start(bf16[32,2048]{1,0:T(8,128)(2,1)S(1)} %get-tuple-element.345), channel_id=1, source_target_pairs={{0,3},{1,0},{2,1},{3,2},{4,7},{5,4},{6,5},{7,6},{8,11},{9,8},{10,9... | collective-permute-start | bytes 393224 | tf_op jit(solution)/shard_map/ppermute | solution.py:723
  (77 other events, 598.2 us)
Sparse Core Ops, SparseCore 0:
  158.6 82.0 all-gather.2

commit v3 on v1

--- a/solution.py
+++ b/solution.py
@@ -94,11 +94,14 @@
     return square, bend, root
 
 
-def weight_views(refs):
-    first, up, down = refs
-    split = 3 * first.shape[0]
-    views = [first.at[:, pl.ds(0, split)], first.at[:, pl.ds(split, first.shape[1] - split)]]
-    return views + [up, down]
+def weight_views(ref):
+    width = ref.shape[0]
+    hidden = (ref.shape[1] - 4 * width) // 2
+    views, at = [], 0
+    for size in (3 * width, width, hidden, hidden):
+        views.append(ref.at[:, pl.ds(at, size)])
+        at += size
+    return views
 
 
 def fetch(pairs, own, sems):
@@ -131,10 +134,10 @@
     info_ref, cur_ref, nxt_ref = refs[:3]
     refs = refs[3:]
     skip_ref = refs.pop(0) if mode == "skip" else None
-    mine, other = weight_views(refs[:3]), weight_views(refs[3:6])
-    low_store, wide_store, z_ref = refs[8:11]
-    held = refs[11:15]
-    x_ref, qkv_ref, left_ref, y_ref, u_ref, sems, out_sems = refs[15:]
+    mine, other = weight_views(refs[0]), weight_views(refs[1])
+    low_store, wide_store, z_ref = refs[4:7]
+    held = refs[7:11]
+    x_ref, qkv_ref, left_ref, y_ref, u_ref, sems, out_sems = refs[11:]
     arrived = fetch(list(zip(mine, other, held)), info_ref[section, 1], sems)
     w_qkv, w_out, w_up, w_down = held
     low_base, wide_base = section % 2 * LOW_SLOTS, section % 2 * WIDE_SLOTS
@@ -217,10 +220,10 @@
         cur_ref, prv_ref = refs[:2]
         refs = refs[2:]
     skip_ref = refs.pop(0) if mode == "skip" else None
-    mine, other = weight_views(refs[:3]), weight_views(refs[3:6])
-    low_store, wide_store, gx_ref = refs[8:11]
-    held = refs[11:15]
-    x_ref, qkv_ref, right_ref, y_ref, u_ref, sems, in_sems, out_sem = refs[15:]
+    mine, other = weight_views(refs[0]), weight_views(refs[1])
+    low_store, wide_store, gx_ref = refs[4:7]
+    held = refs[7:11]
+    x_ref, qkv_ref, right_ref, y_ref, u_ref, sems, in_sems, out_sem = refs[11:]
     low_base, wide_base = section % 2 * LOW_SLOTS, section % 2 * WIDE_SLOTS
     in_copies = [
         pltpu.make_async_copy(store.at[pl.ds(at, room.shape[0])], room, in_sems.at[index])
@@ -330,11 +333,12 @@
 
 
 def pick_kernel(ranges, *refs):
-    store_ref = refs[1]
-    outs, sems = refs[2:-1], refs[-1]
+    core_ref, store_ref = refs[:2]
+    outs, sems = refs[3:-1], refs[-1]
     copies = []
-    for index, (at, count) in enumerate(ranges):
-        source = store_ref.at[pl.ds(at, count)]
+    for index, (at, count, given) in enumerate(ranges):
+        base = at + (1 - core_ref[0]) * LOW_SLOTS if given else at
+        source = store_ref.at[pl.ds(base, count)]
         copies.append(pltpu.make_async_copy(source, outs[index], sems.at[index]))
         copies[-1].start()
     for copy in copies:
@@ -343,9 +347,9 @@
 
 def weight_kernel(inner, *refs):
     info_ref, store_ref = refs[:2]
-    received = refs[2:6]
-    near_refs, far_refs = refs[6 : 6 + inner], refs[6 + inner : 6 + 2 * inner]
-    left, right, room, sems = refs[6 + 2 * inner :]
+    received = refs[2:4]
+    near_refs, far_refs = refs[4 : 4 + inner], refs[4 + inner : 4 + 2 * inner]
+    left, right, room, sems = refs[4 + 2 * inner :]
     copies = []
     for into, at, count, got in ((left, LEFT_AT, LEFT_SLOTS, 0), (right, RIGHT_AT, RIGHT_SLOTS, 1)):
         for index in range(count):
@@ -353,17 +357,12 @@
             for part in range(2):
                 goal = into.at[pl.ds(part * WIN, WIN), columns]
                 sem = sems.at[len(copies)]
-                for side in range(2):
-
-                    @pl.when(info_ref[0] == side)
-                    def _():
-                        if part == 0:
-                            source = store_ref.at[side * LOW_SLOTS + at + index]
-                        else:
-                            source = received[2 * got + side].at[index]
-                        pltpu.make_async_copy(source, goal, sem).start()
-
-                copies.append(pltpu.make_async_copy(store_ref.at[at + index], goal, sem))
+                if part == 0:
+                    source = store_ref.at[info_ref[0] * LOW_SLOTS + at + index]
+                else:
+                    source = received[got].at[index]
+                copies.append(pltpu.make_async_copy(source, goal, sem))
+                copies[-1].start()
     for copy in copies:
         copy.wait()
     width, step = room.shape
@@ -417,7 +416,7 @@
     core_index = section_index % 2
     micro_count, row_count, width = tokens.shape
     hidden = w_up.shape[2]
-    mine = (jnp.concatenate([w_qkv[0], w_out[0]], axis=1), w_up[0], w_down[0])
+    mine = jnp.concatenate([w_qkv[0], w_out[0], w_up[0], w_down[0]], axis=1)
 
     def place(section, tok):
         return section * tok_count + tok % tok_count
@@ -426,15 +425,16 @@
         return lax.ppermute(block, ("section", "tok"), route)
 
     def hop(block, low_pair, step, tok_shift):
+        middle = half_pairs - 1
         route = []
         for pair in range(pair_count - 1):
-            if pair % 2 == low_pair % 2:
+            if (pair > middle) - (pair < middle) == (low_pair > middle) - (low_pair < middle):
                 for core in range(2):
                     for tok in range(tok_count):
                         low, high = 2 * pair + core, 2 * pair + 2 + core
                         origin, goal = (low, high) if step > 0 else (high, low)
                         route.append((place(origin, tok + tok_shift), place(goal, tok)))
-        return moved(block, route)
+        return moved(block, sorted(route))
 
     def along(block, tok_shift, sections):
         route = []
@@ -453,28 +453,39 @@
                         route.append((place(origin, tok), place(2 * goal + core, tok)))
         return moved(block, sorted(route))
 
-    outer_pairs = [pair for pair in range(pair_count) if pair not in (half_pairs - 1, half_pairs)]
-
-    def swap(block, origins):
+    def swap(block):
         route = [
             (place(section, tok), place(section ^ 1, tok))
             for section in range(section_count)
-            if section % 2 in origins
             for tok in range(tok_count)
         ]
         return moved(block, route)
 
+    def inner_hops(block, pair, sign):
+        goal = pair_count - 1 - pair
+        return [
+            moved(
+                block,
+                sorted(
+                    (place(2 * pair + core, tok + sign * index), place(2 * goal + core, tok))
+                    for core in range(2)
+                    for tok in range(tok_count)
+                ),
+            )
+            for index in range(4)
+        ]
+
     everyone = range(section_count)
     last_encoder = section_count // 2 - 1
     encoders = range(last_encoder - 1)
-    inner_encoders = range(last_encoder - 1, last_encoder + 1)
-    inner_decoders = range(last_encoder + 1, last_encoder + 3)
     decoders = range(last_encoder + 3, section_count)
 
     def far_along(block, blocks, limit, sign, sections):
         bit = 1
         while bit <= limit:
-            shifted = along(block, sign * bit, sections)
+            inner = sections[:2] if sections[0] > 0 else sections[-2:]
+            taking = [one for one in sections if bit < tok_count // 2 or one not in inner]
+            shifted = along(block, sign * bit, taking)
             block = jnp.where((blocks // bit) % 2 == 1, shifted, block)
             bit *= 2
         return block
@@ -488,7 +499,7 @@
     shifts = (table - before + WIN) % WIN
     start = jnp.sum(jnp.where(order[:, None] >= order[None, :], shifts[None, :], 0), axis=1)
 
-    other = tuple(swap(weight, (0, 1)) for weight in mine)
+    other = swap(mine)
 
     info = jnp.stack(
         [
@@ -519,11 +530,11 @@
 
     def section_call(kernel, name, inputs, stores, rooms, sems):
         inputs = [info, *inputs]
-        first = len(inputs) + 6
+        first = len(inputs) + 2
         result = pl.pallas_call(
             kernel,
             out_shape=store_shapes + (rows_bf,),
-            in_specs=[SMEM] + [VMEM] * (len(inputs) - 1) + [HBM] * 8,
+            in_specs=[SMEM] + [VMEM] * (len(inputs) - 1) + [HBM] * 4,
             out_specs=(HBM, HBM, VMEM),
             input_output_aliases={first: 0, first + 1: 1},
             scratch_shapes=weight_rooms
@@ -532,7 +543,7 @@
             + [pltpu.SemaphoreType.DMA((count,)) for count in sems],
             compiler_params=params,
             name=name,
-        )(*inputs, *mine, *other, *stores)
+        )(*inputs, mine, other, *stores)
         return tuple(result[:2]), result[2]
 
     def forward(section, cur, nxt, skip, stores):
@@ -565,17 +576,19 @@
             (4, 2),
         )
 
+    core_scalar = core_index[None].astype(jnp.int32)
+
     def picked(stores, *ranges):
         result = pl.pallas_call(
             lambda *refs: pick_kernel(ranges, *refs),
             out_shape=(store_shapes[0],)
-            + tuple(jax.ShapeDtypeStruct((count, WIN, SLOT), BF16) for _, count in ranges),
-            in_specs=[HBM],
+            + tuple(jax.ShapeDtypeStruct((count, WIN, SLOT), BF16) for _, count, _ in ranges),
+            in_specs=[SMEM, HBM],
             out_specs=(HBM,) + (VMEM,) * len(ranges),
-            input_output_aliases={0: 0},
+            input_output_aliases={1: 0},
             scratch_shapes=[pltpu.SemaphoreType.DMA((len(ranges),))],
             name="pick",
-        )(stores[0])
+        )(core_scalar, stores[0])
         return (result[0], stores[1]), result[1:]
 
     def unwritten():
@@ -616,111 +629,105 @@
         near = far_along(blocks, counts, limit, sign, sections)
         return near, along(near, sign, sections)
 
-    def short_shift(block, count, limit, sign, sections):
-        blocks = [block]
-        for _ in range(limit + 1):
-            blocks.append(along(blocks[-1], sign, sections))
+    def near_and_beside(blocks, count):
         near, beside = blocks[0], blocks[1]
-        for index in range(1, limit + 1):
+        for index in range(1, len(blocks) - 1):
             near = jnp.where(count == index, blocks[index], near)
             beside = jnp.where(count == index, blocks[index + 1], beside)
         return near, beside
 
+    def outer_skips(stores, first, second, limit, sign, sections, with_aim):
+        stores, posts = picked(stores, (first, 1, False), (second, 1, False))
+        post = jnp.concatenate(posts, axis=0)
+        counts = [jnp.full((1, 1, width), each // WIN) for each in reaches_seen]
+        if with_aim:
+            post = jnp.concatenate([post, aim_here], axis=2)
+            extra = jnp.full((1, 1, channels), target_reach // WIN)
+            counts = [jnp.concatenate([count, extra], axis=2) for count in counts]
+        near, beside = long_shift(
+            mirror(post, outer_encoders if sign > 0 else outer_decoders),
+            jnp.concatenate(counts, axis=0),
+            limit,
+            sign,
+            sections,
+        )
+        rows = []
+        for slot in range(2):
+            here, there = near[slot, :, :width], beside[slot, :, :width]
+            left = reaches_seen[slot] % WIN
+            rows.append(cut(here, there, left) if sign > 0 else cut(there, here, WIN - left))
+        if with_aim:
+            aims = [
+                cut(near[slot, :, width:], beside[slot, :, width:], target_reach % WIN)
+                for slot in range(2)
+            ]
+            rows.append(jnp.concatenate(aims, axis=1))
+        return stores, rows
+
+    outer_encoders = range(half_pairs - 1)
+    outer_decoders = range(half_pairs + 1, pair_count)
     skips = {}
     aim = None
     for pair in range(pair_count):
         low, high = 2 * pair, 2 * pair + 1
         stores, z_low = forward(low, cur, nxt, skips.get(low), stores)
         nxt = along(z_low, 1, everyone)
+        if pair == half_pairs - 1:
+            inner = inner_hops(z_low, pair, 1)
         stores, z_high = forward(high, z_low, nxt, skips.get(high), stores)
+        if pair == half_pairs - 1:
+            z_high, *inner = together(z_high, *inner)
         if pair < pair_count - 1:
             nxt = hop(z_high, pair, 1, 1)
             cur = hop(z_high, pair, 1, 0)
+        if pair == half_pairs - 2:
+            stores, rows = outer_skips(
+                stores, Z_AT, LOW_SLOTS + Z_AT, tok_count - 1, 1, decoders, True
+            )
+            cur, nxt, *rows = together(cur, nxt, *rows)
+            aim = rows[2]
+            for goal in range(half_pairs + 1, pair_count):
+                skips[2 * goal + 1], skips[2 * goal] = rows[:2]
         if pair == half_pairs - 1:
             reach = start[low + 3] - start[low]
-            near, beside = short_shift(
-                mirror(z_low, (pair,)), reach // WIN, 2, 1, inner_decoders
-            )
+            near, beside = near_and_beside(inner, reach // WIN)
             skips[low + 3] = cut(near, beside, reach % WIN)
-            cur, nxt, skips[low + 3] = together(cur, nxt, skips[low + 3])
-            stores, posts = picked(stores, (Z_AT, 1), (LOW_SLOTS + Z_AT, 1))
-            post = jnp.concatenate([jnp.concatenate(posts, axis=0), aim_here], axis=2)
-            cur, nxt, post = together(cur, nxt, post)
-            counts = [
-                jnp.concatenate(
-                    [
-                        jnp.full((1, 1, width), each // WIN),
-                        jnp.full((1, 1, channels), target_reach // WIN),
-                    ],
-                    axis=2,
-                )
-                for each in reaches_seen
-            ]
-            near, beside = long_shift(
-                mirror(post, outer_pairs),
-                jnp.concatenate(counts, axis=0),
-                tok_count - 1,
-                1,
-                decoders,
-            )
-            outer_skip = [
-                cut(near[slot, :, :width], beside[slot, :, :width], reaches_seen[slot] % WIN)
-                for slot in range(2)
-            ]
-            aim = jnp.concatenate(
-                [
-                    cut(near[slot, :, width:], beside[slot, :, width:], target_reach % WIN)
-                    for slot in range(2)
-                ],
-                axis=1,
-            )
-            for goal in range(half_pairs + 1, pair_count):
-                skips[2 * goal + 1], skips[2 * goal] = outer_skip
 
     skips = {}
     sources = (z_high, aim, w_head)
     for pair in range(pair_count - 1, -1, -1):
         low, high = 2 * pair, 2 * pair + 1
         stores, gx_high = backward(high, sources, skips.get(high), stores)
-        sources = (gx_high, along(gx_high, -1, everyone))
+        prv = along(gx_high, -1, everyone)
+        if pair == half_pairs:
+            inner = inner_hops(gx_high, pair, -1)
+        sources = (gx_high, prv)
         stores, gx_low = backward(low, sources, skips.get(low), stores)
+        if pair == half_pairs:
+            gx_low, *inner = together(gx_low, *inner)
         if pair > 0:
             prv = hop(gx_low, pair - 1, -1, -1)
             cur = hop(gx_low, pair - 1, -1, 0)
             sources = (cur, prv)
+        if pair == half_pairs + 1:
+            stores, rows = outer_skips(
+                stores, LOW_SLOTS + GX_AT, GX_AT, tok_count - 2, -1, encoders, False
+            )
+            cur, prv, *rows = together(cur, prv, *rows)
+            sources = (cur, prv)
+            for goal in range(half_pairs - 1):
+                skips[2 * goal], skips[2 * goal + 1] = rows
         if pair == half_pairs:
             reach = start[high] - start[high - 3]
-            near, beside = short_shift(
-                mirror(gx_high, (pair,)), reach // WIN, 2, -1, inner_encoders
-            )
+            near, beside = near_and_beside(inner, reach // WIN)
             skips[high - 3] = cut(beside, near, WIN - reach % WIN)
-            cur, prv, skips[high - 3] = together(cur, prv, skips[high - 3])
-            stores, posts = picked(stores, (LOW_SLOTS + GX_AT, 1), (GX_AT, 1))
-            cur, prv, post = together(cur, prv, jnp.concatenate(posts, axis=0))
+        if pair == half_pairs - 1:
+            stores, given = picked(stores, (LEFT_AT, LEFT_SLOTS, True))
+            cur, prv, left_other = together(cur, prv, swap(given[0]))
             sources = (cur, prv)
-            counts = jnp.stack([each // WIN for each in reaches_seen])[:, None, None]
-            near, beside = long_shift(
-                mirror(post, outer_pairs), counts, tok_count - 2, -1, encoders
-            )
-            outer_skip = [
-                cut(beside[slot], near[slot], WIN - reaches_seen[slot] % WIN) for slot in range(2)
-            ]
-            for goal in range(half_pairs - 1):
-                skips[2 * goal], skips[2 * goal + 1] = outer_skip
-        if pair == half_pairs - 1:
-            stores, lefts = picked(
-                stores, (LEFT_AT, LEFT_SLOTS), (LOW_SLOTS + LEFT_AT, LEFT_SLOTS)
-            )
-            left_low = swap(lefts[0], (1,))
-            left_high = swap(lefts[1], (0,))
-            cur, prv, left_low, left_high = together(cur, prv, left_low, left_high)
-            sources = (cur, prv)
-
-    stores, rights = picked(
-        stores, (RIGHT_AT, RIGHT_SLOTS), (LOW_SLOTS + RIGHT_AT, RIGHT_SLOTS)
-    )
-    right_high = swap(rights[1], (0,))
-    right_low = swap(rights[0], (1,))
+
+    stores, given = picked(stores, (RIGHT_AT, RIGHT_SLOTS, True))
+    right_other = swap(given[0])
     total = 4 * width + 2 * hidden
     inner = 4
     outer = tok_count // inner
@@ -732,7 +739,7 @@
         lambda *refs: weight_kernel(inner, *refs),
         out_shape=[jax.ShapeDtypeStruct((outer, strip, split), BF16)] * inner
         + [jax.ShapeDtypeStruct((inner, strip, total - split), BF16)] * outer,
-        in_specs=[SMEM] + [HBM] * 5,
+        in_specs=[SMEM] + [HBM] * 3,
         out_specs=[VMEM] * (inner + outer),
         scratch_shapes=[
             pltpu.VMEM((2 * WIN, LEFT_SLOTS * SLOT), BF16),
@@ -745,10 +752,8 @@
     )(
         jnp.stack([core_index, tok_in, tok_out]).astype(jnp.int32),
         stores[0],
-        left_low,
-        left_high,
-        right_low,
-        right_high,
+        left_other,
+        right_other,
     )
     near_parts, far_parts = parts[:inner], parts[inner:]
 

time: 761 us -> 718 us (0.943)
  waiting for transfers between devices: 276 us -> 399 us
  starting transfers between devices: 274 us -> 185 us
  Pallas kernels: 134 us -> 70.4 us
  local copies, waits for them, and re-layouts: 27 us -> 7.02 us
    ppermute x72 -> x68, waiting for transfers between devices: 217 us -> 340 us  [moved(): return lax.ppermute(block, ('section', 'tok'), route)]
    ppermute x72 -> x68, starting transfers between devices: 245 us -> 158 us  [moved(): return lax.ppermute(block, ('section', 'tok'), route)]
    pallas_call x32, Pallas kernels: 118 us -> 55.9 us  [section_call(): pl.pallas_call(kernel, out_shape=store_shapes + (rows_bf,), in_specs=[SME...]
    unnamed x39 -> x23, local copies, waits for them, and re-layouts: 18.1 us -> 3.11 us
  transfers between devices with their start and end apart: 84 -> 80, of which waited for: 39 -> 40; matrix products, arithmetic and copies ran while one was open for 2% -> 1% of each run, Pallas kernels for 4% -> 0%
where the time goes in v3:
time: 718 us; the launch traced here: 708 us
  waiting for transfers between devices  399 us (56%)
  starting transfers between devices  185 us (26%)
  Pallas kernels  70.4 us (10%)
  blocking collectives  19.6 us (3%)
  other arithmetic  16.9 us (2%)
  between operations  9.75 us (1%)
    ppermute x68, waiting for transfers between devices, moved(): return lax.ppermute(block, ('section', 'tok'), route)  340 us
    ppermute x68, starting transfers between devices, moved(): return lax.ppermute(block, ('section', 'tok'), route)  158 us
    ppermute x12, waiting for transfers between devices, ring(): return lax.ppermute(block, 'tok', route)  59.4 us
    pallas_call x32, Pallas kernels, section_call(): pl.pallas_call(kernel, out_shape=store_shapes + (rows_bf,), in_specs=[SME...  55.9 us
    ppermute x12, starting transfers between devices, ring(): return lax.ppermute(block, 'tok', route)  26.8 us
    unnamed x1, blocking collectives  19.6 us
  transfers between devices with their start and end apart: 80, of which 40 were waited for; matrix products, arithmetic and copies ran while one was open for 1% of the time, Pallas kernels for 0%

profile of v3, /device:TPU:35, one launch (start us, length us, event | category | flops | bytes accessed | tf_op | source)
XLA Modules:
  0.0 707.9 jit_solution(16345906517802736983)
XLA Ops:
  0.6 6.5 pad_maximum_fusion.refs_3_.refs_4_
  10.8 19.6 %all-reduce.3 = s32[16]{0:T(128)S(1)} all-reduce(s32[16]{0:T(128)S(1)} %dynamic-update-slice), channel_id=2, replica_groups=mesh['section'=16,'tok'=16] {'section'}, use_global_device_ids=true, to_apply=%add.3 | all-reduce | flops 16 | bytes 128
  32.8 6.1 forward_plain.8
  39.2 3.6 collective-permute-done.2.refs_2_
  42.7 6.1 forward_plain.9
  59.7 16.3 %collective-permute-start.6 = (bf16[128,512]{1,0:T(8,128)(2,1)S(1)}, bf16[128,512]{1,0:T(8,128)(2,1)S(1)}, u32[]{:S(2)}, u32[]{:S(2)}) collective-permute-start(bf16[128,512]{1,0:T(8,128)(2,1)S(1)} %get-tuple-element.153), channel_id=1, source_target_pairs={{0,32},{1,33},{2,34},{3,35},{4,36},{5,37},{6,38},{7,39},{8,40},{9,... | collective-permute-start | bytes 393224 | tf_op jit(solution)/shard_map/ppermute | solution.py:425
  81.3 4.1 collective-permute-start.8
  93.3 7.4 %collective-permute-done.11 = bf16[2,128,640]{2,1,0:T(8,128)(2,1)S(1)} collective-permute-done((bf16[2,128,640]{2,1,0:T(8,128)(2,1)S(1)}, bf16[2,128,640]{2,1,0:T(8,128)(2,1)S(1)}, u32[]{:S(2)}, u32[]{:S(2)}) %collective-permute-start.11) | collective-permute-done | bytes 327712 | tf_op jit(solution)/shard_map/ppermute | solution.py:425
  109.7 7.1 %collective-permute-start.10 = (bf16[128,512]{1,0:T(8,128)(2,1)S(1)}, bf16[128,512]{1,0:T(8,128)(2,1)S(1)}, u32[]{:S(2)}, u32[]{:S(2)}) collective-permute-start(bf16[128,512]{1,0:T(8,128)(2,1)S(1)} %get-tuple-element.159), channel_id=1, source_target_pairs={{0,47},{1,32},{2,33},{3,34},{4,35},{5,36},{6,37},{7,38},{8,39},{9,... | collective-permute-start | bytes 393224 | tf_op jit(solution)/shard_map/ppermute | solution.py:425
  116.9 7.6 %collective-permute-start.9 = (bf16[128,512]{1,0:T(8,128)(2,1)S(1)}, bf16[128,512]{1,0:T(8,128)(2,1)S(1)}, u32[]{:S(2)}, u32[]{:S(2)}) collective-permute-start(bf16[128,512]{1,0:T(8,128)(2,1)S(1)} %get-tuple-element.159), channel_id=1, source_target_pairs={{0,32},{1,33},{2,34},{3,35},{4,36},{5,37},{6,38},{7,39},{8,40},{9,... | collective-permute-start | bytes 393224 | tf_op jit(solution)/shard_map/ppermute | solution.py:425
  149.8 4.0 collective-permute-start.30
  167.8 3.6 collective-permute-start.34
  176.5 3.6 collective-permute-start.37
  188.7 3.8 collective-permute-done.40.refs_2_
  197.7 164.5 %collective-permute-done.43 = bf16[2,128,512]{2,1,0:T(8,128)(2,1)S(1)} collective-permute-done((bf16[2,128,512]{2,1,0:T(8,128)(2,1)S(1)}, bf16[2,128,512]{2,1,0:T(8,128)(2,1)S(1)}, u32[]{:S(2)}, u32[]{:S(2)}) %collective-permute-start.43) | collective-permute-done | bytes 262176 | tf_op jit(solution)/shard_map/ppermute | solution.py:425
  362.1 4.9 collective-permute-start.44
  367.1 4.6 collective-permute-done.44
  371.7 6.8 collective-permute-start.45
  378.6 4.6 collective-permute-done.45
  385.8 17.2 %collective-permute-done.46 = bf16[2,128,512]{2,1,0:T(8,128)(2,1)S(1)} collective-permute-done((bf16[2,128,512]{2,1,0:T(8,128)(2,1)S(1)}, bf16[2,128,512]{2,1,0:T(8,128)(2,1)S(1)}, u32[]{:S(2)}, u32[]{:S(2)}) %collective-permute-start.46) | collective-permute-done | bytes 262176 | tf_op jit(solution)/shard_map/ppermute | solution.py:425
  403.0 3.5 collective-permute-start.47
  406.6 8.1 %collective-permute-done.47 = bf16[2,128,512]{2,1,0:T(8,128)(2,1)S(1)} collective-permute-done((bf16[2,128,512]{2,1,0:T(8,128)(2,1)S(1)}, bf16[2,128,512]{2,1,0:T(8,128)(2,1)S(1)}, u32[]{:S(2)}, u32[]{:S(2)}) %collective-permute-start.47) | collective-permute-done | bytes 262176 | tf_op jit(solution)/shard_map/ppermute | solution.py:425
  414.7 3.4 collective-permute-start.48
  419.5 8.8 %collective-permute-done.48 = bf16[2,128,512]{2,1,0:T(8,128)(2,1)S(1)} collective-permute-done((bf16[2,128,512]{2,1,0:T(8,128)(2,1)S(1)}, bf16[2,128,512]{2,1,0:T(8,128)(2,1)S(1)}, u32[]{:S(2)}, u32[]{:S(2)}) %collective-permute-start.48) | collective-permute-done | bytes 262176 | tf_op jit(solution)/shard_map/ppermute | solution.py:425
  432.3 4.2 collective-permute-done.49.refs_2_
  440.0 7.9 %collective-permute-done.56.refs_2_ = bf16[128,512]{1,0:T(8,128)(2,1)S(1)} collective-permute-done((bf16[128,512]{1,0:T(8,128)(2,1)S(1)}, bf16[128,512]{1,0:T(8,128)(2,1)S(1)}, u32[]{:S(2)}, u32[]{:S(2)}) %collective-permute-start.56) | collective-permute-done | bytes 131104 | tf_op jit(solution)/shard_map/ppermute | solution.py:425
  451.0 38.5 %collective-permute-start.59 = (bf16[7,128,512]{2,1,0:T(8,128)(2,1)}, bf16[7,128,512]{2,1,0:T(8,128)(2,1)S(1)}, u32[]{:S(2)}, u32[]{:S(2)}) collective-permute-start(bf16[7,128,512]{2,1,0:T(8,128)(2,1)} %get-tuple-element.244), channel_id=1, source_target_pairs={{0,16},{1,17},{2,18},{3,19},{4,20},{5,21},{6,22},{7,23},{8,24},{9,... | collective-permute-start | bytes 2752520 | tf_op jit(solution)/shard_map/ppermute | solution.py:425
  492.1 4.4 collective-permute-done.57.refs_1_
  496.5 5.5 collective-permute-done.58.refs_2_
  502.9 5.7 collective-permute-done.60.refs_2_
  515.5 4.9 collective-permute-done.62.refs_2_
  521.2 5.0 collective-permute-done.63.refs_2_
  529.8 38.4 %collective-permute-done.64.refs_1_ = bf16[128,512]{1,0:T(8,128)(2,1)S(1)} collective-permute-done((bf16[128,512]{1,0:T(8,128)(2,1)S(1)}, bf16[128,512]{1,0:T(8,128)(2,1)S(1)}, u32[]{:S(2)}, u32[]{:S(2)}) %collective-permute-start.64) | collective-permute-done | bytes 131104 | tf_op jit(solution)/shard_map/ppermute | solution.py:425
  568.2 5.2 collective-permute-done.65.refs_2_
  573.4 9.5 %backward_skip.12 = (bf16[224,128,512]{2,1,0:T(8,128)(2,1)}, f32[112,128,512]{2,1,0:T(8,128)}, bf16[128,512]{1,0:T(8,128)(2,1)S(1)}) custom-call(s32[16,4]{1,0:T(8,128)S(1)} %copy.149.refs_0_, bf16[128,512]{1,0:T(8,128)(2,1)S(1)} %collective-permute-done.64.refs_1_, ...), custom_call_target="tpu_custom_call", output_to_operand_aliasing={{0}: (6, {}), {1}: (7, {})} | custom-call | tf_op jit(solution)/shard_map/backward_skip/pallas_call | solution.py:534
  583.0 3.8 collective-permute-done.66.refs_2_
  586.8 9.9 %backward_skip.13 = (bf16[224,128,512]{2,1,0:T(8,128)(2,1)}, f32[112,128,512]{2,1,0:T(8,128)}, bf16[128,512]{1,0:T(8,128)(2,1)}) custom-call(s32[16,4]{1,0:T(8,128)S(1)} %copy.149.refs_0_, bf16[128,512]{1,0:T(8,128)(2,1)S(1)} %get-tuple-element.263.refs_1_, ...), custom_call_target="tpu_custom_call", output_to_operand_aliasing={{0}: (6, {}), {1}: (7, {})} | custom-call | tf_op jit(solution)/shard_map/backward_skip/pallas_call | solution.py:534
  599.1 4.7 collective-permute-start.67
  607.5 6.6 weight_grads.1
  614.4 3.7 collective-permute-start.69
  618.0 9.6 %collective-permute-start.72 = (bf16[4,32,2048]{2,1,0:T(8,128)(2,1)}, bf16[4,32,2048]{2,1,0:T(8,128)(2,1)S(1)}, u32[]{:S(2)}, u32[]{:S(2)}) collective-permute-start(bf16[4,32,2048]{2,1,0:T(8,128)(2,1)} %get-tuple-element.276), channel_id=1, source_target_pairs={{0,8},{1,9},{2,10},{3,11},{4,12},{5,13},{6,14},{7,15},{8,0},{9,1},... | collective-permute-start | bytes 1572872 | tf_op jit(solution)/shard_map/ppermute | solution.py:769
  627.6 4.6 collective-permute-done.71
  635.1 25.4 %collective-permute-done.72 = bf16[4,32,2048]{2,1,0:T(8,128)(2,1)S(1)} collective-permute-done((bf16[4,32,2048]{2,1,0:T(8,128)(2,1)}, bf16[4,32,2048]{2,1,0:T(8,128)(2,1)S(1)}, u32[]{:S(2)}, u32[]{:S(2)}) %collective-permute-start.72) | collective-permute-done | bytes 524320 | tf_op jit(solution)/shard_map/ppermute | solution.py:769
  660.4 8.0 %collective-permute-done.73 = bf16[4,32,2048]{2,1,0:T(8,128)(2,1)} collective-permute-done((bf16[4,32,2048]{2,1,0:T(8,128)(2,1)S(1)}, bf16[4,32,2048]{2,1,0:T(8,128)(2,1)}, u32[]{:S(2)}, u32[]{:S(2)}) %collective-permute-start.73) | collective-permute-done | bytes 524320 | tf_op jit(solution)/shard_map/ppermute | solution.py:769
  672.7 5.5 collective-permute-start.78
  678.3 3.3 collective-permute-start.75
  685.2 14.8 %collective-permute-done.75 = bf16[32,4096]{1,0:T(8,128)(2,1)S(1)} collective-permute-done((bf16[32,4096]{1,0:T(8,128)(2,1)S(1)}, bf16[32,4096]{1,0:T(8,128)(2,1)S(1)}, u32[]{:S(2)}, u32[]{:S(2)}) %collective-permute-start.75) | collective-permute-done | bytes 262176 | tf_op jit(solution)/shard_map/ppermute | solution.py:769
  700.0 5.2 collective-permute-done.76
  (236 shorter events, 138.0 us)
Async XLA Ops:
  7.1 25.6 %collective-permute-start.1 = (bf16[512,6144]{1,0:T(8,128)(2,1)}, bf16[512,6144]{1,0:T(8,128)(2,1)}, u32[]{:S(2)}, u32[]{:S(2)}) collective-permute-start(bf16[512,6144]{1,0:T(8,128)(2,1)} %pad_maximum_fusion.refs_3_.refs_4_), channel_id=1, source_target_pairs={{0,16},{1,17},{2,18},{3,19},{4,20},{5,21},{6,22},{7,23},{8,24},{9,... | collective-permute-start | bytes 18874376 | tf_op jit(solution)/shard_map/ppermute | solution.py:425
  7.8 24.9 %collective-permute-start = (bf16[128,512]{1,0:T(8,128)(2,1)S(1)}, bf16[128,512]{1,0:T(8,128)(2,1)S(1)}, u32[]{:S(2)}, u32[]{:S(2)}) collective-permute-start(bf16[128,512]{1,0:T(8,128)(2,1)S(1)} %dynamic-slice_bitcast_fusion.6.refs_1_), channel_id=1, source_target_pairs={{1,0},{2,1},{3,2},{4,3},{5,4},{6,5},{7,6},{8,7},{9,8},{10,9},{11,1... | collective-permute-start | bytes 393224 | tf_op jit(solution)/shard_map/ppermute | solution.py:425
  59.7 19.1 %collective-permute-start.6 = (bf16[128,512]{1,0:T(8,128)(2,1)S(1)}, bf16[128,512]{1,0:T(8,128)(2,1)S(1)}, u32[]{:S(2)}, u32[]{:S(2)}) collective-permute-start(bf16[128,512]{1,0:T(8,128)(2,1)S(1)} %get-tuple-element.153), channel_id=1, source_target_pairs={{0,32},{1,33},{2,34},{3,35},{4,36},{5,37},{6,38},{7,39},{8,40},{9,... | collective-permute-start | bytes 393224 | tf_op jit(solution)/shard_map/ppermute | solution.py:425
  81.3 7.1 collective-permute-start.8
  91.9 8.8 %collective-permute-start.11 = (bf16[2,128,640]{2,1,0:T(8,128)(2,1)S(1)}, bf16[2,128,640]{2,1,0:T(8,128)(2,1)S(1)}, u32[]{:S(2)}, u32[]{:S(2)}) collective-permute-start(bf16[2,128,640]{2,1,0:T(8,128)(2,1)S(1)} %maximum_maximum_fusion), channel_id=1, source_target_pairs={{0,224},{1,225},{2,226},{3,227},{4,228},{5,229},{6,230},{7,231},{8... | collective-permute-start | bytes 983048 | tf_op jit(solution)/shard_map/ppermute | solution.py:425
  100.7 6.7 collective-permute-start.12
  109.0 15.5 %collective-permute-start.15 = (bf16[2,128,640]{2,1,0:T(8,128)(2,1)S(1)}, bf16[2,128,640]{2,1,0:T(8,128)(2,1)S(1)}, u32[]{:S(2)}, u32[]{:S(2)}) collective-permute-start(bf16[2,128,640]{2,1,0:T(8,128)(2,1)S(1)} %broadcast_select_fusion.2), channel_id=1, source_target_pairs={{200,192},{201,193},{202,194},{203,195},{204,196},{205,197},{206,1... | collective-permute-start | bytes 983048 | tf_op jit(solution)/shard_map/ppermute | solution.py:425
  109.7 16.2 %collective-permute-start.10 = (bf16[128,512]{1,0:T(8,128)(2,1)S(1)}, bf16[128,512]{1,0:T(8,128)(2,1)S(1)}, u32[]{:S(2)}, u32[]{:S(2)}) collective-permute-start(bf16[128,512]{1,0:T(8,128)(2,1)S(1)} %get-tuple-element.159), channel_id=1, source_target_pairs={{0,47},{1,32},{2,33},{3,34},{4,35},{5,36},{6,37},{7,38},{8,39},{9,... | collective-permute-start | bytes 393224 | tf_op jit(solution)/shard_map/ppermute | solution.py:425
  116.9 9.5 %collective-permute-start.9 = (bf16[128,512]{1,0:T(8,128)(2,1)S(1)}, bf16[128,512]{1,0:T(8,128)(2,1)S(1)}, u32[]{:S(2)}, u32[]{:S(2)}) collective-permute-start(bf16[128,512]{1,0:T(8,128)(2,1)S(1)} %get-tuple-element.159), channel_id=1, source_target_pairs={{0,32},{1,33},{2,34},{3,35},{4,36},{5,37},{6,38},{7,39},{8,40},{9,... | collective-permute-start | bytes 393224 | tf_op jit(solution)/shard_map/ppermute | solution.py:425
  149.8 7.2 %collective-permute-start.30 = (bf16[128,512]{1,0:T(8,128)(2,1)S(1)}, bf16[128,512]{1,0:T(8,128)(2,1)S(1)}, u32[]{:S(2)}, u32[]{:S(2)}) collective-permute-start(bf16[128,512]{1,0:T(8,128)(2,1)S(1)} %get-tuple-element.192.refs_1_), channel_id=1, source_target_pairs={{1,0},{2,1},{3,2},{4,3},{5,4},{6,5},{7,6},{8,7},{9,8},{10,9},{11,1... | collective-permute-start | bytes 393224 | tf_op jit(solution)/shard_map/ppermute | solution.py:425
  159.9 6.0 collective-permute-start.33
  176.5 6.1 collective-permute-start.37
  185.7 6.8 collective-permute-start.40
  196.4 165.8 %collective-permute-start.43 = (bf16[2,128,512]{2,1,0:T(8,128)(2,1)S(1)}, bf16[2,128,512]{2,1,0:T(8,128)(2,1)S(1)}, u32[]{:S(2)}, u32[]{:S(2)}) collective-permute-start(bf16[2,128,512]{2,1,0:T(8,128)(2,1)S(1)} %pad_maximum_fusion.1), channel_id=1, source_target_pairs={{160,64},{161,65},{162,66},{163,67},{164,68},{165,69},{166,70},{16... | collective-permute-start | bytes 786440 | tf_op jit(solution)/shard_map/ppermute | solution.py:425
  362.1 9.6 %collective-permute-start.44 = (bf16[2,128,512]{2,1,0:T(8,128)(2,1)S(1)}, bf16[2,128,512]{2,1,0:T(8,128)(2,1)S(1)}, u32[]{:S(2)}, u32[]{:S(2)}) collective-permute-start(bf16[2,128,512]{2,1,0:T(8,128)(2,1)S(1)} %collective-permute-done.43), channel_id=1, source_target_pairs={{15,0},{0,1},{1,2},{2,3},{3,4},{4,5},{5,6},{6,7},{7,8},{8,9},{9,10... | collective-permute-start | bytes 786440 | tf_op jit(solution)/shard_map/ppermute | solution.py:425
  371.7 11.4 %collective-permute-start.45 = (bf16[2,128,512]{2,1,0:T(8,128)(2,1)S(1)}, bf16[2,128,512]{2,1,0:T(8,128)(2,1)S(1)}, u32[]{:S(2)}, u32[]{:S(2)}) collective-permute-start(bf16[2,128,512]{2,1,0:T(8,128)(2,1)S(1)} %broadcast_select_fusion.4), channel_id=1, source_target_pairs={{14,0},{15,1},{0,2},{1,3},{2,4},{3,5},{4,6},{5,7},{6,8},{7,9},{8,1... | collective-permute-start | bytes 786440 | tf_op jit(solution)/shard_map/ppermute | solution.py:425
  383.2 19.8 %collective-permute-start.46 = (bf16[2,128,512]{2,1,0:T(8,128)(2,1)S(1)}, bf16[2,128,512]{2,1,0:T(8,128)(2,1)S(1)}, u32[]{:S(2)}, u32[]{:S(2)}) collective-permute-start(bf16[2,128,512]{2,1,0:T(8,128)(2,1)S(1)} %broadcast_select_fusion.5), channel_id=1, source_target_pairs={{12,0},{13,1},{14,2},{15,3},{0,4},{1,5},{2,6},{3,7},{4,8},{5,9},{6... | collective-permute-start | bytes 786440 | tf_op jit(solution)/shard_map/ppermute | solution.py:425
  403.0 11.7 %collective-permute-start.47 = (bf16[2,128,512]{2,1,0:T(8,128)(2,1)S(1)}, bf16[2,128,512]{2,1,0:T(8,128)(2,1)S(1)}, u32[]{:S(2)}, u32[]{:S(2)}) collective-permute-start(bf16[2,128,512]{2,1,0:T(8,128)(2,1)S(1)} %broadcast_select_fusion.6), channel_id=1, source_target_pairs={{8,0},{9,1},{10,2},{11,3},{12,4},{13,5},{14,6},{15,7},{0,8},{1,9},... | collective-permute-start | bytes 786440 | tf_op jit(solution)/shard_map/ppermute | solution.py:425
  414.7 13.6 %collective-permute-start.48 = (bf16[2,128,512]{2,1,0:T(8,128)(2,1)S(1)}, bf16[2,128,512]{2,1,0:T(8,128)(2,1)S(1)}, u32[]{:S(2)}, u32[]{:S(2)}) collective-permute-start(bf16[2,128,512]{2,1,0:T(8,128)(2,1)S(1)} %broadcast_select_fusion.7), channel_id=1, source_target_pairs={{15,0},{0,1},{1,2},{2,3},{3,4},{4,5},{5,6},{6,7},{7,8},{8,9},{9,10... | collective-permute-start | bytes 786440 | tf_op jit(solution)/shard_map/ppermute | solution.py:425
  418.1 10.6 %collective-permute-start.41 = (bf16[128,512]{1,0:T(8,128)(2,1)S(1)}, bf16[128,512]{1,0:T(8,128)(2,1)S(1)}, u32[]{:S(2)}, u32[]{:S(2)}) collective-permute-start(bf16[128,512]{1,0:T(8,128)(2,1)S(1)} %get-tuple-element.220), channel_id=1, source_target_pairs={{160,128},{161,129},{162,130},{163,131},{164,132},{165,133},{166,1... | collective-permute-start | bytes 393224 | tf_op jit(solution)/shard_map/ppermute | solution.py:425
  418.8 9.9 %collective-permute-start.42 = (bf16[128,512]{1,0:T(8,128)(2,1)S(1)}, bf16[128,512]{1,0:T(8,128)(2,1)S(1)}, u32[]{:S(2)}, u32[]{:S(2)}) collective-permute-start(bf16[128,512]{1,0:T(8,128)(2,1)S(1)} %get-tuple-element.220), channel_id=1, source_target_pairs={{160,129},{161,130},{162,131},{163,132},{164,133},{165,134},{166,1... | collective-permute-start | bytes 393224 | tf_op jit(solution)/shard_map/ppermute | solution.py:425
  429.5 7.0 collective-permute-start.49
  429.6 7.9 %collective-permute-start.50 = (bf16[128,512]{1,0:T(8,128)(2,1)S(1)}, bf16[128,512]{1,0:T(8,128)(2,1)S(1)}, u32[]{:S(2)}, u32[]{:S(2)}) collective-permute-start(bf16[128,512]{1,0:T(8,128)(2,1)S(1)} %get-tuple-element.228.refs_1_), channel_id=1, source_target_pairs={{128,96},{129,97},{130,98},{131,99},{132,100},{133,101},{134,102},... | collective-permute-start | bytes 393224 | tf_op jit(solution)/shard_map/ppermute | solution.py:425
  430.3 7.2 %collective-permute-start.51 = (bf16[128,512]{1,0:T(8,128)(2,1)S(1)}, bf16[128,512]{1,0:T(8,128)(2,1)S(1)}, u32[]{:S(2)}, u32[]{:S(2)}) collective-permute-start(bf16[128,512]{1,0:T(8,128)(2,1)S(1)} %get-tuple-element.228.refs_1_), channel_id=1, source_target_pairs={{128,97},{129,98},{130,99},{131,100},{132,101},{133,102},{134,103}... | collective-permute-start | bytes 393224 | tf_op jit(solution)/shard_map/ppermute | solution.py:425
  431.0 6.5 collective-permute-start.52
  431.6 5.9 collective-permute-start.53
  439.7 8.2 %collective-permute-start.56 = (bf16[128,512]{1,0:T(8,128)(2,1)S(1)}, bf16[128,512]{1,0:T(8,128)(2,1)S(1)}, u32[]{:S(2)}, u32[]{:S(2)}) collective-permute-start(bf16[128,512]{1,0:T(8,128)(2,1)S(1)} %get-tuple-element.235.refs_1_), channel_id=1, source_target_pairs={{15,0},{0,1},{1,2},{2,3},{3,4},{4,5},{5,6},{6,7},{7,8},{8,9},{9,10... | collective-permute-start | bytes 393224 | tf_op jit(solution)/shard_map/ppermute | solution.py:425
  451.0 51.0 %collective-permute-start.59 = (bf16[7,128,512]{2,1,0:T(8,128)(2,1)}, bf16[7,128,512]{2,1,0:T(8,128)(2,1)S(1)}, u32[]{:S(2)}, u32[]{:S(2)}) collective-permute-start(bf16[7,128,512]{2,1,0:T(8,128)(2,1)} %get-tuple-element.244), channel_id=1, source_target_pairs={{0,16},{1,17},{2,18},{3,19},{4,20},{5,21},{6,22},{7,23},{8,24},{9,... | collective-permute-start | bytes 2752520 | tf_op jit(solution)/shard_map/ppermute | solution.py:425
  489.5 7.0 collective-permute-start.57
  490.8 11.2 %collective-permute-start.58 = (bf16[128,512]{1,0:T(8,128)(2,1)S(1)}, bf16[128,512]{1,0:T(8,128)(2,1)S(1)}, u32[]{:S(2)}, u32[]{:S(2)}) collective-permute-start(bf16[128,512]{1,0:T(8,128)(2,1)S(1)} %get-tuple-element.242), channel_id=1, source_target_pairs={{32,1},{33,2},{34,3},{35,4},{36,5},{37,6},{38,7},{39,8},{40,9},{41... | collective-permute-start | bytes 393224 | tf_op jit(solution)/shard_map/ppermute | solution.py:425
  502.8 5.8 collective-permute-start.60
  509.8 5.7 collective-permute-start.61
  511.1 9.3 %collective-permute-start.62 = (bf16[128,512]{1,0:T(8,128)(2,1)S(1)}, bf16[128,512]{1,0:T(8,128)(2,1)S(1)}, u32[]{:S(2)}, u32[]{:S(2)}) collective-permute-start(bf16[128,512]{1,0:T(8,128)(2,1)S(1)} %get-tuple-element.254), channel_id=1, source_target_pairs={{32,1},{33,2},{34,3},{35,4},{36,5},{37,6},{38,7},{39,8},{40,9},{41... | collective-permute-start | bytes 393224 | tf_op jit(solution)/shard_map/ppermute | solution.py:425
  527.2 41.0 %collective-permute-start.64 = (bf16[128,512]{1,0:T(8,128)(2,1)S(1)}, bf16[128,512]{1,0:T(8,128)(2,1)S(1)}, u32[]{:S(2)}, u32[]{:S(2)}) collective-permute-start(bf16[128,512]{1,0:T(8,128)(2,1)S(1)} %get-tuple-element.260), channel_id=1, source_target_pairs={{32,0},{33,1},{34,2},{35,3},{36,4},{37,5},{38,6},{39,7},{40,8},{41... | collective-permute-start | bytes 393224 | tf_op jit(solution)/shard_map/ppermute | solution.py:425
  528.5 44.9 %collective-permute-start.65 = (bf16[128,512]{1,0:T(8,128)(2,1)S(1)}, bf16[128,512]{1,0:T(8,128)(2,1)S(1)}, u32[]{:S(2)}, u32[]{:S(2)}) collective-permute-start(bf16[128,512]{1,0:T(8,128)(2,1)S(1)} %get-tuple-element.260), channel_id=1, source_target_pairs={{32,1},{33,2},{34,3},{35,4},{36,5},{37,6},{38,7},{39,8},{40,9},{41... | collective-permute-start | bytes 393224 | tf_op jit(solution)/shard_map/ppermute | solution.py:425
  599.1 7.4 %collective-permute-start.67 = (bf16[9,128,512]{2,1,0:T(8,128)(2,1)}, bf16[9,128,512]{2,1,0:T(8,128)(2,1)S(1)}, u32[]{:S(2)}, u32[]{:S(2)}) collective-permute-start(bf16[9,128,512]{2,1,0:T(8,128)(2,1)} %get-tuple-element.269), channel_id=1, source_target_pairs={{0,16},{1,17},{2,18},{3,19},{4,20},{5,21},{6,22},{7,23},{8,24},{9,... | collective-permute-start | bytes 3538952 | tf_op jit(solution)/shard_map/ppermute | solution.py:425
  614.2 18.0 %collective-permute-start.71 = (bf16[4,32,2048]{2,1,0:T(8,128)(2,1)S(1)}, bf16[4,32,2048]{2,1,0:T(8,128)(2,1)S(1)}, u32[]{:S(2)}, u32[]{:S(2)}) collective-permute-start(bf16[4,32,2048]{2,1,0:T(8,128)(2,1)S(1)} %get-tuple-element.275), channel_id=1, source_target_pairs={{0,4},{1,5},{2,6},{3,7},{4,8},{5,9},{6,10},{7,11},{8,12},{9,13},{1... | collective-permute-start | bytes 1572872 | tf_op jit(solution)/shard_map/ppermute | solution.py:769
  614.3 55.5 %collective-permute-start.68 = (bf16[4,32,4096]{2,1,0:T(8,128)(2,1)}, bf16[4,32,4096]{2,1,0:T(8,128)(2,1)}, u32[]{:S(2)}, u32[]{:S(2)}) collective-permute-start(bf16[4,32,4096]{2,1,0:T(8,128)(2,1)} %get-tuple-element.271), channel_id=1, source_target_pairs={{0,1},{1,2},{2,3},{3,0},{4,5},{5,6},{6,7},{7,4},{8,9},{9,10},{10,1... | collective-permute-start | bytes 3145736 | tf_op jit(solution)/shard_map/ppermute | solution.py:769
  614.4 55.4 %collective-permute-start.69 = (bf16[4,32,4096]{2,1,0:T(8,128)(2,1)}, bf16[4,32,4096]{2,1,0:T(8,128)(2,1)}, u32[]{:S(2)}, u32[]{:S(2)}) collective-permute-start(bf16[4,32,4096]{2,1,0:T(8,128)(2,1)} %get-tuple-element.272), channel_id=1, source_target_pairs={{0,2},{1,3},{2,0},{3,1},{4,6},{5,7},{6,4},{7,5},{8,10},{9,11},{10,... | collective-permute-start | bytes 3145736 | tf_op jit(solution)/shard_map/ppermute | solution.py:769
  618.0 51.8 %collective-permute-start.70 = (bf16[4,32,4096]{2,1,0:T(8,128)(2,1)}, bf16[4,32,4096]{2,1,0:T(8,128)(2,1)}, u32[]{:S(2)}, u32[]{:S(2)}) collective-permute-start(bf16[4,32,4096]{2,1,0:T(8,128)(2,1)} %get-tuple-element.273), channel_id=1, source_target_pairs={{0,3},{1,0},{2,1},{3,2},{4,7},{5,4},{6,5},{7,6},{8,11},{9,8},{10,9... | collective-permute-start | bytes 3145736 | tf_op jit(solution)/shard_map/ppermute | solution.py:769
  618.0 42.4 %collective-permute-start.72 = (bf16[4,32,2048]{2,1,0:T(8,128)(2,1)}, bf16[4,32,2048]{2,1,0:T(8,128)(2,1)S(1)}, u32[]{:S(2)}, u32[]{:S(2)}) collective-permute-start(bf16[4,32,2048]{2,1,0:T(8,128)(2,1)} %get-tuple-element.276), channel_id=1, source_target_pairs={{0,8},{1,9},{2,10},{3,11},{4,12},{5,13},{6,14},{7,15},{8,0},{9,1},... | collective-permute-start | bytes 1572872 | tf_op jit(solution)/shard_map/ppermute | solution.py:769
  632.2 36.2 %collective-permute-start.73 = (bf16[4,32,2048]{2,1,0:T(8,128)(2,1)S(1)}, bf16[4,32,2048]{2,1,0:T(8,128)(2,1)}, u32[]{:S(2)}, u32[]{:S(2)}) collective-permute-start(bf16[4,32,2048]{2,1,0:T(8,128)(2,1)S(1)} %get-tuple-element.277), channel_id=1, source_target_pairs={{0,12},{1,13},{2,14},{3,15},{4,0},{5,1},{6,2},{7,3},{8,4},{9,5},{1... | collective-permute-start | bytes 1572872 | tf_op jit(solution)/shard_map/ppermute | solution.py:769
  672.4 9.2 %collective-permute-start.77 = (bf16[32,2048]{1,0:T(8,128)(2,1)S(1)}, bf16[32,2048]{1,0:T(8,128)(2,1)S(1)}, u32[]{:S(2)}, u32[]{:S(2)}) collective-permute-start(bf16[32,2048]{1,0:T(8,128)(2,1)S(1)} %get-tuple-element.283), channel_id=1, source_target_pairs={{0,1},{1,2},{2,3},{3,0},{4,5},{5,6},{6,7},{7,4},{8,9},{9,10},{10,1... | collective-permute-start | bytes 393224 | tf_op jit(solution)/shard_map/ppermute | solution.py:769
  672.7 10.2 %collective-permute-start.78 = (bf16[32,2048]{1,0:T(8,128)(2,1)S(1)}, bf16[32,2048]{1,0:T(8,128)(2,1)S(1)}, u32[]{:S(2)}, u32[]{:S(2)}) collective-permute-start(bf16[32,2048]{1,0:T(8,128)(2,1)S(1)} %get-tuple-element.285), channel_id=1, source_target_pairs={{0,2},{1,3},{2,0},{3,1},{4,6},{5,7},{6,4},{7,5},{8,10},{9,11},{10,... | collective-permute-start | bytes 393224 | tf_op jit(solution)/shard_map/ppermute | solution.py:769
  678.2 6.2 collective-permute-start.79
  678.2 7.0 collective-permute-start.74
  678.3 21.7 %collective-permute-start.75 = (bf16[32,4096]{1,0:T(8,128)(2,1)S(1)}, bf16[32,4096]{1,0:T(8,128)(2,1)S(1)}, u32[]{:S(2)}, u32[]{:S(2)}) collective-permute-start(bf16[32,4096]{1,0:T(8,128)(2,1)S(1)} %get-tuple-element.282), channel_id=1, source_target_pairs={{0,8},{1,9},{2,10},{3,11},{4,12},{5,13},{6,14},{7,15},{8,0},{9,1},... | collective-permute-start | bytes 786440 | tf_op jit(solution)/shard_map/ppermute | solution.py:769
  681.6 23.7 %collective-permute-start.76 = (bf16[32,4096]{1,0:T(8,128)(2,1)S(1)}, bf16[32,4096]{1,0:T(8,128)(2,1)S(1)}, u32[]{:S(2)}, u32[]{:S(2)}) collective-permute-start(bf16[32,4096]{1,0:T(8,128)(2,1)S(1)} %get-tuple-element.281), channel_id=1, source_target_pairs={{0,12},{1,13},{2,14},{3,15},{4,0},{5,1},{6,2},{7,3},{8,4},{9,5},{1... | collective-permute-start | bytes 786440 | tf_op jit(solution)/shard_map/ppermute | solution.py:769
  (42 other events, 422.5 us)

commit v4 on v3

--- a/solution.py
+++ b/solution.py
@@ -636,7 +636,7 @@
             beside = jnp.where(count == index, blocks[index + 1], beside)
         return near, beside
 
-    def outer_skips(stores, first, second, limit, sign, sections, with_aim):
+    def outer_skips(stores, held, first, second, limit, sign, sections, with_aim):
         stores, posts = picked(stores, (first, 1, False), (second, 1, False))
         post = jnp.concatenate(posts, axis=0)
         counts = [jnp.full((1, 1, width), each // WIN) for each in reaches_seen]
@@ -644,6 +644,7 @@
             post = jnp.concatenate([post, aim_here], axis=2)
             extra = jnp.full((1, 1, channels), target_reach // WIN)
             counts = [jnp.concatenate([count, extra], axis=2) for count in counts]
+        post, *held = together(post, *held)
         near, beside = long_shift(
             mirror(post, outer_encoders if sign > 0 else outer_decoders),
             jnp.concatenate(counts, axis=0),
@@ -662,7 +663,7 @@
                 for slot in range(2)
             ]
             rows.append(jnp.concatenate(aims, axis=1))
-        return stores, rows
+        return stores, held, rows
 
     outer_encoders = range(half_pairs - 1)
     outer_decoders = range(half_pairs + 1, pair_count)
@@ -674,20 +675,20 @@
         nxt = along(z_low, 1, everyone)
         if pair == half_pairs - 1:
             inner = inner_hops(z_low, pair, 1)
+            nxt, *rows = together(nxt, *rows)
+            aim = rows[2]
+            for goal in range(half_pairs + 1, pair_count):
+                skips[2 * goal + 1], skips[2 * goal] = rows[:2]
         stores, z_high = forward(high, z_low, nxt, skips.get(high), stores)
         if pair == half_pairs - 1:
-            z_high, *inner = together(z_high, *inner)
+            z_high, *inner[:2] = together(z_high, *inner[:2])
         if pair < pair_count - 1:
             nxt = hop(z_high, pair, 1, 1)
             cur = hop(z_high, pair, 1, 0)
         if pair == half_pairs - 2:
-            stores, rows = outer_skips(
-                stores, Z_AT, LOW_SLOTS + Z_AT, tok_count - 1, 1, decoders, True
+            stores, (cur, nxt), rows = outer_skips(
+                stores, (cur, nxt), Z_AT, LOW_SLOTS + Z_AT, tok_count - 1, 1, decoders, True
             )
-            cur, nxt, *rows = together(cur, nxt, *rows)
-            aim = rows[2]
-            for goal in range(half_pairs + 1, pair_count):
-                skips[2 * goal + 1], skips[2 * goal] = rows[:2]
         if pair == half_pairs - 1:
             reach = start[low + 3] - start[low]
             near, beside = near_and_beside(inner, reach // WIN)
@@ -701,22 +702,21 @@
         prv = along(gx_high, -1, everyone)
         if pair == half_pairs:
             inner = inner_hops(gx_high, pair, -1)
+            prv, *rows = together(prv, *rows)
+            for goal in range(half_pairs - 1):
+                skips[2 * goal], skips[2 * goal + 1] = rows
         sources = (gx_high, prv)
         stores, gx_low = backward(low, sources, skips.get(low), stores)
         if pair == half_pairs:
-            gx_low, *inner = together(gx_low, *inner)
+            gx_low, *inner[:2] = together(gx_low, *inner[:2])
         if pair > 0:
             prv = hop(gx_low, pair - 1, -1, -1)
             cur = hop(gx_low, pair - 1, -1, 0)
             sources = (cur, prv)
         if pair == half_pairs + 1:
-            stores, rows = outer_skips(
-                stores, LOW_SLOTS + GX_AT, GX_AT, tok_count - 2, -1, encoders, False
+            stores, sources, rows = outer_skips(
+                stores, sources, LOW_SLOTS + GX_AT, GX_AT, tok_count - 2, -1, encoders, False
             )
-            cur, prv, *rows = together(cur, prv, *rows)
-            sources = (cur, prv)
-            for goal in range(half_pairs - 1):
-                skips[2 * goal], skips[2 * goal + 1] = rows
         if pair == half_pairs:
             reach = start[high] - start[high - 3]
             near, beside = near_and_beside(inner, reach // WIN)

time: 718 us -> 745 us (1.038)
  waiting for transfers between devices: 399 us -> 426 us
    ppermute x68, waiting for transfers between devices: 340 us -> 367 us  [moved(): return lax.ppermute(block, ('section', 'tok'), route)]
  transfers between devices with their start and end apart: 80 -> 80, of which waited for: 40 -> 38; matrix products, arithmetic and copies ran while one was open for 1% -> 2% of each run, Pallas kernels for 0% -> 1%
where the time goes in v4:
time: 745 us; the launch traced here: 735 us
  waiting for transfers between devices  426 us (57%)
  starting transfers between devices  185 us (25%)
  Pallas kernels  70.4 us (9%)
  blocking collectives  19.6 us (3%)
  other arithmetic  16.9 us (2%)
  between operations  9.71 us (1%)
    ppermute x68, waiting for transfers between devices, moved(): return lax.ppermute(block, ('section', 'tok'), route)  367 us
    ppermute x68, starting transfers between devices, moved(): return lax.ppermute(block, ('section', 'tok'), route)  154 us
    ppermute x12, waiting for transfers between devices, ring(): return lax.ppermute(block, 'tok', route)  59.5 us
    pallas_call x32, Pallas kernels, section_call(): pl.pallas_call(kernel, out_shape=store_shapes + (rows_bf,), in_specs=[SME...  55.9 us
    ppermute x12, starting transfers between devices, ring(): return lax.ppermute(block, 'tok', route)  31.2 us
    unnamed x1, blocking collectives  19.6 us
  transfers between devices with their start and end apart: 80, of which 38 were waited for; matrix products, arithmetic and copies ran while one was open for 2% of the time, Pallas kernels for 1%

profile of v4, /device:TPU:35, one launch (start us, length us, event | category | flops | bytes accessed | tf_op | source)
XLA Modules:
  0.0 735.0 jit_solution(13778039299028713115)
XLA Ops:
  0.6 6.5 pad_maximum_fusion.refs_3_.refs_4_
  10.8 19.6 %all-reduce.3 = s32[16]{0:T(128)S(1)} all-reduce(s32[16]{0:T(128)S(1)} %dynamic-update-slice), channel_id=2, replica_groups=mesh['section'=16,'tok'=16] {'section'}, use_global_device_ids=true, to_apply=%add.3 | all-reduce | flops 16 | bytes 128
  32.8 6.1 forward_plain.8
  39.2 3.6 collective-permute-done.2.refs_2_
  42.7 6.1 forward_plain.9
  55.7 3.2 collective-permute-done.5.refs_2_
  59.7 16.3 %collective-permute-start.6 = (bf16[128,512]{1,0:T(8,128)(2,1)S(1)}, bf16[128,512]{1,0:T(8,128)(2,1)S(1)}, u32[]{:S(2)}, u32[]{:S(2)}) collective-permute-start(bf16[128,512]{1,0:T(8,128)(2,1)S(1)} %get-tuple-element.153), channel_id=1, source_target_pairs={{0,32},{1,33},{2,34},{3,35},{4,36},{5,37},{6,38},{7,39},{8,40},{9,... | collective-permute-start | bytes 393224 | tf_op jit(solution)/shard_map/ppermute | solution.py:425
  81.3 4.1 collective-permute-start.8
  89.1 5.7 collective-permute-start.10
  94.9 9.0 %collective-permute-start.9 = (bf16[128,512]{1,0:T(8,128)(2,1)S(1)}, bf16[128,512]{1,0:T(8,128)(2,1)S(1)}, u32[]{:S(2)}, u32[]{:S(2)}) collective-permute-start(bf16[128,512]{1,0:T(8,128)(2,1)S(1)} %get-tuple-element.162), channel_id=1, source_target_pairs={{0,32},{1,33},{2,34},{3,35},{4,36},{5,37},{6,38},{7,39},{8,40},{9,... | collective-permute-start | bytes 393224 | tf_op jit(solution)/shard_map/ppermute | solution.py:425
  108.2 7.4 %collective-permute-done.12 = bf16[2,128,640]{2,1,0:T(8,128)(2,1)S(1)} collective-permute-done((bf16[2,128,640]{2,1,0:T(8,128)(2,1)S(1)}, bf16[2,128,640]{2,1,0:T(8,128)(2,1)S(1)}, u32[]{:S(2)}, u32[]{:S(2)}) %collective-permute-start.12) | collective-permute-done | bytes 327712 | tf_op jit(solution)/shard_map/ppermute | solution.py:425
  125.7 4.1 collective-permute-start.11
  160.5 4.1 collective-permute-start.33
  169.5 5.4 collective-permute-done.34.refs_2_
  178.2 6.3 collective-permute-done.37.refs_2_
  187.7 5.9 collective-permute-done.40.refs_2_
  200.1 203.6 %collective-permute-done.44 = bf16[2,128,512]{2,1,0:T(8,128)(2,1)S(1)} collective-permute-done((bf16[2,128,512]{2,1,0:T(8,128)(2,1)S(1)}, bf16[2,128,512]{2,1,0:T(8,128)(2,1)S(1)}, u32[]{:S(2)}, u32[]{:S(2)}) %collective-permute-start.44) | collective-permute-done | bytes 262176 | tf_op jit(solution)/shard_map/ppermute | solution.py:425
  405.8 5.1 collective-permute-done.45
  412.8 7.9 %collective-permute-done.46 = bf16[2,128,512]{2,1,0:T(8,128)(2,1)S(1)} collective-permute-done((bf16[2,128,512]{2,1,0:T(8,128)(2,1)S(1)}, bf16[2,128,512]{2,1,0:T(8,128)(2,1)S(1)}, u32[]{:S(2)}, u32[]{:S(2)}) %collective-permute-start.46) | collective-permute-done | bytes 262176 | tf_op jit(solution)/shard_map/ppermute | solution.py:425
  422.7 16.2 %collective-permute-done.47 = bf16[2,128,512]{2,1,0:T(8,128)(2,1)S(1)} collective-permute-done((bf16[2,128,512]{2,1,0:T(8,128)(2,1)S(1)}, bf16[2,128,512]{2,1,0:T(8,128)(2,1)S(1)}, u32[]{:S(2)}, u32[]{:S(2)}) %collective-permute-start.47) | collective-permute-done | bytes 262176 | tf_op jit(solution)/shard_map/ppermute | solution.py:425
  438.9 3.4 collective-permute-start.48
  442.3 6.4 collective-permute-done.48
  448.8 11.1 %collective-permute-start.49 = (bf16[2,128,512]{2,1,0:T(8,128)(2,1)S(1)}, bf16[2,128,512]{2,1,0:T(8,128)(2,1)S(1)}, u32[]{:S(2)}, u32[]{:S(2)}) collective-permute-start(bf16[2,128,512]{2,1,0:T(8,128)(2,1)S(1)} %broadcast_select_fusion.7), channel_id=1, source_target_pairs={{15,0},{0,1},{1,2},{2,3},{3,4},{4,5},{5,6},{6,7},{7,8},{8,9},{9,10... | collective-permute-start | bytes 786440 | tf_op jit(solution)/shard_map/ppermute | solution.py:425
  460.7 6.1 collective-permute-start.43
  476.8 6.9 collective-permute-done.54.refs_2_
  486.9 31.0 %collective-permute-start.59 = (bf16[7,128,512]{2,1,0:T(8,128)(2,1)}, bf16[7,128,512]{2,1,0:T(8,128)(2,1)S(1)}, u32[]{:S(2)}, u32[]{:S(2)}) collective-permute-start(bf16[7,128,512]{2,1,0:T(8,128)(2,1)} %get-tuple-element.244), channel_id=1, source_target_pairs={{0,16},{1,17},{2,18},{3,19},{4,20},{5,21},{6,22},{7,23},{8,24},{9,... | collective-permute-start | bytes 2752520 | tf_op jit(solution)/shard_map/ppermute | solution.py:425
  520.5 4.4 collective-permute-done.57.refs_1_
  524.9 5.5 collective-permute-done.58.refs_2_
  531.2 5.7 collective-permute-done.60.refs_2_
  540.7 3.1 collective-permute-done.61.refs_1_
  543.9 4.9 collective-permute-done.62.refs_2_
  549.6 5.0 collective-permute-done.63.refs_2_
  558.2 31.7 %collective-permute-done.64.refs_1_ = bf16[128,512]{1,0:T(8,128)(2,1)S(1)} collective-permute-done((bf16[128,512]{1,0:T(8,128)(2,1)S(1)}, bf16[128,512]{1,0:T(8,128)(2,1)S(1)}, u32[]{:S(2)}, u32[]{:S(2)}) %collective-permute-start.64) | collective-permute-done | bytes 131104 | tf_op jit(solution)/shard_map/ppermute | solution.py:425
  589.8 4.9 collective-permute-done.65.refs_2_
  594.7 9.5 %backward_skip.12 = (bf16[224,128,512]{2,1,0:T(8,128)(2,1)}, f32[112,128,512]{2,1,0:T(8,128)}, bf16[128,512]{1,0:T(8,128)(2,1)S(1)}) custom-call(s32[16,4]{1,0:T(8,128)S(1)} %copy.149.refs_0_, bf16[128,512]{1,0:T(8,128)(2,1)S(1)} %collective-permute-done.64.refs_1_, ...), custom_call_target="tpu_custom_call", output_to_operand_aliasing={{0}: (6, {}), {1}: (7, {})} | custom-call | tf_op jit(solution)/shard_map/backward_skip/pallas_call | solution.py:534
  604.3 4.3 collective-permute-done.66.refs_2_
  608.6 9.9 %backward_skip.13 = (bf16[224,128,512]{2,1,0:T(8,128)(2,1)}, f32[112,128,512]{2,1,0:T(8,128)}, bf16[128,512]{1,0:T(8,128)(2,1)}) custom-call(s32[16,4]{1,0:T(8,128)S(1)} %copy.149.refs_0_, bf16[128,512]{1,0:T(8,128)(2,1)S(1)} %get-tuple-element.263.refs_1_, ...), custom_call_target="tpu_custom_call", output_to_operand_aliasing={{0}: (6, {}), {1}: (7, {})} | custom-call | tf_op jit(solution)/shard_map/backward_skip/pallas_call | solution.py:534
  620.9 5.7 collective-permute-start.67
  630.3 6.6 weight_grads.1
  637.9 5.9 collective-permute-start.69
  643.9 10.9 %collective-permute-start.72 = (bf16[4,32,2048]{2,1,0:T(8,128)(2,1)}, bf16[4,32,2048]{2,1,0:T(8,128)(2,1)S(1)}, u32[]{:S(2)}, u32[]{:S(2)}) collective-permute-start(bf16[4,32,2048]{2,1,0:T(8,128)(2,1)} %get-tuple-element.276), channel_id=1, source_target_pairs={{0,8},{1,9},{2,10},{3,11},{4,12},{5,13},{6,14},{7,15},{8,0},{9,1},... | collective-permute-start | bytes 1572872 | tf_op jit(solution)/shard_map/ppermute | solution.py:769
  654.8 4.6 collective-permute-done.71
  662.3 25.4 %collective-permute-done.72 = bf16[4,32,2048]{2,1,0:T(8,128)(2,1)S(1)} collective-permute-done((bf16[4,32,2048]{2,1,0:T(8,128)(2,1)}, bf16[4,32,2048]{2,1,0:T(8,128)(2,1)S(1)}, u32[]{:S(2)}, u32[]{:S(2)}) %collective-permute-start.72) | collective-permute-done | bytes 524320 | tf_op jit(solution)/shard_map/ppermute | solution.py:769
  687.6 8.0 %collective-permute-done.73 = bf16[4,32,2048]{2,1,0:T(8,128)(2,1)} collective-permute-done((bf16[4,32,2048]{2,1,0:T(8,128)(2,1)S(1)}, bf16[4,32,2048]{2,1,0:T(8,128)(2,1)}, u32[]{:S(2)}, u32[]{:S(2)}) %collective-permute-start.73) | collective-permute-done | bytes 524320 | tf_op jit(solution)/shard_map/ppermute | solution.py:769
  699.9 5.4 collective-permute-start.78
  705.5 3.3 collective-permute-start.75
  712.3 14.8 %collective-permute-done.75 = bf16[32,4096]{1,0:T(8,128)(2,1)S(1)} collective-permute-done((bf16[32,4096]{1,0:T(8,128)(2,1)S(1)}, bf16[32,4096]{1,0:T(8,128)(2,1)S(1)}, u32[]{:S(2)}, u32[]{:S(2)}) %collective-permute-start.75) | collective-permute-done | bytes 262176 | tf_op jit(solution)/shard_map/ppermute | solution.py:769
  727.2 5.2 collective-permute-done.76
  (236 shorter events, 129.5 us)
Async XLA Ops:
  7.1 25.6 %collective-permute-start.1 = (bf16[512,6144]{1,0:T(8,128)(2,1)}, bf16[512,6144]{1,0:T(8,128)(2,1)}, u32[]{:S(2)}, u32[]{:S(2)}) collective-permute-start(bf16[512,6144]{1,0:T(8,128)(2,1)} %pad_maximum_fusion.refs_3_.refs_4_), channel_id=1, source_target_pairs={{0,16},{1,17},{2,18},{3,19},{4,20},{5,21},{6,22},{7,23},{8,24},{9,... | collective-permute-start | bytes 18874376 | tf_op jit(solution)/shard_map/ppermute | solution.py:425
  7.8 24.9 %collective-permute-start = (bf16[128,512]{1,0:T(8,128)(2,1)S(1)}, bf16[128,512]{1,0:T(8,128)(2,1)S(1)}, u32[]{:S(2)}, u32[]{:S(2)}) collective-permute-start(bf16[128,512]{1,0:T(8,128)(2,1)S(1)} %dynamic-slice_bitcast_fusion.6.refs_1_), channel_id=1, source_target_pairs={{1,0},{2,1},{3,2},{4,3},{5,4},{6,5},{7,6},{8,7},{9,8},{10,9},{11,1... | collective-permute-start | bytes 393224 | tf_op jit(solution)/shard_map/ppermute | solution.py:425
  54.1 4.8 collective-permute-start.5
  59.7 19.1 %collective-permute-start.6 = (bf16[128,512]{1,0:T(8,128)(2,1)S(1)}, bf16[128,512]{1,0:T(8,128)(2,1)S(1)}, u32[]{:S(2)}, u32[]{:S(2)}) collective-permute-start(bf16[128,512]{1,0:T(8,128)(2,1)S(1)} %get-tuple-element.153), channel_id=1, source_target_pairs={{0,32},{1,33},{2,34},{3,35},{4,36},{5,37},{6,38},{7,39},{8,40},{9,... | collective-permute-start | bytes 393224 | tf_op jit(solution)/shard_map/ppermute | solution.py:425
  76.0 4.5 collective-permute-start.7
  81.3 7.1 collective-permute-start.8
  89.1 17.6 %collective-permute-start.10 = (bf16[128,512]{1,0:T(8,128)(2,1)S(1)}, bf16[128,512]{1,0:T(8,128)(2,1)S(1)}, u32[]{:S(2)}, u32[]{:S(2)}) collective-permute-start(bf16[128,512]{1,0:T(8,128)(2,1)S(1)} %get-tuple-element.162), channel_id=1, source_target_pairs={{0,47},{1,32},{2,33},{3,34},{4,35},{5,36},{6,37},{7,38},{8,39},{9,... | collective-permute-start | bytes 393224 | tf_op jit(solution)/shard_map/ppermute | solution.py:425
  94.9 11.8 %collective-permute-start.9 = (bf16[128,512]{1,0:T(8,128)(2,1)S(1)}, bf16[128,512]{1,0:T(8,128)(2,1)S(1)}, u32[]{:S(2)}, u32[]{:S(2)}) collective-permute-start(bf16[128,512]{1,0:T(8,128)(2,1)S(1)} %get-tuple-element.162), channel_id=1, source_target_pairs={{0,32},{1,33},{2,34},{3,35},{4,36},{5,37},{6,38},{7,39},{8,40},{9,... | collective-permute-start | bytes 393224 | tf_op jit(solution)/shard_map/ppermute | solution.py:425
  106.7 8.8 %collective-permute-start.12 = (bf16[2,128,640]{2,1,0:T(8,128)(2,1)S(1)}, bf16[2,128,640]{2,1,0:T(8,128)(2,1)S(1)}, u32[]{:S(2)}, u32[]{:S(2)}) collective-permute-start(bf16[2,128,640]{2,1,0:T(8,128)(2,1)S(1)} %maximum_maximum_fusion), channel_id=1, source_target_pairs={{0,224},{1,225},{2,226},{3,227},{4,228},{5,229},{6,230},{7,231},{8... | collective-permute-start | bytes 983048 | tf_op jit(solution)/shard_map/ppermute | solution.py:425
  115.5 6.7 collective-permute-start.13
  123.8 7.3 collective-permute-start.16
  125.7 6.9 collective-permute-start.11
  134.7 4.6 collective-permute-start.23
  152.8 4.9 collective-permute-start.30
  160.5 6.0 collective-permute-start.33
  168.5 6.4 collective-permute-start.34
  178.0 6.4 collective-permute-start.37
  187.6 6.0 collective-permute-start.40
  198.8 204.9 %collective-permute-start.44 = (bf16[2,128,512]{2,1,0:T(8,128)(2,1)S(1)}, bf16[2,128,512]{2,1,0:T(8,128)(2,1)S(1)}, u32[]{:S(2)}, u32[]{:S(2)}) collective-permute-start(bf16[2,128,512]{2,1,0:T(8,128)(2,1)S(1)} %pad_maximum_fusion.1), channel_id=1, source_target_pairs={{160,64},{161,65},{162,66},{163,67},{164,68},{165,69},{166,70},{16... | collective-permute-start | bytes 786440 | tf_op jit(solution)/shard_map/ppermute | solution.py:425
  403.8 7.1 collective-permute-start.45
  410.9 9.8 %collective-permute-start.46 = (bf16[2,128,512]{2,1,0:T(8,128)(2,1)S(1)}, bf16[2,128,512]{2,1,0:T(8,128)(2,1)S(1)}, u32[]{:S(2)}, u32[]{:S(2)}) collective-permute-start(bf16[2,128,512]{2,1,0:T(8,128)(2,1)S(1)} %broadcast_select_fusion.4), channel_id=1, source_target_pairs={{14,0},{15,1},{0,2},{1,3},{2,4},{3,5},{4,6},{5,7},{6,8},{7,9},{8,1... | collective-permute-start | bytes 786440 | tf_op jit(solution)/shard_map/ppermute | solution.py:425
  420.8 18.1 %collective-permute-start.47 = (bf16[2,128,512]{2,1,0:T(8,128)(2,1)S(1)}, bf16[2,128,512]{2,1,0:T(8,128)(2,1)S(1)}, u32[]{:S(2)}, u32[]{:S(2)}) collective-permute-start(bf16[2,128,512]{2,1,0:T(8,128)(2,1)S(1)} %broadcast_select_fusion.5), channel_id=1, source_target_pairs={{12,0},{13,1},{14,2},{15,3},{0,4},{1,5},{2,6},{3,7},{4,8},{5,9},{6... | collective-permute-start | bytes 786440 | tf_op jit(solution)/shard_map/ppermute | solution.py:425
  438.9 9.8 %collective-permute-start.48 = (bf16[2,128,512]{2,1,0:T(8,128)(2,1)S(1)}, bf16[2,128,512]{2,1,0:T(8,128)(2,1)S(1)}, u32[]{:S(2)}, u32[]{:S(2)}) collective-permute-start(bf16[2,128,512]{2,1,0:T(8,128)(2,1)S(1)} %broadcast_select_fusion.6), channel_id=1, source_target_pairs={{8,0},{9,1},{10,2},{11,3},{12,4},{13,5},{14,6},{15,7},{0,8},{1,9},... | collective-permute-start | bytes 786440 | tf_op jit(solution)/shard_map/ppermute | solution.py:425
  448.8 20.0 %collective-permute-start.49 = (bf16[2,128,512]{2,1,0:T(8,128)(2,1)S(1)}, bf16[2,128,512]{2,1,0:T(8,128)(2,1)S(1)}, u32[]{:S(2)}, u32[]{:S(2)}) collective-permute-start(bf16[2,128,512]{2,1,0:T(8,128)(2,1)S(1)} %broadcast_select_fusion.7), channel_id=1, source_target_pairs={{15,0},{0,1},{1,2},{2,3},{3,4},{4,5},{5,6},{6,7},{7,8},{8,9},{9,10... | collective-permute-start | bytes 786440 | tf_op jit(solution)/shard_map/ppermute | solution.py:425
  460.7 9.5 %collective-permute-start.43 = (bf16[128,512]{1,0:T(8,128)(2,1)S(1)}, bf16[128,512]{1,0:T(8,128)(2,1)S(1)}, u32[]{:S(2)}, u32[]{:S(2)}) collective-permute-start(bf16[128,512]{1,0:T(8,128)(2,1)S(1)} %get-tuple-element.228.refs_1_), channel_id=1, source_target_pairs={{15,0},{0,1},{1,2},{2,3},{3,4},{4,5},{5,6},{6,7},{7,8},{8,9},{9,10... | collective-permute-start | bytes 393224 | tf_op jit(solution)/shard_map/ppermute | solution.py:425
  474.6 9.1 %collective-permute-start.54 = (bf16[128,512]{1,0:T(8,128)(2,1)S(1)}, bf16[128,512]{1,0:T(8,128)(2,1)S(1)}, u32[]{:S(2)}, u32[]{:S(2)}) collective-permute-start(bf16[128,512]{1,0:T(8,128)(2,1)S(1)} %get-tuple-element.237.refs_1_), channel_id=1, source_target_pairs={{15,0},{0,1},{1,2},{2,3},{3,4},{4,5},{5,6},{6,7},{7,8},{8,9},{9,10... | collective-permute-start | bytes 393224 | tf_op jit(solution)/shard_map/ppermute | solution.py:425
  486.9 43.5 %collective-permute-start.59 = (bf16[7,128,512]{2,1,0:T(8,128)(2,1)}, bf16[7,128,512]{2,1,0:T(8,128)(2,1)S(1)}, u32[]{:S(2)}, u32[]{:S(2)}) collective-permute-start(bf16[7,128,512]{2,1,0:T(8,128)(2,1)} %get-tuple-element.244), channel_id=1, source_target_pairs={{0,16},{1,17},{2,18},{3,19},{4,20},{5,21},{6,22},{7,23},{8,24},{9,... | collective-permute-start | bytes 2752520 | tf_op jit(solution)/shard_map/ppermute | solution.py:425
  517.9 7.0 collective-permute-start.57
  519.2 11.2 %collective-permute-start.58 = (bf16[128,512]{1,0:T(8,128)(2,1)S(1)}, bf16[128,512]{1,0:T(8,128)(2,1)S(1)}, u32[]{:S(2)}, u32[]{:S(2)}) collective-permute-start(bf16[128,512]{1,0:T(8,128)(2,1)S(1)} %get-tuple-element.242), channel_id=1, source_target_pairs={{32,1},{33,2},{34,3},{35,4},{36,5},{37,6},{38,7},{39,8},{40,9},{41... | collective-permute-start | bytes 393224 | tf_op jit(solution)/shard_map/ppermute | solution.py:425
  531.1 5.8 collective-permute-start.60
  538.1 5.7 collective-permute-start.61
  539.4 9.3 %collective-permute-start.62 = (bf16[128,512]{1,0:T(8,128)(2,1)S(1)}, bf16[128,512]{1,0:T(8,128)(2,1)S(1)}, u32[]{:S(2)}, u32[]{:S(2)}) collective-permute-start(bf16[128,512]{1,0:T(8,128)(2,1)S(1)} %get-tuple-element.254), channel_id=1, source_target_pairs={{32,1},{33,2},{34,3},{35,4},{36,5},{37,6},{38,7},{39,8},{40,9},{41... | collective-permute-start | bytes 393224 | tf_op jit(solution)/shard_map/ppermute | solution.py:425
  549.5 5.1 collective-permute-start.63
  555.6 34.3 %collective-permute-start.64 = (bf16[128,512]{1,0:T(8,128)(2,1)S(1)}, bf16[128,512]{1,0:T(8,128)(2,1)S(1)}, u32[]{:S(2)}, u32[]{:S(2)}) collective-permute-start(bf16[128,512]{1,0:T(8,128)(2,1)S(1)} %get-tuple-element.260), channel_id=1, source_target_pairs={{32,0},{33,1},{34,2},{35,3},{36,4},{37,5},{38,6},{39,7},{40,8},{41... | collective-permute-start | bytes 393224 | tf_op jit(solution)/shard_map/ppermute | solution.py:425
  556.9 37.8 %collective-permute-start.65 = (bf16[128,512]{1,0:T(8,128)(2,1)S(1)}, bf16[128,512]{1,0:T(8,128)(2,1)S(1)}, u32[]{:S(2)}, u32[]{:S(2)}) collective-permute-start(bf16[128,512]{1,0:T(8,128)(2,1)S(1)} %get-tuple-element.260), channel_id=1, source_target_pairs={{32,1},{33,2},{34,3},{35,4},{36,5},{37,6},{38,7},{39,8},{40,9},{41... | collective-permute-start | bytes 393224 | tf_op jit(solution)/shard_map/ppermute | solution.py:425
  620.9 8.4 %collective-permute-start.67 = (bf16[9,128,512]{2,1,0:T(8,128)(2,1)}, bf16[9,128,512]{2,1,0:T(8,128)(2,1)S(1)}, u32[]{:S(2)}, u32[]{:S(2)}) collective-permute-start(bf16[9,128,512]{2,1,0:T(8,128)(2,1)} %get-tuple-element.269), channel_id=1, source_target_pairs={{0,16},{1,17},{2,18},{3,19},{4,20},{5,21},{6,22},{7,23},{8,24},{9,... | collective-permute-start | bytes 3538952 | tf_op jit(solution)/shard_map/ppermute | solution.py:425
  637.0 22.4 %collective-permute-start.71 = (bf16[4,32,2048]{2,1,0:T(8,128)(2,1)S(1)}, bf16[4,32,2048]{2,1,0:T(8,128)(2,1)S(1)}, u32[]{:S(2)}, u32[]{:S(2)}) collective-permute-start(bf16[4,32,2048]{2,1,0:T(8,128)(2,1)S(1)} %get-tuple-element.275), channel_id=1, source_target_pairs={{0,4},{1,5},{2,6},{3,7},{4,8},{5,9},{6,10},{7,11},{8,12},{9,13},{1... | collective-permute-start | bytes 1572872 | tf_op jit(solution)/shard_map/ppermute | solution.py:769
  637.9 59.0 %collective-permute-start.68 = (bf16[4,32,4096]{2,1,0:T(8,128)(2,1)}, bf16[4,32,4096]{2,1,0:T(8,128)(2,1)}, u32[]{:S(2)}, u32[]{:S(2)}) collective-permute-start(bf16[4,32,4096]{2,1,0:T(8,128)(2,1)} %get-tuple-element.271), channel_id=1, source_target_pairs={{0,1},{1,2},{2,3},{3,0},{4,5},{5,6},{6,7},{7,4},{8,9},{9,10},{10,1... | collective-permute-start | bytes 3145736 | tf_op jit(solution)/shard_map/ppermute | solution.py:769
  637.9 59.1 %collective-permute-start.69 = (bf16[4,32,4096]{2,1,0:T(8,128)(2,1)}, bf16[4,32,4096]{2,1,0:T(8,128)(2,1)}, u32[]{:S(2)}, u32[]{:S(2)}) collective-permute-start(bf16[4,32,4096]{2,1,0:T(8,128)(2,1)} %get-tuple-element.272), channel_id=1, source_target_pairs={{0,2},{1,3},{2,0},{3,1},{4,6},{5,7},{6,4},{7,5},{8,10},{9,11},{10,... | collective-permute-start | bytes 3145736 | tf_op jit(solution)/shard_map/ppermute | solution.py:769
  643.9 53.1 %collective-permute-start.70 = (bf16[4,32,4096]{2,1,0:T(8,128)(2,1)}, bf16[4,32,4096]{2,1,0:T(8,128)(2,1)}, u32[]{:S(2)}, u32[]{:S(2)}) collective-permute-start(bf16[4,32,4096]{2,1,0:T(8,128)(2,1)} %get-tuple-element.273), channel_id=1, source_target_pairs={{0,3},{1,0},{2,1},{3,2},{4,7},{5,4},{6,5},{7,6},{8,11},{9,8},{10,9... | collective-permute-start | bytes 3145736 | tf_op jit(solution)/shard_map/ppermute | solution.py:769
  643.9 43.8 %collective-permute-start.72 = (bf16[4,32,2048]{2,1,0:T(8,128)(2,1)}, bf16[4,32,2048]{2,1,0:T(8,128)(2,1)S(1)}, u32[]{:S(2)}, u32[]{:S(2)}) collective-permute-start(bf16[4,32,2048]{2,1,0:T(8,128)(2,1)} %get-tuple-element.276), channel_id=1, source_target_pairs={{0,8},{1,9},{2,10},{3,11},{4,12},{5,13},{6,14},{7,15},{8,0},{9,1},... | collective-permute-start | bytes 1572872 | tf_op jit(solution)/shard_map/ppermute | solution.py:769
  659.4 36.2 %collective-permute-start.73 = (bf16[4,32,2048]{2,1,0:T(8,128)(2,1)S(1)}, bf16[4,32,2048]{2,1,0:T(8,128)(2,1)}, u32[]{:S(2)}, u32[]{:S(2)}) collective-permute-start(bf16[4,32,2048]{2,1,0:T(8,128)(2,1)S(1)} %get-tuple-element.277), channel_id=1, source_target_pairs={{0,12},{1,13},{2,14},{3,15},{4,0},{5,1},{6,2},{7,3},{8,4},{9,5},{1... | collective-permute-start | bytes 1572872 | tf_op jit(solution)/shard_map/ppermute | solution.py:769
  699.5 9.2 %collective-permute-start.77 = (bf16[32,2048]{1,0:T(8,128)(2,1)S(1)}, bf16[32,2048]{1,0:T(8,128)(2,1)S(1)}, u32[]{:S(2)}, u32[]{:S(2)}) collective-permute-start(bf16[32,2048]{1,0:T(8,128)(2,1)S(1)} %get-tuple-element.283), channel_id=1, source_target_pairs={{0,1},{1,2},{2,3},{3,0},{4,5},{5,6},{6,7},{7,4},{8,9},{9,10},{10,1... | collective-permute-start | bytes 393224 | tf_op jit(solution)/shard_map/ppermute | solution.py:769
  699.9 10.2 %collective-permute-start.78 = (bf16[32,2048]{1,0:T(8,128)(2,1)S(1)}, bf16[32,2048]{1,0:T(8,128)(2,1)S(1)}, u32[]{:S(2)}, u32[]{:S(2)}) collective-permute-start(bf16[32,2048]{1,0:T(8,128)(2,1)S(1)} %get-tuple-element.285), channel_id=1, source_target_pairs={{0,2},{1,3},{2,0},{3,1},{4,6},{5,7},{6,4},{7,5},{8,10},{9,11},{10,... | collective-permute-start | bytes 393224 | tf_op jit(solution)/shard_map/ppermute | solution.py:769
  705.3 6.2 collective-permute-start.79
  705.4 7.0 collective-permute-start.74
  705.5 21.7 %collective-permute-start.75 = (bf16[32,4096]{1,0:T(8,128)(2,1)S(1)}, bf16[32,4096]{1,0:T(8,128)(2,1)S(1)}, u32[]{:S(2)}, u32[]{:S(2)}) collective-permute-start(bf16[32,4096]{1,0:T(8,128)(2,1)S(1)} %get-tuple-element.282), channel_id=1, source_target_pairs={{0,8},{1,9},{2,10},{3,11},{4,12},{5,13},{6,14},{7,15},{8,0},{9,1},... | collective-permute-start | bytes 786440 | tf_op jit(solution)/shard_map/ppermute | solution.py:769
  708.8 23.7 %collective-permute-start.76 = (bf16[32,4096]{1,0:T(8,128)(2,1)S(1)}, bf16[32,4096]{1,0:T(8,128)(2,1)S(1)}, u32[]{:S(2)}, u32[]{:S(2)}) collective-permute-start(bf16[32,4096]{1,0:T(8,128)(2,1)S(1)} %get-tuple-element.281), channel_id=1, source_target_pairs={{0,12},{1,13},{2,14},{3,15},{4,0},{5,1},{6,2},{7,3},{8,4},{9,5},{1... | collective-permute-start | bytes 786440 | tf_op jit(solution)/shard_map/ppermute | solution.py:769
  (42 other events, 465.8 us)
